TPU v7x, 256 devices: a whole 4x4x8 slice. The times are simulated.
256 devices in a mesh: lon: 64 (over y_lo, z, x), grp: 4 (over y_hi, core).
Axes of the slice: x: 4, y: 4 (y_hi: 2, y_lo: 2; y = y_hi * 2 + y_lo), z: 8, core: 2. Of those that a mesh axis runs over, the one named last changes fastest.
Arguments:
- left_feat: bfloat16 [320, 512, 128], P('grp', 'lon'), may hold values from -6 to 6
- right_feat: bfloat16 [320, 512, 128], P('grp', 'lon'), may hold values from -6 to 6
- conv_cot: bfloat16 [48, 32, 512, 128], P('grp', None, 'lon'), may hold values from -6 to 6
- conv_weight: bfloat16 [32, 40, 3, 3, 3], replicated, may hold values from -0.1875 to 0.1875
- disparity_shift: int32 [512, 128], P('lon'), may hold values from 0 to 47
- valid_mask: int32 [512, 128], P('lon'), may hold values 0 or 1
Outputs:
- left_grad: float32 [320, 512, 128], P('grp', 'lon')
- right_grad: float32 [320, 512, 128], P('grp', 'lon')
- weight_grad: float32 [32, 40, 3, 3, 3], replicated
Inputs may be any that keep to these rules, and one draw needn't show every extreme that they name: `disparity_shift`: a column shift of the right features.
All inputs are finite; a program needn't handle non-finite values. No bound on the sum of `valid_mask` on one device may be relied on, other than what follows from the above.
Results may differ from a plain program's by a relative error of at most 0.0032.
Values may be sent and summed in bfloat16 or wider, within the bound.
No kernel may reach another device: no remote copies, remote signals or barrier semaphores. Data moves between devices by JAX's collectives and lax.ppermute only.
A program may use at most 192 MiB of HBM per device.

v0:
```python
import math

import jax
import jax.numpy as jnp
from jax import lax
from jax.sharding import PartitionSpec as P

CG = 8
DISP = 48
REACH = 6


photo_weight = 0.5


def shifted_2(value, axis, steps):
    count = lax.axis_size(axis)
    pairs = [(source, (source + steps) % count) for source in range(count)]
    return lax.ppermute(value, axis, pairs)


def padded_2(shard, sides, width, wrap):
    for axis, dim in sides:
        devices, length = (lax.axis_size(axis), shard.shape[dim])
        up = [(i, (i + 1) % devices) for i in range(devices if wrap else devices - 1)]
        down = [(j, i) for i, j in up]
        last = lax.slice_in_dim(shard, length - width, length, axis=dim)
        initial = lax.slice_in_dim(shard, 0, width, axis=dim)
        before = lax.ppermute(last, axis, up)
        after = lax.ppermute(initial, axis, down)
        shard = jnp.concatenate([before, shard, after], axis=dim)
    return shard


def transpose_conv(padded, kernel):
    result = lax.conv_general_dilated(
        padded[None],
        kernel,
        window_strides=(1, 1, 1),
        padding="VALID",
        rhs_dilation=(2, 2, 2),
        dimension_numbers=("NDCWH", "IODWH", "NDCWH"),
        preferred_element_type=jnp.float32,
    )
    return result[0]


def filter_conv(padded, volume):
    depth, groups_here, columns, height = volume.shape
    taps_a = []
    for tap_a in range(3):
        taps_b = []
        for tap_b in range(3):
            taps_e = []
            for tap_e in range(3):
                window = padded[
                    4 - 2 * tap_a : 4 - 2 * tap_a + depth,
                    :,
                    4 - 2 * tap_b : 4 - 2 * tap_b + columns,
                    4 - 2 * tap_e : 4 - 2 * tap_e + height,
                ]
                taps_e.append(
                    jnp.einsum("dowh,dgwh->og", window, volume, preferred_element_type=jnp.float32)
                )
            taps_b.append(jnp.stack(taps_e, axis=-1))
        taps_a.append(jnp.stack(taps_b, axis=-2))
    return jnp.stack(taps_a, axis=2)


def shards(left_feat, right_feat, conv_cot, conv_weight, disparity_shift, valid_mask):
    channels, columns, height = left_feat.shape
    local_groups = channels // CG
    offset = REACH * columns
    grad_scale = 1.0 / math.sqrt(DISP * columns * lax.axis_size("lon") * height)
    panels = [shifted_2(right_feat, "lon", distance) for distance in range(REACH, 0, -1)]
    extended = jnp.concatenate(panels + [right_feat], axis=1)
    left_wide = left_feat.astype(jnp.float32)
    cost_list = []
    warped = jnp.zeros(left_feat.shape, jnp.float32)
    for disparity in range(DISP):
        shifted = extended[:, offset - disparity : offset - disparity + columns, :].astype(
            jnp.float32
        )
        product = (left_wide * shifted).reshape(local_groups, CG, columns, height)
        cost_list.append(jnp.sum(product, axis=1) / CG)
        chosen = (disparity_shift == disparity).astype(jnp.float32)
        warped = warped + chosen * shifted
    cost_local = jnp.stack(cost_list).astype(jnp.bfloat16)
    residual = valid_mask.astype(jnp.float32) * (left_wide - warped)
    padded_lon = padded_2(conv_cot, (("lon", 2),), 2, True)
    flipped = conv_weight[:, :, ::-1, ::-1, ::-1]
    cost_swapped = lax.all_to_all(cost_local, "grp", split_axis=0, concat_axis=1, tiled=True)
    padded = padded_2(padded_lon, (("grp", 0),), 2, False)
    padded = jnp.pad(padded, ((0, 0), (0, 0), (0, 0), (2, 2)))
    grad_part = transpose_conv(padded, flipped)
    filter_part = filter_conv(padded, cost_swapped)
    weight_grad = lax.psum(filter_part, ("lon", "grp")) * grad_scale
    grad_cost = lax.all_to_all(
        grad_part.astype(jnp.bfloat16), "grp", split_axis=1, concat_axis=0, tiled=True
    )
    left_grad = photo_weight * residual
    blocks = [
        jnp.zeros((channels, columns, height), jnp.float32) for index_block in range(REACH + 1)
    ]
    for disparity in range(DISP):
        start_col = offset - disparity
        shifted = extended[:, start_col : start_col + columns, :].astype(jnp.float32)
        weight = jnp.repeat(grad_cost[disparity].astype(jnp.float32), CG, axis=0) / CG
        left_grad = left_grad + weight * shifted
        chosen = (disparity_shift == disparity).astype(jnp.float32)
        gradient_term = weight * left_wide - photo_weight * chosen * residual
        first_block = start_col // columns
        inner = start_col % columns
        if inner == 0:
            blocks[first_block] = blocks[first_block] + gradient_term
        else:
            blocks[first_block] = (
                blocks[first_block].at[:, inner:, :].add(gradient_term[:, : columns - inner, :])
            )
            blocks[first_block + 1] = (
                blocks[first_block + 1].at[:, :inner, :].add(gradient_term[:, columns - inner :, :])
            )
    right_grad = blocks[REACH]
    for distance in range(1, REACH + 1):
        outgoing = blocks[REACH - distance]
        right_grad = right_grad + shifted_2(outgoing, "lon", -distance)
    return (left_grad, right_grad, weight_grad)


def solution(mesh):
    placed = (
        P("grp", "lon", None),
        P("grp", "lon", None),
        P("grp", None, "lon", None),
        P(),
        P("lon", None),
        P("lon", None),
    )
    return jax.shard_map(
        shards,
        mesh=mesh,
        in_specs=placed,
        out_specs=(P("grp", "lon", None), P("grp", "lon", None), P()),
        check_vma=False,
    )
```

profile of v0, /device:TPU:4, one launch (start us, length us, event | category | flops | bytes accessed | tf_op | source)
XLA Modules:
  0.0 927.2 jit_solution(10163813453098852901)
XLA Ops:
  13.9 4.3 collective-permute-start.1
  202.5 9.0 copy.163
  211.5 4.4 pad.179.clone
  218.3 19.9 %select_convert_fusion = bf16[12,8,8,17,40]{4,2,3,1,0:T(8,128)(2,1)S(1)} fusion(pred[8,17]{0,1:T(8,128)(4,1)S(1)} %copy-done.142, bf16[32,40,3,3,3]{1,0,4,3,2:T(8,128)(2,1)S(1)} %copy-done, bf16[16,32,12,1,7,4]{1,4,5,2,0,3:T(8,128)(2,1)S(1)} %slice.3081, bf16[16,32,12,1,8,17]{1,4,5,2,0,3:T(8,128)(2,1)S(1)} %copy.99), kind=kOutput, calls=%fused_computation.107 | convolution fusion | flops 909668352 | bytes 3128968 | tf_op jit(solution)/shard_map/conv_general_dilated | solution.py:36
  240.7 5.1 copy.101
  245.8 9.2 all-to-all-start
  256.4 4.1 fusion.14
  260.6 9.8 %all-to-all-done = bf16[12,40,8,128]{3,2,0,1:T(8,128)(2,1)} async-done(((bf16[12,40,8,128]{3,2,0,1:T(8,128)(2,1)}), bf16[12,40,8,128]{3,2,0,1:T(8,128)(2,1)}, u32[]{:S(2)}, u32[]{:S(2)}) %all-to-all-start) | async-done | bytes 983072 | tf_op jit(solution)/shard_map/all_to_all | solution.py:98
  275.0 3.8 fusion.144
  281.9 3.7 scatter-add.295
  287.5 4.5 scatter-add.299
  293.8 4.5 scatter-add.300
  300.0 4.5 scatter-add.301
  319.9 3.7 scatter-add.319
  323.6 3.7 scatter-add.306
  331.2 4.5 scatter-add.321
  337.5 4.9 scatter-add.324
  343.2 4.5 scatter-add.325
  357.3 4.5 scatter-add.280
  363.9 3.7 scatter-add.329
  375.2 3.7 scatter-add.330
  382.9 4.5 scatter-add.345
  389.2 4.5 scatter-add.346
  395.4 4.5 scatter-add.349
  409.6 3.7 scatter-add.351
  421.0 3.7 scatter-add.354
  428.6 4.5 scatter-add.369
  434.9 4.5 scatter-add.370
  441.2 4.7 scatter-add.371
  455.4 3.7 scatter-add.375
  466.8 3.7 scatter-add.376
  474.4 4.5 scatter-add.391
  480.6 4.5 scatter-add.394
  486.9 4.5 scatter-add.395
  508.9 4.4 scatter-add.411
  513.3 3.7 scatter-add.400
  520.8 4.5 scatter-add.415
  527.1 4.5 scatter-add.416
  532.3 4.5 scatter-add.419
  536.9 5.9 collective-permute-start.15
  544.4 3.9 scatter-add.404
  595.0 4.5 scatter-add.284
  602.5 4.4 scatter-add.286
  621.2 4.2 all-to-all-start.1
  631.7 3.7 scatter-add.310
  641.7 4.6 fusion.135
  665.8 7.4 collective-permute-done.10
  675.4 242.7 %all-reduce.9.cloned.1.call-done = f32[32,40,3,3,3]{1,0,4,3,2:T(8,128)} async-done(((f32[32,40,3,3,3]{1,0,4,3,2:T(8,128)}), f32[32,40,3,3,3]{1,0,4,3,2:T(8,128)}) %all-reduce.9.cloned.1.call-update) | async-done | bytes 138256 | tf_op jit(solution)/shard_map/psum | solution.py:97
  (639 shorter events, 431.9 us)
Async XLA Ops:
  7.2 210.9 %copy-start = (bf16[32,40,3,3,3]{1,0,4,3,2:T(8,128)(2,1)S(1)}, bf16[32,40,3,3,3]{1,0,4,3,2:T(8,128)(2,1)}, u32[]{:S(2)}) copy-start(bf16[32,40,3,3,3]{1,0,4,3,2:T(8,128)(2,1)} %param.177) | copy-start | bytes 207364
  7.2 53.6 %copy-start.12 = (bf16[80,8,128]{2,1,0:T(8,128)(2,1)S(1)}, bf16[80,8,128]{2,1,0:T(8,128)(2,1)}, u32[]{:S(2)}) copy-start(bf16[80,8,128]{2,1,0:T(8,128)(2,1)} %param.175) | copy-start | bytes 491524
  7.2 53.7 %copy-start.2 = (bf16[80,8,128]{2,1,0:T(8,128)(2,1)S(1)}, bf16[80,8,128]{2,1,0:T(8,128)(2,1)}, u32[]{:S(2)}) copy-start(bf16[80,8,128]{2,1,0:T(8,128)(2,1)} %param.174) | copy-start | bytes 491524
  7.2 50.2 %collective-permute-start.3 = (bf16[80,8,128]{2,1,0:T(8,128)(2,1)}, bf16[80,8,128]{2,1,0:T(8,128)(2,1)S(1)}, u32[]{:S(2)}, u32[]{:S(2)}) collective-permute-start(bf16[80,8,128]{2,1,0:T(8,128)(2,1)} %param.175), channel_id=1, source_target_pairs={{0,16},{4,20},{8,24},{12,28},{16,32},{20,36},{24,40},{28,44},{32,4... | collective-permute-start | bytes 491528 | tf_op jit(solution)/shard_map/ppermute | solution.py:19
  9.2 45.9 %collective-permute-start.4 = (bf16[80,8,128]{2,1,0:T(8,128)(2,1)}, bf16[80,8,128]{2,1,0:T(8,128)(2,1)S(1)}, u32[]{:S(2)}, u32[]{:S(2)}) collective-permute-start(bf16[80,8,128]{2,1,0:T(8,128)(2,1)} %param.175), channel_id=1, source_target_pairs={{0,20},{4,24},{8,28},{12,32},{16,36},{20,40},{24,44},{28,48},{32,5... | collective-permute-start | bytes 491528 | tf_op jit(solution)/shard_map/ppermute | solution.py:19
  11.7 46.1 %collective-permute-start.2 = (bf16[80,8,128]{2,1,0:T(8,128)(2,1)}, bf16[80,8,128]{2,1,0:T(8,128)(2,1)S(1)}, u32[]{:S(2)}, u32[]{:S(2)}) collective-permute-start(bf16[80,8,128]{2,1,0:T(8,128)(2,1)} %param.175), channel_id=1, source_target_pairs={{0,12},{4,16},{8,20},{12,24},{16,28},{20,32},{24,36},{28,40},{32,4... | collective-permute-start | bytes 491528 | tf_op jit(solution)/shard_map/ppermute | solution.py:19
  13.9 44.0 %collective-permute-start.1 = (bf16[80,8,128]{2,1,0:T(8,128)(2,1)}, bf16[80,8,128]{2,1,0:T(8,128)(2,1)S(1)}, u32[]{:S(2)}, u32[]{:S(2)}) collective-permute-start(bf16[80,8,128]{2,1,0:T(8,128)(2,1)} %param.175), channel_id=1, source_target_pairs={{0,8},{4,12},{8,16},{12,20},{16,24},{20,28},{24,32},{28,36},{32,40... | collective-permute-start | bytes 491528 | tf_op jit(solution)/shard_map/ppermute | solution.py:19
  18.2 35.7 %collective-permute-start.5 = (bf16[80,8,128]{2,1,0:T(8,128)(2,1)}, bf16[80,8,128]{2,1,0:T(8,128)(2,1)S(1)}, u32[]{:S(2)}, u32[]{:S(2)}) collective-permute-start(bf16[80,8,128]{2,1,0:T(8,128)(2,1)} %param.175), channel_id=1, source_target_pairs={{0,24},{4,28},{8,32},{12,36},{16,40},{20,44},{24,48},{28,52},{32,5... | collective-permute-start | bytes 491528 | tf_op jit(solution)/shard_map/ppermute | solution.py:19
  21.8 36.0 %copy-start.26 = (bf16[12,32,8,128]{3,1,2,0:T(8,128)(2,1)}, bf16[12,32,8,128]{3,1,2,0:T(8,128)(2,1)S(1)}, u32[]{:S(2)}) copy-start(bf16[12,32,8,128]{3,1,2,0:T(8,128)(2,1)S(1)} %copy.94) | copy-start | bytes 2359300
  53.9 6.9 collective-permute-start
  55.1 135.6 %collective-permute-start.6 = (bf16[12,32,2,128]{3,1,2,0:T(8,128)(2,1)}, bf16[12,32,2,128]{3,1,2,0:T(8,128)(2,1)}, u32[]{:S(2)}, u32[]{:S(2)}) collective-permute-start(bf16[12,32,2,128]{3,1,2,0:T(8,128)(2,1)} %get-tuple-element.1184), channel_id=1, source_target_pairs={{0,4},{4,8},{8,12},{12,16},{16,20},{20,24},{24,28},{28,32},{32,36}... | collective-permute-start | bytes 589832 | tf_op jit(solution)/shard_map/ppermute | solution.py:29
  57.4 134.5 %collective-permute-start.7 = (bf16[12,32,2,128]{3,1,2,0:T(8,128)(2,1)}, bf16[12,32,2,128]{3,1,2,0:T(8,128)(2,1)}, u32[]{:S(2)}, u32[]{:S(2)}) collective-permute-start(bf16[12,32,2,128]{3,1,2,0:T(8,128)(2,1)} %get-tuple-element.1183), channel_id=1, source_target_pairs={{4,0},{8,4},{12,8},{16,12},{20,16},{24,20},{28,24},{32,28},{36,32}... | collective-permute-start | bytes 589832 | tf_op jit(solution)/shard_map/ppermute | solution.py:30
  125.8 65.9 %copy-start.7 = (bf16[12,32,8,128]{3,2,1,0:T(8,128)(2,1)S(1)}, bf16[12,32,8,128]{3,2,1,0:T(8,128)(2,1)}, u32[]{:S(2)}) copy-start(bf16[12,32,8,128]{3,2,1,0:T(8,128)(2,1)} %param.176) | copy-start | bytes 2359300
  192.9 5.0 collective-permute-start.9
  194.2 4.1 collective-permute-start.8
  245.8 24.6 %all-to-all-start = ((bf16[12,40,8,128]{3,2,0,1:T(8,128)(2,1)}), bf16[12,40,8,128]{3,2,0,1:T(8,128)(2,1)}, u32[]{:S(2)}, u32[]{:S(2)}) async-start(bf16[12,40,8,128]{3,2,0,1:T(8,128)(2,1)} %copy.101), calls=%async_computation | async-start | bytes 1966080 | tf_op jit(solution)/shard_map/all_to_all | solution.py:98
  280.9 23.6 %copy-start.24 = (f32[80,8,128]{2,1,0:T(8,128)}, f32[80,8,128]{2,1,0:T(8,128)S(1)}, u32[]{:S(2)}) copy-start(f32[80,8,128]{2,1,0:T(8,128)S(1)} %get-tuple-element.1240) | copy-start | bytes 983044
  281.8 22.7 %copy-start.56 = (f32[10,8,128]{2,1,0:T(8,128)S(1)}, f32[10,8,128]{2,1,0:T(8,128)}, u32[]{:S(2)}) copy-start(f32[10,8,128]{2,1,0:T(8,128)} %get-tuple-element.1174) | copy-start | bytes 122884
  281.8 22.7 %copy-start.136 = (f32[8,128]{1,0:T(8,128)S(1)}, f32[8,128]{1,0:T(8,128)}, u32[]{:S(2)}) copy-start(f32[8,128]{1,0:T(8,128)} %get-tuple-element.1376) | copy-start | bytes 12292
  281.8 22.7 %copy-start.137 = (f32[8,128]{1,0:T(8,128)S(1)}, f32[8,128]{1,0:T(8,128)}, u32[]{:S(2)}) copy-start(f32[8,128]{1,0:T(8,128)} %get-tuple-element.1378) | copy-start | bytes 12292
  281.8 22.7 %copy-start.138 = (f32[8,128]{1,0:T(8,128)S(1)}, f32[8,128]{1,0:T(8,128)}, u32[]{:S(2)}) copy-start(f32[8,128]{1,0:T(8,128)} %get-tuple-element.1380) | copy-start | bytes 12292
  281.8 22.7 %copy-start.139 = (f32[8,128]{1,0:T(8,128)S(1)}, f32[8,128]{1,0:T(8,128)}, u32[]{:S(2)}) copy-start(f32[8,128]{1,0:T(8,128)} %get-tuple-element.1382) | copy-start | bytes 12292
  281.8 22.7 %copy-start.140 = (f32[8,128]{1,0:T(8,128)S(1)}, f32[8,128]{1,0:T(8,128)}, u32[]{:S(2)}) copy-start(f32[8,128]{1,0:T(8,128)} %get-tuple-element.1384) | copy-start | bytes 12292
  281.9 22.7 %copy-start.141 = (f32[8,128]{1,0:T(8,128)S(1)}, f32[8,128]{1,0:T(8,128)}, u32[]{:S(2)}) copy-start(f32[8,128]{1,0:T(8,128)} %get-tuple-element.1386) | copy-start | bytes 12292
  317.8 24.6 %copy-start.29 = (f32[80,8,128]{2,1,0:T(8,128)S(1)}, f32[80,8,128]{2,1,0:T(8,128)}, u32[]{:S(2)}) copy-start(f32[80,8,128]{2,1,0:T(8,128)} %get-tuple-element.1234) | copy-start | bytes 983044
  470.5 22.5 %copy-start.61 = (f32[10,8,128]{2,1,0:T(8,128)S(1)}, f32[10,8,128]{2,1,0:T(8,128)}, u32[]{:S(2)}) copy-start(f32[10,8,128]{2,1,0:T(8,128)} %get-tuple-element.1136) | copy-start | bytes 122884
  470.5 22.5 %copy-start.62 = (f32[10,8,128]{2,1,0:T(8,128)S(1)}, f32[10,8,128]{2,1,0:T(8,128)}, u32[]{:S(2)}) copy-start(f32[10,8,128]{2,1,0:T(8,128)} %get-tuple-element.1137) | copy-start | bytes 122884
  470.5 22.5 %copy-start.63 = (f32[10,8,128]{2,1,0:T(8,128)S(1)}, f32[10,8,128]{2,1,0:T(8,128)}, u32[]{:S(2)}) copy-start(f32[10,8,128]{2,1,0:T(8,128)} %get-tuple-element.1138) | copy-start | bytes 122884
  470.5 22.5 %copy-start.64 = (f32[10,8,128]{2,1,0:T(8,128)S(1)}, f32[10,8,128]{2,1,0:T(8,128)}, u32[]{:S(2)}) copy-start(f32[10,8,128]{2,1,0:T(8,128)} %get-tuple-element.1139) | copy-start | bytes 122884
  470.5 22.5 %copy-start.65 = (f32[10,8,128]{2,1,0:T(8,128)S(1)}, f32[10,8,128]{2,1,0:T(8,128)}, u32[]{:S(2)}) copy-start(f32[10,8,128]{2,1,0:T(8,128)} %get-tuple-element.1140) | copy-start | bytes 122884
  470.5 22.5 %copy-start.79 = (f32[8,128]{1,0:T(8,128)S(1)}, f32[8,128]{1,0:T(8,128)}, u32[]{:S(2)}) copy-start(f32[8,128]{1,0:T(8,128)} %get-tuple-element.1320) | copy-start | bytes 12292
  470.5 22.5 %copy-start.80 = (f32[8,128]{1,0:T(8,128)S(1)}, f32[8,128]{1,0:T(8,128)}, u32[]{:S(2)}) copy-start(f32[8,128]{1,0:T(8,128)} %get-tuple-element.1322) | copy-start | bytes 12292
  470.6 22.5 %copy-start.81 = (f32[8,128]{1,0:T(8,128)S(1)}, f32[8,128]{1,0:T(8,128)}, u32[]{:S(2)}) copy-start(f32[8,128]{1,0:T(8,128)} %get-tuple-element.1326) | copy-start | bytes 12292
  470.6 22.5 %copy-start.82 = (f32[8,128]{1,0:T(8,128)S(1)}, f32[8,128]{1,0:T(8,128)}, u32[]{:S(2)}) copy-start(f32[8,128]{1,0:T(8,128)} %get-tuple-element.1406) | copy-start | bytes 12292
  506.1 25.5 %copy-start.35 = (f32[80,8,128]{2,1,0:T(8,128)S(1)}, f32[80,8,128]{2,1,0:T(8,128)}, u32[]{:S(2)}) copy-start(f32[80,8,128]{2,1,0:T(8,128)} %get-tuple-element.1273) | copy-start | bytes 983044
  532.3 57.3 %copy-start.9 = (f32[80,6,128]{2,1,0:T(8,128)S(1)}, f32[80,6,128]{2,1,0:T(8,128)}, u32[]{:S(2)}) copy-start(f32[80,6,128]{2,1,0:T(8,128)} %get-tuple-element.1411) | copy-start | bytes 737284
  536.9 126.1 %collective-permute-start.15 = (f32[80,8,128]{2,1,0:T(8,128)S(1)}, f32[80,8,128]{2,1,0:T(8,128)}, u32[]{:S(2)}, u32[]{:S(2)}) collective-permute-start(f32[80,8,128]{2,1,0:T(8,128)S(1)} %scatter-add.419), channel_id=1, source_target_pairs={{0,232},{4,236},{8,240},{12,244},{16,248},{20,252},{24,0},{28,4},{... | collective-permute-start | bytes 983048 | tf_op jit(solution)/shard_map/ppermute | solution.py:19
  553.8 112.0 %collective-permute-start.14 = (f32[80,8,128]{2,1,0:T(8,128)}, f32[80,8,128]{2,1,0:T(8,128)}, u32[]{:S(2)}, u32[]{:S(2)}) collective-permute-start(f32[80,8,128]{2,1,0:T(8,128)} %scatter-add.406), channel_id=1, source_target_pairs={{0,236},{4,240},{8,244},{12,248},{16,252},{20,0},{24,4},{28,8},{32... | collective-permute-start | bytes 983048 | tf_op jit(solution)/shard_map/ppermute | solution.py:19
  564.6 101.1 %collective-permute-start.13 = (f32[80,8,128]{2,1,0:T(8,128)}, f32[80,8,128]{2,1,0:T(8,128)}, u32[]{:S(2)}, u32[]{:S(2)}) collective-permute-start(f32[80,8,128]{2,1,0:T(8,128)} %scatter-add.384), channel_id=1, source_target_pairs={{0,240},{4,244},{8,248},{12,252},{16,0},{20,4},{24,8},{28,12},{32,... | collective-permute-start | bytes 983048 | tf_op jit(solution)/shard_map/ppermute | solution.py:19
  575.5 90.3 %collective-permute-start.12 = (f32[80,8,128]{2,1,0:T(8,128)}, f32[80,8,128]{2,1,0:T(8,128)}, u32[]{:S(2)}, u32[]{:S(2)}) collective-permute-start(f32[80,8,128]{2,1,0:T(8,128)} %scatter-add.360), channel_id=1, source_target_pairs={{0,244},{4,248},{8,252},{12,0},{16,4},{20,8},{24,12},{28,16},{32,2... | collective-permute-start | bytes 983048 | tf_op jit(solution)/shard_map/ppermute | solution.py:19
  589.0 76.7 %collective-permute-start.11 = (f32[80,8,128]{2,1,0:T(8,128)}, f32[80,8,128]{2,1,0:T(8,128)}, u32[]{:S(2)}, u32[]{:S(2)}) collective-permute-start(f32[80,8,128]{2,1,0:T(8,128)} %scatter-add.336), channel_id=1, source_target_pairs={{0,248},{4,252},{8,0},{12,4},{16,8},{20,12},{24,16},{28,20},{32,24... | collective-permute-start | bytes 983048 | tf_op jit(solution)/shard_map/ppermute | solution.py:19
  599.5 42.1 %copy-start.14 = (bf16[80,8,128]{2,1,0:T(8,128)(2,1)S(1)}, bf16[80,8,128]{2,1,0:T(8,128)(2,1)}, u32[]{:S(2)}) copy-start(bf16[80,8,128]{2,1,0:T(8,128)(2,1)} %param.175) | copy-start | bytes 491524
  599.5 42.1 %copy-start.17 = (bf16[80,8,128]{2,1,0:T(8,128)(2,1)S(1)}, bf16[80,8,128]{2,1,0:T(8,128)(2,1)}, u32[]{:S(2)}) copy-start(bf16[80,8,128]{2,1,0:T(8,128)(2,1)} %copy-done.15) | copy-start | bytes 491524
  599.5 42.1 %copy-start.48 = (f32[10,8,128]{2,1,0:T(8,128)S(1)}, f32[10,8,128]{2,1,0:T(8,128)}, u32[]{:S(2)}) copy-start(f32[10,8,128]{2,1,0:T(8,128)} %copy-done.47) | copy-start | bytes 122884
  621.2 25.1 %all-to-all-start.1 = ((bf16[48,10,8,128]{3,2,1,0:T(8,128)(2,1)}), bf16[48,10,8,128]{3,2,1,0:T(8,128)(2,1)}, u32[]{:S(2)}, u32[]{:S(2)}) async-start(bf16[48,10,8,128]{3,2,1,0:T(8,128)(2,1)} %constant_dynamic-update-slice_fusion.15), calls=%async_computation.1 | async-start | bytes 1966080 | tf_op jit(solution)/shard_map/all_to_all | solution.py:92
  625.4 292.7 %all-reduce.9.cloned.1.call-start = ((), (), s32[]{:S(2)}) async-start(), calls=%async_computation.2 | async-start | bytes 884736 | tf_op jit(solution)/shard_map/psum | solution.py:97
  662.6 257.3 %copy-start.1 = (bf16[32,40,3,3,3]{1,0,4,3,2:T(8,128)(2,1)S(1)}, bf16[32,40,3,3,3]{1,0,4,3,2:T(8,128)(2,1)}, u32[]{:S(2)}) copy-start(bf16[32,40,3,3,3]{1,0,4,3,2:T(8,128)(2,1)} %param.177) | copy-start | bytes 207364
  663.1 10.0 %collective-permute-start.10 = (f32[80,8,128]{2,1,0:T(8,128)S(1)}, f32[80,8,128]{2,1,0:T(8,128)S(1)}, u32[]{:S(2)}, u32[]{:S(2)}) collective-permute-start(f32[80,8,128]{2,1,0:T(8,128)S(1)} %copy-done.37), channel_id=1, source_target_pairs={{0,252},{4,0},{8,4},{12,8},{16,12},{20,16},{24,20},{28,24},{32,28}... | collective-permute-start | bytes 983048 | tf_op jit(solution)/shard_map/ppermute | solution.py:19
  (114 other events, 1209.2 us)
Sparse Core Ops, SparseCore 0:
  665.9 252.2 all-reduce.8
where the time goes:
time: 946 us; the launch traced here: 927 us
  other arithmetic  313 us (33%)
  waiting for transfers between devices  263 us (28%)
  local copies, waits for them, and re-layouts  254 us (27%)
  starting transfers between devices  45.7 us (5%)
  matrix products  34.5 us (4%)
  between operations  17.1 us (2%)
    psum x1, waiting for transfers between devices, shards(): weight_grad = lax.psum(filter_part, ('lon', 'grp')) * grad_scale  243 us
    scatter-add x30, local copies, waits for them, and re-layouts, shards(): blocks[first_block + 1].at[:, :inner, :]  107 us
    scatter-add x30, local copies, waits for them, and re-layouts, shards(): blocks[first_block].at[:, inner:, :]  104 us
    reduce_sum x48, other arithmetic, shards(): cost_list.append(jnp.sum(product, axis=1) / CG)  73.3 us
    unnamed x47, other arithmetic  62.7 us
    add x29, other arithmetic, shards(): blocks[first_block + 1].at[:, :inner, :]  38.2 us
    add x24, other arithmetic, shards(): blocks[first_block].at[:, inner:, :]  34.4 us
    convert_element_type x48, other arithmetic, shards(): chosen = (disparity_shift == disparity).astype(jnp.float32)  28.4 us
  transfers between devices with their start and end apart: 19, of which 5 were waited for; matrix products, arithmetic and copies ran while one was open for 31% of the time, Pallas kernels for 0%

commit v1 on v0

v1 whole, which is shorter than its diff:
```python
import functools
import math

import jax
import jax.numpy as jnp
import numpy as np
from jax import lax
from jax.experimental import pallas as pl
from jax.experimental.pallas import tpu as pltpu
from jax.sharding import PartitionSpec as P

CG = 8
DISP = 48
OUTC = 32
COLS_HERE = 8
BLOCKS = 7
ROWS = 384
F32 = jnp.float32
BF16 = jnp.bfloat16
MIB = 1024 * 1024


def filter_column():
    index = np.arange(ROWS)
    own, left = index < 256, index < 320
    column = np.where(own, index % 8, np.where(left, index % 2 - 2, index % 2 + 8))
    channel = np.where(own, index // 8, np.where(left, (index - 256) // 2, (index - 320) // 2))
    return column, channel


def plane_copies(rank, own, halo, planes, first, sems):
    copies = []
    for k in range(4):
        start = (rank ^ k) * 12 + first
        copies.append(
            pltpu.make_async_copy(
                own[k], planes.at[pl.ds(start, 12), pl.ds(0, 256)], sems.at[k]
            )
        )
        copies.append(
            pltpu.make_async_copy(
                halo[k], planes.at[pl.ds(start, 12), pl.ds(256, 128)], sems.at[4 + k]
            )
        )
    return copies


def conv_kernel(rank_ref, kernel_ref, *refs):
    own, halo = refs[0:4], refs[4:8]
    out_ref, planes, sems = refs[8:]
    copies = plane_copies(rank_ref[0], own, halo, planes, 2, sems)
    for copy in copies:
        copy.start()
    planes[0:2] = jnp.zeros((2, ROWS, 128), BF16)
    planes[50:52] = jnp.zeros((2, ROWS, 128), BF16)
    for copy in copies:
        copy.wait()
    lane = lax.broadcasted_iota(jnp.int32, (80, 128), 1)

    def pair(index, carry):
        d = index * 2
        parts = []
        for a in range(3):
            parts.append(
                jnp.concatenate([planes[d + 4 - 2 * a], planes[d + 5 - 2 * a]], axis=1)
            )
        columns = jnp.concatenate(parts, axis=0)
        product = jnp.dot(kernel_ref[...], columns, preferred_element_type=F32)
        for half in range(2):
            part = product[:, half * 128 : half * 128 + 128]
            ahead = jnp.where(lane < 126, pltpu.roll(part[0:80], 126, 1), 0.0)
            behind = jnp.where(lane >= 2, pltpu.roll(part[160:240], 2, 1), 0.0)
            out_ref[d + half] = (part[80:160] + ahead + behind).astype(BF16)
        return carry

    lax.fori_loop(0, 24, pair, 0)


def rolled(value, steps, axis):
    return value if steps == 0 else pltpu.roll(value, steps, axis)


def widen(left_ref, panels, left_rolls, wide):
    def two(index, carry):
        rows = pl.ds(pl.multiple_of(index * 16, 16), 16)
        value = left_ref[rows, :].astype(F32)
        for half in range(2):
            part = value[half * 8 : half * 8 + 8]
            place = pl.ds(pl.multiple_of(index * 16 + half * 8, 8), 8)
            for r in range(8):
                left_rolls[r, place, :] = rolled(part, (8 - r) % 8, 0)
        for b in range(BLOCKS):
            wide[b, rows, :] = panels[b][rows, :].astype(F32)
        return carry

    lax.fori_loop(0, 40, two, 0)


def cost_kernel(rank_ref, left_ref, *refs):
    panels = refs[0:7]
    own, halo = refs[7:11], refs[11:15]
    mask_ref, sum_ref, out_ref, left_rolls, wide, planes, volume, total, sems = refs[15:]
    copies = plane_copies(rank_ref[0], own, halo, planes, 0, sems)
    for copy in copies:
        copy.start()
    widen(left_ref, panels, left_rolls, wide)
    volume[0:2] = jnp.zeros((2, 240, 128), BF16)
    volume[50:52] = jnp.zeros((2, 240, 128), BF16)
    row = lax.broadcasted_iota(jnp.int32, (8, 128), 0)
    lane = lax.broadcasted_iota(jnp.int32, (16, 128), 1)

    def groups(index, carry):
        base = index * 128
        for r in range(8):
            sums = []
            for half in range(2):
                line = []
                for b in range(BLOCKS):
                    acc = None
                    for c in range(CG):
                        place = pl.ds(pl.multiple_of(base + half * 64 + c * 8, 8), 8)
                        term = left_rolls[r, place, :] * wide[b, place, :]
                        acc = term if acc is None else acc + term
                    line.append(acc)
                sums.append(line)
            for q in range(6):
                both = []
                for half in range(2):
                    line = sums[half]
                    mixed = jnp.where(row <= 7 - r, line[6 - q], line[5 - q]) if r else line[6 - q]
                    both.append(rolled(mixed, r, 0))
                cost = jnp.concatenate(both, axis=0) * (1.0 / CG)
                d = 8 * q + r
                later = jnp.where(lane >= 2, pltpu.roll(cost, 2, 1), 0.0)
                sooner = jnp.where(lane < 126, pltpu.roll(cost, 126, 1), 0.0)
                for e, value in enumerate((later, cost, sooner)):
                    place = pl.ds(pl.multiple_of(e * 80 + index * 16, 16), 16)
                    volume[d + 2, place, :] = value.astype(BF16)
        return carry

    lax.fori_loop(0, 5, groups, 0)
    for copy in copies:
        copy.wait()
    total[...] = jnp.zeros_like(total)

    def chunk(index, carry):
        d = index * 8
        cot = jnp.concatenate([planes[d + j] for j in range(8)], axis=1)
        for a in range(3):
            cost = jnp.concatenate([volume[d + j + 2 * a] for j in range(8)], axis=1)
            total[a] += lax.dot_general(
                cost, cot, (((1,), (1,)), ((), ())), preferred_element_type=F32
            )
        return carry

    lax.fori_loop(0, 6, chunk, 0)
    out_ref[...] = jnp.zeros_like(out_ref)
    for a in range(3):
        terms = total[a].reshape(30, 8, ROWS)
        for b in range(3):
            picked = jnp.sum(terms * mask_ref[b][None], axis=1)
            out_ref[a * 32 : a * 32 + 30, b * 32 : b * 32 + 32] = jnp.dot(
                picked, sum_ref[...], preferred_element_type=F32, precision=lax.Precision.HIGHEST
            )


def grad_kernel(left_ref, *refs):
    panels = refs[0:7]
    grad_ref, shift_ref, valid_ref = refs[7:10]
    left_out, right_out = refs[10], refs[11:18]
    left_rolls, wide, chosen, counts, weights = refs[18:]
    widen(left_ref, panels, left_rolls, wide)
    row = lax.broadcasted_iota(jnp.int32, (8, 128), 0)
    valid = valid_ref[...].astype(F32)
    shift = shift_ref[...]
    for r in range(8):
        shift_r = rolled(shift, (8 - r) % 8, 0)
        valid_r = rolled(valid, (8 - r) % 8, 0)
        for b in range(BLOCKS):
            q = 6 - b
            at = jnp.where(row <= 7 - r, 8 * q + r, 8 * (q - 1) + r)
            chosen[b, r] = jnp.where(shift_r == at, valid_r, 0.0)
    for b in range(BLOCKS):
        count = chosen[b, 0]
        for r in range(1, 8):
            count = count + chosen[b, r]
        counts[b] = 0.5 * count

    def groups(index, carry):
        pair_rows = pl.ds(pl.multiple_of(index * 16, 16), 16)
        for r in range(8):
            lines = [[], []]
            for q in range(6):
                value = grad_ref[8 * q + r, pair_rows, :].astype(F32)
                for half in range(2):
                    lines[half].append(rolled(value[half * 8 : half * 8 + 8], (8 - r) % 8, 0))
            for half in range(2):
                for b in range(BLOCKS):
                    low = lines[half][6 - b] if b > 0 else 0.0
                    high = lines[half][5 - b] if b < 6 else 0.0
                    mixed = jnp.where(row <= 7 - r, low, high)
                    weights[half, b, r] = mixed * (1.0 / CG) - 0.5 * chosen[b, r]
        base = index * 128
        for half in range(2):
            for b in range(BLOCKS):
                factors = [weights[half, b, r] for r in range(8)]
                count = counts[b]
                for c in range(0, CG, 2):
                    both = []
                    for k in range(2):
                        place = pl.ds(pl.multiple_of(base + half * 64 + (c + k) * 8, 8), 8)
                        acc = count * wide[b, place, :]
                        for r in range(8):
                            acc = acc + factors[r] * left_rolls[r, place, :]
                        both.append(acc)
                    place = pl.ds(pl.multiple_of(base + half * 64 + c * 8, 16), 16)
                    right_out[b][place, :] = jnp.concatenate(both, axis=0).astype(
                        right_out[b].dtype
                    )
            sums = []
            for c in range(CG):
                place = pl.ds(pl.multiple_of(base + half * 64 + c * 8, 8), 8)
                sums.append(0.5 * valid * left_rolls[0, place, :])
            for r in range(8):
                factors = [weights[half, b, r] for b in range(BLOCKS)]
                for c in range(CG):
                    place = pl.ds(pl.multiple_of(base + half * 64 + c * 8, 8), 8)
                    acc = factors[0] * wide[0, place, :]
                    for b in range(1, BLOCKS):
                        acc = acc + factors[b] * wide[b, place, :]
                    sums[c] = sums[c] + rolled(acc, r, 0)
            for c in range(CG):
                place = pl.ds(pl.multiple_of(base + half * 64 + c * 8, 8), 8)
                left_out[place, :] = sums[c]
        return carry

    lax.fori_loop(0, 5, groups, 0)


SMEM = pl.BlockSpec(memory_space=pltpu.SMEM)
VMEM = pl.BlockSpec(memory_space=pltpu.VMEM)
ANY = pl.BlockSpec(memory_space=pl.ANY)


def run_conv(rank, kernel, own, halo):
    return pl.pallas_call(
        conv_kernel,
        out_shape=jax.ShapeDtypeStruct((DISP, 80, 128), BF16),
        in_specs=[SMEM, VMEM] + [ANY] * 8,
        out_specs=VMEM,
        scratch_shapes=[pltpu.VMEM((52, ROWS, 128), BF16), pltpu.SemaphoreType.DMA((8,))],
        compiler_params=pltpu.CompilerParams(vmem_limit_bytes=20 * MIB),
        cost_estimate=pl.CostEstimate(flops=15_000_000_000, bytes_accessed=8_000_000, transcendentals=0),
        name="filter_transpose",
    )(rank, kernel, *own, *halo)


def run_cost(rank, left, panels, own, halo):
    column, channel = filter_column()
    w = np.arange(8)[None, :, None]
    b = np.arange(3)[:, None, None]
    mask = (w == column[None, None, :] + 2 * b - 2).astype(np.float32)
    summing = (channel[:, None] == np.arange(OUTC)[None]).astype(np.float32)
    return pl.pallas_call(
        cost_kernel,
        out_shape=jax.ShapeDtypeStruct((96, 128), F32),
        in_specs=[SMEM, VMEM] + [VMEM] * 7 + [ANY] * 8 + [VMEM] * 2,
        out_specs=VMEM,
        scratch_shapes=[
            pltpu.VMEM((8, 640, 128), F32),
            pltpu.VMEM((BLOCKS, 640, 128), F32),
            pltpu.VMEM((DISP, ROWS, 128), BF16),
            pltpu.VMEM((52, 240, 128), BF16),
            pltpu.VMEM((3, 240, ROWS), F32),
            pltpu.SemaphoreType.DMA((8,)),
        ],
        compiler_params=pltpu.CompilerParams(vmem_limit_bytes=32 * MIB),
        cost_estimate=pl.CostEstimate(flops=15_000_000_000, bytes_accessed=8_000_000, transcendentals=0),
        name="cost_and_filter_grad",
    )(rank, left, *panels, *own, *halo, jnp.asarray(mask), jnp.asarray(summing))


def run_grad(left, panels, grad_cost, shift, valid):
    return pl.pallas_call(
        grad_kernel,
        out_shape=[jax.ShapeDtypeStruct((640, 128), F32)]
        + [jax.ShapeDtypeStruct((640, 128), BF16)] * 6
        + [jax.ShapeDtypeStruct((640, 128), F32)],
        in_specs=[VMEM] * 11,
        out_specs=[VMEM] * 8,
        scratch_shapes=[
            pltpu.VMEM((8, 640, 128), F32),
            pltpu.VMEM((BLOCKS, 640, 128), F32),
            pltpu.VMEM((BLOCKS, 8, 8, 128), F32),
            pltpu.VMEM((BLOCKS, 8, 128), F32),
            pltpu.VMEM((2, BLOCKS, 8, 8, 128), F32),
        ],
        compiler_params=pltpu.CompilerParams(vmem_limit_bytes=32 * MIB),
        cost_estimate=pl.CostEstimate(flops=8_000_000_000, bytes_accessed=4_000_000, transcendentals=0),
        name="feature_grads",
    )(left, *panels, grad_cost, shift, valid)


def conv_matrix(conv_weight, rank):
    column, channel = filter_column()
    local = lax.dynamic_slice_in_dim(conv_weight, rank * 10, 10, axis=1)
    taps = local.transpose(4, 1, 2, 3, 0)
    spread = (np.arange(OUTC)[:, None] == channel[None]).astype(np.float32)
    placed = jnp.einsum(
        "egabo,oc->egabc", taps, jnp.asarray(spread, BF16), preferred_element_type=BF16
    )
    w = np.arange(8)[None, :, None]
    b = np.arange(3)[:, None, None]
    fits = column[None, None, :] == w - 2 * b + 2
    total = None
    for tap in range(3):
        term = jnp.where(
            jnp.asarray(fits[tap])[None, None, :, None, :], placed[:, :, None, :, tap, :], 0
        )
        total = term if total is None else total + term
    return total.reshape(240, 3 * ROWS).astype(BF16)


def moved(value, axis, place):
    pairs = [(i, place(i)) for i in range(lax.axis_size(axis))]
    return lax.ppermute(value, axis, pairs)


def along(value, steps):
    count = lax.axis_size("lon")
    return moved(value, "lon", lambda i: (i + steps) % count)


def across(value, bits):
    return moved(value, "grp", lambda i: i ^ bits)


def summed_over_lon(value):
    total = value
    for k in range(1, 4):
        total = total + moved(value, "lon", lambda i: i - i % 4 + (i + k) % 4)
    value = total
    for k in range(1, 8):
        total = total + moved(value, "lon", lambda i: i - i % 32 + (i + 4 * k) % 32)
    return total + moved(total, "lon", lambda i: i ^ 32)


def shards(left_feat, right_feat, conv_cot, conv_weight, disparity_shift, valid_mask):
    rank = lax.axis_index("grp")
    rank_array = rank.astype(jnp.int32).reshape(1)
    panels = [along(right_feat, k).reshape(640, 128) for k in range(6, 0, -1)]
    panels.append(right_feat.reshape(640, 128))
    left = left_feat.reshape(640, 128)

    own = conv_cot.reshape(12, 256, 128)
    own_far = across(own, 2)
    before = along(conv_cot[:, :, 6:].reshape(12, 64, 128), 1)
    after = along(conv_cot[:, :, :2].reshape(12, 64, 128), -1)
    halo = jnp.concatenate([before, after], axis=1)
    halo_far = across(halo, 2)
    owns = [own, across(own, 1), own_far, across(own_far, 1)]
    halos = [halo, across(halo, 1), halo_far, across(halo_far, 1)]

    grad_cost = run_conv(rank_array, conv_matrix(conv_weight, rank), owns, halos)
    filter_part = run_cost(rank_array, left, panels, owns, halos)
    outs = run_grad(left, panels, grad_cost, disparity_shift, valid_mask)
    left_grad = outs[0].reshape(80, 8, 128)
    right_grad = outs[7]
    for k in range(1, 7):
        right_grad = right_grad + along(outs[1 + 6 - k], -k).astype(F32)
    right_grad = right_grad.reshape(80, 8, 128)

    total = summed_over_lon(filter_part)
    pieces = [total] + [across(total, k) for k in range(1, 4)]
    odd, high = (rank & 1) == 1, (rank & 2) == 2
    pieces = [jnp.where(odd, pieces[k ^ 1], pieces[k]) for k in range(4)]
    pieces = [jnp.where(high, pieces[k ^ 2], pieces[k]) for k in range(4)]
    scale = 1.0 / math.sqrt(DISP * 8 * lax.axis_size("lon") * 128)
    whole = jnp.stack(pieces)[:, :, :96].reshape(4, 3, 32, 3, OUTC)[:, :, :30]
    whole = whole.reshape(4, 3, 3, 10, 3, OUTC) * scale
    weight_grad = whole.transpose(5, 0, 3, 1, 4, 2).reshape(OUTC, 40, 3, 3, 3)
    return (left_grad, right_grad, weight_grad)


def solution(mesh):
    placed = (
        P("grp", "lon", None),
        P("grp", "lon", None),
        P("grp", None, "lon", None),
        P(),
        P("lon", None),
        P("lon", None),
    )
    return jax.shard_map(
        shards,
        mesh=mesh,
        in_specs=placed,
        out_specs=(P("grp", "lon", None), P("grp", "lon", None), P()),
        check_vma=False,
    )
```

time: 946 us -> 149 us (0.16)
  the two profiles are of different devices: /device:TPU:4 before, /device:TPU:69 now
where the time goes in v1:
time: 149 us; the launch traced here: 148 us
  starting transfers between devices  84.4 us (57%)
  Pallas kernels  27.9 us (19%)
  waiting for transfers between devices  25 us (17%)
  local copies, waits for them, and re-layouts  7.51 us (5%)
    ppermute x34, starting transfers between devices, moved(): return lax.ppermute(value, axis, pairs)  84.4 us
    ppermute x34, waiting for transfers between devices, moved(): return lax.ppermute(value, axis, pairs)  25 us
    pallas_call x1, Pallas kernels, run_cost(): pl.pallas_call(cost_kernel, out_shape=jax.ShapeDtypeStruct((96, 128), F32...  11.4 us
    pallas_call x1, Pallas kernels, run_conv(): pl.pallas_call(conv_kernel, out_shape=jax.ShapeDtypeStruct((DISP, 80, 128...  11.1 us
    pallas_call x1, Pallas kernels, run_grad(): pl.pallas_call(grad_kernel, out_shape=[jax.ShapeDtypeStruct((640, 128), F...  5.4 us
    unnamed x35, local copies, waits for them, and re-layouts  4.22 us
  transfers between devices with their start and end apart: 34, of which 7 were waited for; matrix products, arithmetic and copies ran while one was open for 5% of the time, Pallas kernels for 11%

profile of v1, /device:TPU:69, one launch (start us, length us, event | category | flops | bytes accessed | tf_op | source)
XLA Modules:
  0.0 148.4 jit_solution(16453281652786008311)
XLA Ops:
  0.7 3.0 %collective-permute-start.7 = (bf16[12,256,128]{2,1,0:T(8,128)(2,1)}, bf16[12,256,128]{2,1,0:T(8,128)(2,1)S(1)}, u32[]{:S(2)}, u32[]{:S(2)}) collective-permute-start(bf16[12,256,128]{2,1,0:T(8,128)(2,1)} %bitcast.44), channel_id=1, source_target_pairs={{0,2},{1,3},{2,0},{3,1},{4,6},{5,7},{6,4},{7,5},{8,10},{9,11},{10,... | collective-permute-start | bytes 2359304 | tf_op jit(solution)/shard_map/ppermute | solution.py:326
  3.7 1.8 %fusion.2 = (bf16[12,32,2,128]{3,2,1,0:T(2,128)(2,1)S(1)}, bf16[12,32,2,128]{3,2,1,0:T(2,128)(2,1)S(1)}) fusion(bf16[12,32,8,128]{3,2,1,0:T(8,128)(2,1)} %param.14), kind=kLoop, calls=%fused_computation.25 | loop fusion | bytes 786432 | tf_op jit(solution)/shard_map/slice | solution.py:358
  5.5 1.0 collective-permute-start.9
  6.5 0.5 collective-permute-start.10
  7.0 4.0 %collective-permute-done.9 = bf16[12,64,128]{2,1,0:T(8,128)(2,1)S(1)} collective-permute-done((bf16[12,64,128]{2,1,0:T(8,128)(2,1)S(1)}, bf16[12,64,128]{2,1,0:T(8,128)(2,1)S(1)}, u32[]{:S(2)}, u32[]{:S(2)}) %collective-permute-start.9) | collective-permute-done | bytes 196640 | tf_op jit(solution)/shard_map/ppermute | solution.py:326
  11.0 0.8 collective-permute-done.10
  11.8 0.3 collective-permute-start.12
  12.1 3.5 %collective-permute-start.4 = (bf16[80,8,128]{2,1,0:T(8,128)(2,1)S(1)}, bf16[80,8,128]{2,1,0:T(8,128)(2,1)S(1)}, u32[]{:S(2)}, u32[]{:S(2)}) collective-permute-start(bf16[80,8,128]{2,1,0:T(8,128)(2,1)S(1)} %copy-done.3), channel_id=1, source_target_pairs={{0,8},{4,12},{8,16},{12,20},{16,24},{20,28},{24,32},{28,36},{32,40... | collective-permute-start | bytes 491528 | tf_op jit(solution)/shard_map/ppermute | solution.py:326
  15.6 4.9 %collective-permute-start.3 = (bf16[80,8,128]{2,1,0:T(8,128)(2,1)S(1)}, bf16[80,8,128]{2,1,0:T(8,128)(2,1)S(1)}, u32[]{:S(2)}, u32[]{:S(2)}) collective-permute-start(bf16[80,8,128]{2,1,0:T(8,128)(2,1)S(1)} %copy-done.3), channel_id=1, source_target_pairs={{0,12},{4,16},{8,20},{12,24},{16,28},{20,32},{24,36},{28,40},{32,4... | collective-permute-start | bytes 491528 | tf_op jit(solution)/shard_map/ppermute | solution.py:326
  20.6 2.9 %collective-permute-start.6 = (bf16[12,256,128]{2,1,0:T(8,128)(2,1)S(1)}, bf16[12,256,128]{2,1,0:T(8,128)(2,1)S(1)}, u32[]{:S(2)}, u32[]{:S(2)}) collective-permute-start(bf16[12,256,128]{2,1,0:T(8,128)(2,1)S(1)} %bitcast.45), channel_id=1, source_target_pairs={{0,1},{1,0},{2,3},{3,2},{4,5},{5,4},{6,7},{7,6},{8,9},{9,8},{10,11... | collective-permute-start | bytes 2359304 | tf_op jit(solution)/shard_map/ppermute | solution.py:326
  23.6 0.7 copy-done.4
  24.3 1.6 %collective-permute-start.2 = (bf16[80,8,128]{2,1,0:T(8,128)(2,1)S(1)}, bf16[80,8,128]{2,1,0:T(8,128)(2,1)}, u32[]{:S(2)}, u32[]{:S(2)}) collective-permute-start(bf16[80,8,128]{2,1,0:T(8,128)(2,1)S(1)} %copy-done.3), channel_id=1, source_target_pairs={{0,16},{4,20},{8,24},{12,28},{16,32},{20,36},{24,40},{28,44},{32,4... | collective-permute-start | bytes 491528 | tf_op jit(solution)/shard_map/ppermute | solution.py:326
  25.9 0.7 copy-done.6
  26.5 3.5 %collective-permute-start.1 = (bf16[80,8,128]{2,1,0:T(8,128)(2,1)S(1)}, bf16[80,8,128]{2,1,0:T(8,128)(2,1)}, u32[]{:S(2)}, u32[]{:S(2)}) collective-permute-start(bf16[80,8,128]{2,1,0:T(8,128)(2,1)S(1)} %copy-done.3), channel_id=1, source_target_pairs={{0,20},{4,24},{8,28},{12,32},{16,36},{20,40},{24,44},{28,48},{32,5... | collective-permute-start | bytes 491528 | tf_op jit(solution)/shard_map/ppermute | solution.py:326
  30.0 0.8 constant_dynamic-slice_fusion
  30.8 1.8 %copy.27 = bf16[32,10,3,3,3]{0,1,3,2,4:T(8,128)(2,1)} copy(bf16[32,10,3,3,3]{1,0,4,3,2:T(8,128)(2,1)} %constant_dynamic-slice_fusion) | data formatting | bytes 34560
  32.7 1.4 collective-permute-start
  34.1 5.4 %collective-permute-start.11 = (bf16[12,128,128]{2,1,0:T(8,128)(2,1)S(1)}, bf16[12,128,128]{2,1,0:T(8,128)(2,1)S(1)}, u32[]{:S(2)}, u32[]{:S(2)}) collective-permute-start(bf16[12,128,128]{2,1,0:T(8,128)(2,1)S(1)} %constant_dynamic-update-slice_fusion.refs_4_.refs_11_), channel_id=1, source_target_pairs={{0,1},{1,0},{2,3},{3,2},{4,5},{5,4},{6,7},{7,6},{8,9},{9,8},{10,11... | collective-permute-start | bytes 1179656 | tf_op jit(solution)/shard_map/ppermute | solution.py:326
  39.5 1.1 fusion
  40.6 4.7 %collective-permute-done = bf16[80,8,128]{2,1,0:T(8,128)(2,1)S(1)} collective-permute-done((bf16[80,8,128]{2,1,0:T(8,128)(2,1)S(1)}, bf16[80,8,128]{2,1,0:T(8,128)(2,1)S(1)}, u32[]{:S(2)}, u32[]{:S(2)}) %collective-permute-start) | collective-permute-done | bytes 163872 | tf_op jit(solution)/shard_map/ppermute | solution.py:326
  45.4 1.3 collective-permute-start.5
  46.9 9.3 %collective-permute-done.5 = bf16[80,8,128]{2,1,0:T(8,128)(2,1)S(1)} collective-permute-done((bf16[80,8,128]{2,1,0:T(8,128)(2,1)S(1)}, bf16[80,8,128]{2,1,0:T(8,128)(2,1)S(1)}, u32[]{:S(2)}, u32[]{:S(2)}) %collective-permute-start.5) | collective-permute-done | bytes 163872 | tf_op jit(solution)/shard_map/ppermute | solution.py:326
  56.3 11.4 %cost_and_filter_grad.1 = f32[96,128]{1,0:T(8,128)S(1)} custom-call(s32[1]{0:T(128)} %bitcast.8.rank_ref, bf16[640,128]{1,0:T(8,128)(2,1)S(1)} %bitcast.48, bf16[640,128]{1,0:T(8,128)(2,1)S(1)} %bitcast.56, bf16[640,128]{1,0:T(8,128)(2,1)} %bitcast.2.refs_1_, bf16[640,128]{1,0:T(8,128)(2,1)} %bitcast.3.refs_2_, bf16[640,128]{1,0:T(8,128)(2,1)S(1)} %bitcast.54, ...), custom_call_target="tpu_custom_call" | custom-call | flops 15000000512 | bytes 8000000 | tf_op jit(solution)/shard_map/cost_and_filter_grad/pallas_call | solution.py:264
  67.8 1.2 collective-permute-start.22
  69.0 1.9 %collective-permute-start.20 = (f32[96,128]{1,0:T(8,128)S(1)}, f32[96,128]{1,0:T(8,128)S(1)}, u32[]{:S(2)}, u32[]{:S(2)}) collective-permute-start(f32[96,128]{1,0:T(8,128)S(1)} %cost_and_filter_grad.1), channel_id=1, source_target_pairs={{0,4},{4,8},{8,12},{12,0},{16,20},{20,24},{24,28},{28,16},{32,36},... | collective-permute-start | bytes 147464 | tf_op jit(solution)/shard_map/ppermute | solution.py:326
  70.9 0.3 select_add_fusion
  71.2 2.2 %collective-permute-done.21 = f32[96,128]{1,0:T(8,128)S(1)} collective-permute-done((f32[96,128]{1,0:T(8,128)S(1)}, f32[96,128]{1,0:T(8,128)S(1)}, u32[]{:S(2)}, u32[]{:S(2)}) %collective-permute-start.21) | collective-permute-done | bytes 49184 | tf_op jit(solution)/shard_map/ppermute | solution.py:326
  73.5 1.1 collective-permute-start.29
  74.6 5.6 %collective-permute-start.28 = (f32[96,128]{1,0:T(8,128)S(1)}, f32[96,128]{1,0:T(8,128)S(1)}, u32[]{:S(2)}, u32[]{:S(2)}) collective-permute-start(f32[96,128]{1,0:T(8,128)S(1)} %add_add_fusion.1), channel_id=1, source_target_pairs={{0,96},{4,100},{8,104},{12,108},{16,112},{20,116},{24,120},{28,124... | collective-permute-start | bytes 147464 | tf_op jit(solution)/shard_map/ppermute | solution.py:326
  80.2 11.1 %filter_transpose.1.refs_7_ = bf16[48,80,128]{2,1,0:T(8,128)(2,1)S(1)} custom-call(s32[1]{0:T(128)} %bitcast.8.rank_ref, bf16[240,1152]{1,0:T(8,128)(2,1)S(1)} %bitcast.43, bf16[12,256,128]{2,1,0:T(8,128)(2,1)S(1)} %bitcast.47, bf16[12,256,128]{2,1,0:T(8,128)(2,1)S(1)} %collective-permute-done.6.refs_1_.refs_8_, ...), custom_call_target="tpu_custom_call" | custom-call | flops 15000000512 | bytes 8000000 | tf_op jit(solution)/shard_map/filter_transpose/pallas_call | solution.py:246
  91.4 5.6 %collective-permute-start.26 = (f32[96,128]{1,0:T(8,128)S(1)}, f32[96,128]{1,0:T(8,128)S(1)}, u32[]{:S(2)}, u32[]{:S(2)}) collective-permute-start(f32[96,128]{1,0:T(8,128)S(1)} %add_add_fusion.1), channel_id=1, source_target_pairs={{0,64},{4,68},{8,72},{12,76},{16,80},{20,84},{24,88},{28,92},{32,9... | collective-permute-start | bytes 147464 | tf_op jit(solution)/shard_map/ppermute | solution.py:326
  97.0 1.3 collective-permute-start.24
  98.2 2.3 %collective-permute-start.23 = (f32[96,128]{1,0:T(8,128)S(1)}, f32[96,128]{1,0:T(8,128)S(1)}, u32[]{:S(2)}, u32[]{:S(2)}) collective-permute-start(f32[96,128]{1,0:T(8,128)S(1)} %add_add_fusion.1), channel_id=1, source_target_pairs={{0,16},{4,20},{8,24},{12,28},{16,32},{20,36},{24,40},{28,44},{32,4... | collective-permute-start | bytes 147464 | tf_op jit(solution)/shard_map/ppermute | solution.py:326
  100.6 5.4 %feature_grads.1 = (f32[640,128]{1,0:T(8,128)}, bf16[640,128]{1,0:T(8,128)(2,1)S(1)}, bf16[640,128]{1,0:T(8,128)(2,1)S(1)}, bf16[640,128]{1,0:T(8,128)(2,1)S(1)}...) custom-call(bf16[640,128]{1,0:T(8,128)(2,1)S(1)} %bitcast.49, ...), custom_call_target="tpu_custom_call" | custom-call | flops 8000000000 | bytes 4000000 | tf_op jit(solution)/shard_map/feature_grads/pallas_call | solution.py:284
  106.0 1.3 collective-permute-start.14
  107.3 1.9 %collective-permute-start.30 = (f32[96,128]{1,0:T(8,128)S(1)}, f32[96,128]{1,0:T(8,128)S(1)}, u32[]{:S(2)}, u32[]{:S(2)}) collective-permute-start(f32[96,128]{1,0:T(8,128)S(1)} %add_add_fusion), channel_id=1, source_target_pairs={{0,128},{4,132},{8,136},{12,140},{16,144},{20,148},{24,152},{28,15... | collective-permute-start | bytes 147464 | tf_op jit(solution)/shard_map/ppermute | solution.py:326
  109.2 1.8 %collective-permute-start.15 = (bf16[640,128]{1,0:T(8,128)(2,1)S(1)}, bf16[640,128]{1,0:T(8,128)(2,1)S(1)}, u32[]{:S(2)}, u32[]{:S(2)}) collective-permute-start(bf16[640,128]{1,0:T(8,128)(2,1)S(1)} %get-tuple-element.14), channel_id=1, source_target_pairs={{0,248},{4,252},{8,0},{12,4},{16,8},{20,12},{24,16},{28,20},{32,24... | collective-permute-start | bytes 491528 | tf_op jit(solution)/shard_map/ppermute | solution.py:326
  111.1 4.6 %collective-permute-start.18 = (bf16[640,128]{1,0:T(8,128)(2,1)S(1)}, bf16[640,128]{1,0:T(8,128)(2,1)S(1)}, u32[]{:S(2)}, u32[]{:S(2)}) collective-permute-start(bf16[640,128]{1,0:T(8,128)(2,1)S(1)} %get-tuple-element.17), channel_id=1, source_target_pairs={{0,236},{4,240},{8,244},{12,248},{16,252},{20,0},{24,4},{28,8},{32... | collective-permute-start | bytes 491528 | tf_op jit(solution)/shard_map/ppermute | solution.py:326
  115.7 1.9 %collective-permute-start.19 = (bf16[640,128]{1,0:T(8,128)(2,1)S(1)}, bf16[640,128]{1,0:T(8,128)(2,1)S(1)}, u32[]{:S(2)}, u32[]{:S(2)}) collective-permute-start(bf16[640,128]{1,0:T(8,128)(2,1)S(1)} %get-tuple-element.18), channel_id=1, source_target_pairs={{0,232},{4,236},{8,240},{12,244},{16,248},{20,252},{24,0},{28,4},{... | collective-permute-start | bytes 491528 | tf_op jit(solution)/shard_map/ppermute | solution.py:326
  117.6 21.0 %collective-permute-start.33 = (f32[96,128]{1,0:T(8,128)S(1)}, f32[96,128]{1,0:T(8,128)S(1)}, u32[]{:S(2)}, u32[]{:S(2)}) collective-permute-start(f32[96,128]{1,0:T(8,128)S(1)} %add.86), channel_id=1, source_target_pairs={{0,1},{1,0},{2,3},{3,2},{4,5},{5,4},{6,7},{7,6},{8,9},{9,8},{10,11... | collective-permute-start | bytes 147464 | tf_op jit(solution)/shard_map/ppermute | solution.py:326
  138.6 2.8 %collective-permute-start.32 = (f32[96,128]{1,0:T(8,128)S(1)}, f32[96,128]{1,0:T(8,128)S(1)}, u32[]{:S(2)}, u32[]{:S(2)}) collective-permute-start(f32[96,128]{1,0:T(8,128)S(1)} %add.86), channel_id=1, source_target_pairs={{0,2},{1,3},{2,0},{3,1},{4,6},{5,7},{6,4},{7,5},{8,10},{9,11},{10,... | collective-permute-start | bytes 147464 | tf_op jit(solution)/shard_map/ppermute | solution.py:326
  141.4 0.5 collective-permute-start.31
  141.9 0.9 add_bitcast_fusion
  142.7 0.4 collective-permute-done.32
  143.1 3.5 %collective-permute-done.31 = f32[96,128]{1,0:T(8,128)S(1)} collective-permute-done((f32[96,128]{1,0:T(8,128)S(1)}, f32[96,128]{1,0:T(8,128)S(1)}, u32[]{:S(2)}, u32[]{:S(2)}) %collective-permute-start.31) | collective-permute-done | bytes 49184 | tf_op jit(solution)/shard_map/ppermute | solution.py:326
  146.7 0.3 reshape.92
  147.0 0.2 slice_multiply_fusion
  147.4 1.0 copy.25
  (77 shorter events, 1.0 us)
Async XLA Ops:
  0.6 29.4 %copy-start = (bf16[32,40,3,3,3]{1,0,4,3,2:T(8,128)(2,1)S(1)}, bf16[32,40,3,3,3]{1,0,4,3,2:T(8,128)(2,1)}, u32[]{:S(2)}) copy-start(bf16[32,40,3,3,3]{1,0,4,3,2:T(8,128)(2,1)} %param.15) | copy-start | bytes 207364
  0.6 19.9 %copy-start.1 = (bf16[12,32,8,128]{3,2,1,0:T(8,128)(2,1)S(1)}, bf16[12,32,8,128]{3,2,1,0:T(8,128)(2,1)}, u32[]{:S(2)}) copy-start(bf16[12,32,8,128]{3,2,1,0:T(8,128)(2,1)} %param.14) | copy-start | bytes 2359300
  0.7 22.9 %collective-permute-start.7 = (bf16[12,256,128]{2,1,0:T(8,128)(2,1)}, bf16[12,256,128]{2,1,0:T(8,128)(2,1)S(1)}, u32[]{:S(2)}, u32[]{:S(2)}) collective-permute-start(bf16[12,256,128]{2,1,0:T(8,128)(2,1)} %bitcast.44), channel_id=1, source_target_pairs={{0,2},{1,3},{2,0},{3,1},{4,6},{5,7},{6,4},{7,5},{8,10},{9,11},{10,... | collective-permute-start | bytes 2359304 | tf_op jit(solution)/shard_map/ppermute | solution.py:326
  5.5 5.5 %collective-permute-start.9 = (bf16[12,64,128]{2,1,0:T(8,128)(2,1)S(1)}, bf16[12,64,128]{2,1,0:T(8,128)(2,1)S(1)}, u32[]{:S(2)}, u32[]{:S(2)}) collective-permute-start(bf16[12,64,128]{2,1,0:T(8,128)(2,1)S(1)} %bitcast.63), channel_id=1, source_target_pairs={{0,4},{4,8},{8,12},{12,16},{16,20},{20,24},{24,28},{28,32},{32,36}... | collective-permute-start | bytes 589832 | tf_op jit(solution)/shard_map/ppermute | solution.py:326
  6.5 5.3 %collective-permute-start.10 = (bf16[12,64,128]{2,1,0:T(8,128)(2,1)S(1)}, bf16[12,64,128]{2,1,0:T(8,128)(2,1)S(1)}, u32[]{:S(2)}, u32[]{:S(2)}) collective-permute-start(bf16[12,64,128]{2,1,0:T(8,128)(2,1)S(1)} %bitcast.62), channel_id=1, source_target_pairs={{0,252},{4,0},{8,4},{12,8},{16,12},{20,16},{24,20},{28,24},{32,28}... | collective-permute-start | bytes 589832 | tf_op jit(solution)/shard_map/ppermute | solution.py:326
  11.0 1.1 copy-start.3
  11.8 27.6 %collective-permute-start.12 = (bf16[12,128,128]{2,1,0:T(8,128)(2,1)S(1)}, bf16[12,128,128]{2,1,0:T(8,128)(2,1)S(1)}, u32[]{:S(2)}, u32[]{:S(2)}) collective-permute-start(bf16[12,128,128]{2,1,0:T(8,128)(2,1)S(1)} %constant_dynamic-update-slice_fusion.refs_4_.refs_11_), channel_id=1, source_target_pairs={{0,2},{1,3},{2,0},{3,1},{4,6},{5,7},{6,4},{7,5},{8,10},{9,11},{10,... | collective-permute-start | bytes 1179656 | tf_op jit(solution)/shard_map/ppermute | solution.py:326
  12.1 11.5 %collective-permute-start.4 = (bf16[80,8,128]{2,1,0:T(8,128)(2,1)S(1)}, bf16[80,8,128]{2,1,0:T(8,128)(2,1)S(1)}, u32[]{:S(2)}, u32[]{:S(2)}) collective-permute-start(bf16[80,8,128]{2,1,0:T(8,128)(2,1)S(1)} %copy-done.3), channel_id=1, source_target_pairs={{0,8},{4,12},{8,16},{12,20},{16,24},{20,28},{24,32},{28,36},{32,40... | collective-permute-start | bytes 491528 | tf_op jit(solution)/shard_map/ppermute | solution.py:326
  15.6 10.2 %collective-permute-start.3 = (bf16[80,8,128]{2,1,0:T(8,128)(2,1)S(1)}, bf16[80,8,128]{2,1,0:T(8,128)(2,1)S(1)}, u32[]{:S(2)}, u32[]{:S(2)}) collective-permute-start(bf16[80,8,128]{2,1,0:T(8,128)(2,1)S(1)} %copy-done.3), channel_id=1, source_target_pairs={{0,12},{4,16},{8,20},{12,24},{16,28},{20,32},{24,36},{28,40},{32,4... | collective-permute-start | bytes 491528 | tf_op jit(solution)/shard_map/ppermute | solution.py:326
  20.6 35.6 %collective-permute-start.6 = (bf16[12,256,128]{2,1,0:T(8,128)(2,1)S(1)}, bf16[12,256,128]{2,1,0:T(8,128)(2,1)S(1)}, u32[]{:S(2)}, u32[]{:S(2)}) collective-permute-start(bf16[12,256,128]{2,1,0:T(8,128)(2,1)S(1)} %bitcast.45), channel_id=1, source_target_pairs={{0,1},{1,0},{2,3},{3,2},{4,5},{5,4},{6,7},{7,6},{8,9},{9,8},{10,11... | collective-permute-start | bytes 2359304 | tf_op jit(solution)/shard_map/ppermute | solution.py:326
  23.5 32.7 %collective-permute-start.8 = (bf16[12,256,128]{2,1,0:T(8,128)(2,1)S(1)}, bf16[12,256,128]{2,1,0:T(8,128)(2,1)}, u32[]{:S(2)}, u32[]{:S(2)}) collective-permute-start(bf16[12,256,128]{2,1,0:T(8,128)(2,1)S(1)} %collective-permute-done.7.refs_2_.refs_9_), channel_id=1, source_target_pairs={{0,1},{1,0},{2,3},{3,2},{4,5},{5,4},{6,7},{7,6},{8,9},{9,8},{10,11... | collective-permute-start | bytes 2359304 | tf_op jit(solution)/shard_map/ppermute | solution.py:326
  24.3 8.4 %collective-permute-start.2 = (bf16[80,8,128]{2,1,0:T(8,128)(2,1)S(1)}, bf16[80,8,128]{2,1,0:T(8,128)(2,1)}, u32[]{:S(2)}, u32[]{:S(2)}) collective-permute-start(bf16[80,8,128]{2,1,0:T(8,128)(2,1)S(1)} %copy-done.3), channel_id=1, source_target_pairs={{0,16},{4,20},{8,24},{12,28},{16,32},{20,36},{24,40},{28,44},{32,4... | collective-permute-start | bytes 491528 | tf_op jit(solution)/shard_map/ppermute | solution.py:326
  26.5 7.6 %collective-permute-start.1 = (bf16[80,8,128]{2,1,0:T(8,128)(2,1)S(1)}, bf16[80,8,128]{2,1,0:T(8,128)(2,1)}, u32[]{:S(2)}, u32[]{:S(2)}) collective-permute-start(bf16[80,8,128]{2,1,0:T(8,128)(2,1)S(1)} %copy-done.3), channel_id=1, source_target_pairs={{0,20},{4,24},{8,28},{12,32},{16,36},{20,40},{24,44},{28,48},{32,5... | collective-permute-start | bytes 491528 | tf_op jit(solution)/shard_map/ppermute | solution.py:326
  30.8 8.6 %copy-start.12 = (bf16[32,384,1,1,1]{1,0,4,3,2:T(8,128)(2,1)S(1)}, bf16[32,384,1,1,1]{1,0,4,3,2:T(8,128)(2,1)}, u32[]{:S(2)}) copy-start(bf16[32,384,1,1,1]{1,0,4,3,2:T(8,128)(2,1)} %constant.41) | copy-start | bytes 73732
  32.7 12.7 %collective-permute-start = (bf16[80,8,128]{2,1,0:T(8,128)(2,1)S(1)}, bf16[80,8,128]{2,1,0:T(8,128)(2,1)S(1)}, u32[]{:S(2)}, u32[]{:S(2)}) collective-permute-start(bf16[80,8,128]{2,1,0:T(8,128)(2,1)S(1)} %copy-done.3), channel_id=1, source_target_pairs={{0,24},{4,28},{8,32},{12,36},{16,40},{20,44},{24,48},{28,52},{32,5... | collective-permute-start | bytes 491528 | tf_op jit(solution)/shard_map/ppermute | solution.py:326
  34.1 22.1 %collective-permute-start.11 = (bf16[12,128,128]{2,1,0:T(8,128)(2,1)S(1)}, bf16[12,128,128]{2,1,0:T(8,128)(2,1)S(1)}, u32[]{:S(2)}, u32[]{:S(2)}) collective-permute-start(bf16[12,128,128]{2,1,0:T(8,128)(2,1)S(1)} %constant_dynamic-update-slice_fusion.refs_4_.refs_11_), channel_id=1, source_target_pairs={{0,1},{1,0},{2,3},{3,2},{4,5},{5,4},{6,7},{7,6},{8,9},{9,8},{10,11... | collective-permute-start | bytes 1179656 | tf_op jit(solution)/shard_map/ppermute | solution.py:326
  39.5 16.7 %collective-permute-start.13 = (bf16[12,128,128]{2,1,0:T(8,128)(2,1)S(1)}, bf16[12,128,128]{2,1,0:T(8,128)(2,1)S(1)}, u32[]{:S(2)}, u32[]{:S(2)}) collective-permute-start(bf16[12,128,128]{2,1,0:T(8,128)(2,1)S(1)} %collective-permute-done.12.refs_6_.refs_13_), channel_id=1, source_target_pairs={{0,1},{1,0},{2,3},{3,2},{4,5},{5,4},{6,7},{7,6},{8,9},{9,8},{10,11... | collective-permute-start | bytes 1179656 | tf_op jit(solution)/shard_map/ppermute | solution.py:326
  45.4 10.8 %collective-permute-start.5 = (bf16[80,8,128]{2,1,0:T(8,128)(2,1)S(1)}, bf16[80,8,128]{2,1,0:T(8,128)(2,1)S(1)}, u32[]{:S(2)}, u32[]{:S(2)}) collective-permute-start(bf16[80,8,128]{2,1,0:T(8,128)(2,1)S(1)} %copy-done.3), channel_id=1, source_target_pairs={{0,4},{4,8},{8,12},{12,16},{16,20},{20,24},{24,28},{28,32},{32,36}... | collective-permute-start | bytes 491528 | tf_op jit(solution)/shard_map/ppermute | solution.py:326
  46.7 9.5 %copy-start.10 = (f32[384,32]{1,0:T(8,128)S(1)}, f32[384,32]{1,0:T(8,128)}, u32[]{:S(2)}) copy-start(f32[384,32]{1,0:T(8,128)} %constant.35.clone.refs_16_) | copy-start | bytes 147460
  46.7 9.5 %copy-start.7 = (bf16[80,8,128]{2,1,0:T(8,128)(2,1)S(1)}, bf16[80,8,128]{2,1,0:T(8,128)(2,1)}, u32[]{:S(2)}) copy-start(bf16[80,8,128]{2,1,0:T(8,128)(2,1)} %copy-done.6) | copy-start | bytes 491524
  46.8 9.5 %copy-start.2 = (bf16[80,8,128]{2,1,0:T(8,128)(2,1)S(1)}, bf16[80,8,128]{2,1,0:T(8,128)(2,1)}, u32[]{:S(2)}) copy-start(bf16[80,8,128]{2,1,0:T(8,128)(2,1)} %param.12) | copy-start | bytes 491524
  46.8 9.5 %copy-start.5 = (bf16[80,8,128]{2,1,0:T(8,128)(2,1)S(1)}, bf16[80,8,128]{2,1,0:T(8,128)(2,1)}, u32[]{:S(2)}) copy-start(bf16[80,8,128]{2,1,0:T(8,128)(2,1)} %copy-done.4) | copy-start | bytes 491524
  46.9 9.4 %copy-start.11 = (f32[3,8,384]{2,1,0:T(8,128)S(1)}, f32[3,8,384]{2,1,0:T(8,128)}, u32[]{:S(2)}) copy-start(f32[3,8,384]{2,1,0:T(8,128)} %constant.34.clone.refs_15_) | copy-start | bytes 110596
  56.3 14.6 %copy-start.13 = (pred[8,384]{1,0:T(8,128)(4,1)S(1)}, pred[8,384]{1,0:T(8,128)(4,1)}, u32[]{:S(2)}) copy-start(pred[8,384]{1,0:T(8,128)(4,1)} %constant.33.clone) | copy-start | bytes 9220
  56.3 14.6 %copy-start.14 = (pred[8,384]{1,0:T(8,128)(4,1)S(1)}, pred[8,384]{1,0:T(8,128)(4,1)}, u32[]{:S(2)}) copy-start(pred[8,384]{1,0:T(8,128)(4,1)} %constant.32.clone) | copy-start | bytes 9220
  56.3 14.6 %copy-start.15 = (pred[8,384]{1,0:T(8,128)(4,1)S(1)}, pred[8,384]{1,0:T(8,128)(4,1)}, u32[]{:S(2)}) copy-start(pred[8,384]{1,0:T(8,128)(4,1)} %constant.31.clone) | copy-start | bytes 9220
  67.8 3.4 %collective-permute-start.22 = (f32[96,128]{1,0:T(8,128)S(1)}, f32[96,128]{1,0:T(8,128)S(1)}, u32[]{:S(2)}, u32[]{:S(2)}) collective-permute-start(f32[96,128]{1,0:T(8,128)S(1)} %cost_and_filter_grad.1), channel_id=1, source_target_pairs={{0,12},{4,0},{8,4},{12,8},{16,28},{20,16},{24,20},{28,24},{32,44},... | collective-permute-start | bytes 147464 | tf_op jit(solution)/shard_map/ppermute | solution.py:326
  69.0 4.4 %collective-permute-start.21 = (f32[96,128]{1,0:T(8,128)S(1)}, f32[96,128]{1,0:T(8,128)S(1)}, u32[]{:S(2)}, u32[]{:S(2)}) collective-permute-start(f32[96,128]{1,0:T(8,128)S(1)} %cost_and_filter_grad.1), channel_id=1, source_target_pairs={{0,8},{4,12},{8,0},{12,4},{16,24},{20,28},{24,16},{28,20},{32,40},... | collective-permute-start | bytes 147464 | tf_op jit(solution)/shard_map/ppermute | solution.py:326
  69.0 4.4 %collective-permute-start.20 = (f32[96,128]{1,0:T(8,128)S(1)}, f32[96,128]{1,0:T(8,128)S(1)}, u32[]{:S(2)}, u32[]{:S(2)}) collective-permute-start(f32[96,128]{1,0:T(8,128)S(1)} %cost_and_filter_grad.1), channel_id=1, source_target_pairs={{0,4},{4,8},{8,12},{12,0},{16,20},{20,24},{24,28},{28,16},{32,36},... | collective-permute-start | bytes 147464 | tf_op jit(solution)/shard_map/ppermute | solution.py:326
  73.5 23.5 %collective-permute-start.29 = (f32[96,128]{1,0:T(8,128)S(1)}, f32[96,128]{1,0:T(8,128)S(1)}, u32[]{:S(2)}, u32[]{:S(2)}) collective-permute-start(f32[96,128]{1,0:T(8,128)S(1)} %add_add_fusion.1), channel_id=1, source_target_pairs={{0,112},{4,116},{8,120},{12,124},{16,0},{20,4},{24,8},{28,12},{32,... | collective-permute-start | bytes 147464 | tf_op jit(solution)/shard_map/ppermute | solution.py:326
  74.6 23.7 %collective-permute-start.28 = (f32[96,128]{1,0:T(8,128)S(1)}, f32[96,128]{1,0:T(8,128)S(1)}, u32[]{:S(2)}, u32[]{:S(2)}) collective-permute-start(f32[96,128]{1,0:T(8,128)S(1)} %add_add_fusion.1), channel_id=1, source_target_pairs={{0,96},{4,100},{8,104},{12,108},{16,112},{20,116},{24,120},{28,124... | collective-permute-start | bytes 147464 | tf_op jit(solution)/shard_map/ppermute | solution.py:326
  80.2 20.4 %copy-start.8 = (s32[8,128]{1,0:T(8,128)S(1)}, s32[8,128]{1,0:T(8,128)}, u32[]{:S(2)}) copy-start(s32[8,128]{1,0:T(8,128)} %refs_8_.1) | copy-start | bytes 12292
  80.2 20.4 %copy-start.9 = (s32[8,128]{1,0:T(8,128)S(1)}, s32[8,128]{1,0:T(8,128)}, u32[]{:S(2)}) copy-start(s32[8,128]{1,0:T(8,128)} %refs_9_.1) | copy-start | bytes 12292
  91.3 14.6 %collective-permute-start.27 = (f32[96,128]{1,0:T(8,128)S(1)}, f32[96,128]{1,0:T(8,128)S(1)}, u32[]{:S(2)}, u32[]{:S(2)}) collective-permute-start(f32[96,128]{1,0:T(8,128)S(1)} %add_add_fusion.1), channel_id=1, source_target_pairs={{0,80},{4,84},{8,88},{12,92},{16,96},{20,100},{24,104},{28,108},{3... | collective-permute-start | bytes 147464 | tf_op jit(solution)/shard_map/ppermute | solution.py:326
  91.4 15.8 %collective-permute-start.26 = (f32[96,128]{1,0:T(8,128)S(1)}, f32[96,128]{1,0:T(8,128)S(1)}, u32[]{:S(2)}, u32[]{:S(2)}) collective-permute-start(f32[96,128]{1,0:T(8,128)S(1)} %add_add_fusion.1), channel_id=1, source_target_pairs={{0,64},{4,68},{8,72},{12,76},{16,80},{20,84},{24,88},{28,92},{32,9... | collective-permute-start | bytes 147464 | tf_op jit(solution)/shard_map/ppermute | solution.py:326
  97.0 10.3 %collective-permute-start.25 = (f32[96,128]{1,0:T(8,128)S(1)}, f32[96,128]{1,0:T(8,128)S(1)}, u32[]{:S(2)}, u32[]{:S(2)}) collective-permute-start(f32[96,128]{1,0:T(8,128)S(1)} %add_add_fusion.1), channel_id=1, source_target_pairs={{0,48},{4,52},{8,56},{12,60},{16,64},{20,68},{24,72},{28,76},{32,8... | collective-permute-start | bytes 147464 | tf_op jit(solution)/shard_map/ppermute | solution.py:326
  97.0 10.3 %collective-permute-start.24 = (f32[96,128]{1,0:T(8,128)S(1)}, f32[96,128]{1,0:T(8,128)S(1)}, u32[]{:S(2)}, u32[]{:S(2)}) collective-permute-start(f32[96,128]{1,0:T(8,128)S(1)} %add_add_fusion.1), channel_id=1, source_target_pairs={{0,32},{4,36},{8,40},{12,44},{16,48},{20,52},{24,56},{28,60},{32,6... | collective-permute-start | bytes 147464 | tf_op jit(solution)/shard_map/ppermute | solution.py:326
  98.2 9.0 %collective-permute-start.23 = (f32[96,128]{1,0:T(8,128)S(1)}, f32[96,128]{1,0:T(8,128)S(1)}, u32[]{:S(2)}, u32[]{:S(2)}) collective-permute-start(f32[96,128]{1,0:T(8,128)S(1)} %add_add_fusion.1), channel_id=1, source_target_pairs={{0,16},{4,20},{8,24},{12,28},{16,32},{20,36},{24,40},{28,44},{32,4... | collective-permute-start | bytes 147464 | tf_op jit(solution)/shard_map/ppermute | solution.py:326
  106.0 9.7 %collective-permute-start.14 = (bf16[640,128]{1,0:T(8,128)(2,1)S(1)}, bf16[640,128]{1,0:T(8,128)(2,1)S(1)}, u32[]{:S(2)}, u32[]{:S(2)}) collective-permute-start(bf16[640,128]{1,0:T(8,128)(2,1)S(1)} %get-tuple-element.13), channel_id=1, source_target_pairs={{0,252},{4,0},{8,4},{12,8},{16,12},{20,16},{24,20},{28,24},{32,28}... | collective-permute-start | bytes 491528 | tf_op jit(solution)/shard_map/ppermute | solution.py:326
  107.3 3.8 %collective-permute-start.30 = (f32[96,128]{1,0:T(8,128)S(1)}, f32[96,128]{1,0:T(8,128)S(1)}, u32[]{:S(2)}, u32[]{:S(2)}) collective-permute-start(f32[96,128]{1,0:T(8,128)S(1)} %add_add_fusion), channel_id=1, source_target_pairs={{0,128},{4,132},{8,136},{12,140},{16,144},{20,148},{24,152},{28,15... | collective-permute-start | bytes 147464 | tf_op jit(solution)/shard_map/ppermute | solution.py:326
  109.2 8.5 %collective-permute-start.15 = (bf16[640,128]{1,0:T(8,128)(2,1)S(1)}, bf16[640,128]{1,0:T(8,128)(2,1)S(1)}, u32[]{:S(2)}, u32[]{:S(2)}) collective-permute-start(bf16[640,128]{1,0:T(8,128)(2,1)S(1)} %get-tuple-element.14), channel_id=1, source_target_pairs={{0,248},{4,252},{8,0},{12,4},{16,8},{20,12},{24,16},{28,20},{32,24... | collective-permute-start | bytes 491528 | tf_op jit(solution)/shard_map/ppermute | solution.py:326
  110.9 27.7 %collective-permute-start.16 = (bf16[640,128]{1,0:T(8,128)(2,1)S(1)}, bf16[640,128]{1,0:T(8,128)(2,1)S(1)}, u32[]{:S(2)}, u32[]{:S(2)}) collective-permute-start(bf16[640,128]{1,0:T(8,128)(2,1)S(1)} %get-tuple-element.15), channel_id=1, source_target_pairs={{0,244},{4,248},{8,252},{12,0},{16,4},{20,8},{24,12},{28,16},{32,2... | collective-permute-start | bytes 491528 | tf_op jit(solution)/shard_map/ppermute | solution.py:326
  110.9 30.5 %collective-permute-start.17 = (bf16[640,128]{1,0:T(8,128)(2,1)S(1)}, bf16[640,128]{1,0:T(8,128)(2,1)S(1)}, u32[]{:S(2)}, u32[]{:S(2)}) collective-permute-start(bf16[640,128]{1,0:T(8,128)(2,1)S(1)} %get-tuple-element.16), channel_id=1, source_target_pairs={{0,240},{4,244},{8,248},{12,252},{16,0},{20,4},{24,8},{28,12},{32,... | collective-permute-start | bytes 491528 | tf_op jit(solution)/shard_map/ppermute | solution.py:326
  111.1 30.8 %collective-permute-start.18 = (bf16[640,128]{1,0:T(8,128)(2,1)S(1)}, bf16[640,128]{1,0:T(8,128)(2,1)S(1)}, u32[]{:S(2)}, u32[]{:S(2)}) collective-permute-start(bf16[640,128]{1,0:T(8,128)(2,1)S(1)} %get-tuple-element.17), channel_id=1, source_target_pairs={{0,236},{4,240},{8,244},{12,248},{16,252},{20,0},{24,4},{28,8},{32... | collective-permute-start | bytes 491528 | tf_op jit(solution)/shard_map/ppermute | solution.py:326
  115.7 26.2 %collective-permute-start.19 = (bf16[640,128]{1,0:T(8,128)(2,1)S(1)}, bf16[640,128]{1,0:T(8,128)(2,1)S(1)}, u32[]{:S(2)}, u32[]{:S(2)}) collective-permute-start(bf16[640,128]{1,0:T(8,128)(2,1)S(1)} %get-tuple-element.18), channel_id=1, source_target_pairs={{0,232},{4,236},{8,240},{12,244},{16,248},{20,252},{24,0},{28,4},{... | collective-permute-start | bytes 491528 | tf_op jit(solution)/shard_map/ppermute | solution.py:326
  117.6 25.1 %collective-permute-start.33 = (f32[96,128]{1,0:T(8,128)S(1)}, f32[96,128]{1,0:T(8,128)S(1)}, u32[]{:S(2)}, u32[]{:S(2)}) collective-permute-start(f32[96,128]{1,0:T(8,128)S(1)} %add.86), channel_id=1, source_target_pairs={{0,1},{1,0},{2,3},{3,2},{4,5},{5,4},{6,7},{7,6},{8,9},{9,8},{10,11... | collective-permute-start | bytes 147464 | tf_op jit(solution)/shard_map/ppermute | solution.py:326
  138.6 4.5 %collective-permute-start.32 = (f32[96,128]{1,0:T(8,128)S(1)}, f32[96,128]{1,0:T(8,128)S(1)}, u32[]{:S(2)}, u32[]{:S(2)}) collective-permute-start(f32[96,128]{1,0:T(8,128)S(1)} %add.86), channel_id=1, source_target_pairs={{0,2},{1,3},{2,0},{3,1},{4,6},{5,7},{6,4},{7,5},{8,10},{9,11},{10,... | collective-permute-start | bytes 147464 | tf_op jit(solution)/shard_map/ppermute | solution.py:326
  141.4 5.2 %collective-permute-start.31 = (f32[96,128]{1,0:T(8,128)S(1)}, f32[96,128]{1,0:T(8,128)S(1)}, u32[]{:S(2)}, u32[]{:S(2)}) collective-permute-start(f32[96,128]{1,0:T(8,128)S(1)} %add.86), channel_id=1, source_target_pairs={{0,3},{1,2},{2,1},{3,0},{4,7},{5,6},{6,5},{7,4},{8,11},{9,10},{10,... | collective-permute-start | bytes 147464 | tf_op jit(solution)/shard_map/ppermute | solution.py:326
  (2 other events, 1.3 us)

commit v2 on v1

--- a/solution.py
+++ b/solution.py
@@ -28,33 +28,33 @@
     return column, channel
 
 
-def plane_copies(rank, own, halo, planes, first, sems):
-    copies = []
-    for k in range(4):
-        start = (rank ^ k) * 12 + first
-        copies.append(
-            pltpu.make_async_copy(
-                own[k], planes.at[pl.ds(start, 12), pl.ds(0, 256)], sems.at[k]
-            )
-        )
-        copies.append(
-            pltpu.make_async_copy(
-                halo[k], planes.at[pl.ds(start, 12), pl.ds(256, 128)], sems.at[4 + k]
-            )
-        )
-    return copies
-
-
-def conv_kernel(rank_ref, kernel_ref, *refs):
-    own, halo = refs[0:4], refs[4:8]
-    out_ref, planes, sems = refs[8:]
-    copies = plane_copies(rank_ref[0], own, halo, planes, 2, sems)
-    for copy in copies:
-        copy.start()
-    planes[0:2] = jnp.zeros((2, ROWS, 128), BF16)
-    planes[50:52] = jnp.zeros((2, ROWS, 128), BF16)
-    for copy in copies:
-        copy.wait()
+SLABS = 8
+
+
+class PlaneLoad:
+    def __init__(self, rank, slabs, planes, first, sems):
+        self.copies = []
+        for k in range(4):
+            place = pl.ds((rank ^ k) * 12 + first, 12)
+            for part, (row, rows) in enumerate(((0, 256), (256, 128))):
+                self.copies.append(
+                    pltpu.make_async_copy(
+                        slabs[4 * part + k],
+                        planes.at[place, pl.ds(row, rows)],
+                        sems.at[4 * part + k],
+                    )
+                )
+
+    def start(self):
+        for copy in self.copies:
+            copy.start()
+
+    def wait(self):
+        for copy in self.copies:
+            copy.wait()
+
+
+def transposed_filter(kernel_ref, planes, emit, unroll):
     lane = lax.broadcasted_iota(jnp.int32, (80, 128), 1)
 
     def pair(index, carry):
@@ -70,14 +70,36 @@
             part = product[:, half * 128 : half * 128 + 128]
             ahead = jnp.where(lane < 126, pltpu.roll(part[0:80], 126, 1), 0.0)
             behind = jnp.where(lane >= 2, pltpu.roll(part[160:240], 2, 1), 0.0)
-            out_ref[d + half] = (part[80:160] + ahead + behind).astype(BF16)
+            emit(d + half, part[80:160] + ahead + behind)
         return carry
 
-    lax.fori_loop(0, 24, pair, 0)
+    lax.fori_loop(0, 24, pair, 0, unroll=unroll)
+
+
+def conv_kernel(rank_ref, kernel_ref, *refs):
+    slabs, (out_ref, planes, sems) = refs[0:SLABS], refs[SLABS:]
+    load = PlaneLoad(rank_ref[0], slabs, planes, 2, sems)
+    load.start()
+    planes[0:2] = jnp.zeros((2, ROWS, 128), BF16)
+    planes[50:52] = jnp.zeros((2, ROWS, 128), BF16)
+    load.wait()
+
+    def emit(d, value):
+        out_ref[d] = value.astype(BF16)
+
+    transposed_filter(kernel_ref, planes, emit, 4)
 
 
 def rolled(value, steps, axis):
     return value if steps == 0 else pltpu.roll(value, steps, axis)
+
+
+PANELS = 6
+
+
+def panel_places(refs):
+    one, two, three, four, pair, own = refs
+    return [(pair, 640), (pair, 0), (four, 0), (three, 0), (two, 0), (one, 0), (own, 0)]
 
 
 def widen(left_ref, panels, left_rolls, wide):
@@ -90,19 +112,18 @@
             for r in range(8):
                 left_rolls[r, place, :] = rolled(part, (8 - r) % 8, 0)
         for b in range(BLOCKS):
-            wide[b, rows, :] = panels[b][rows, :].astype(F32)
+            panel, first = panels[b]
+            there = pl.ds(pl.multiple_of(first + index * 16, 16), 16)
+            value = panel[there, :].astype(F32)
+            wide[b, rows, :] = value
         return carry
 
     lax.fori_loop(0, 40, two, 0)
 
 
-def cost_kernel(rank_ref, left_ref, *refs):
-    panels = refs[0:7]
-    own, halo = refs[7:11], refs[11:15]
-    mask_ref, sum_ref, out_ref, left_rolls, wide, planes, volume, total, sems = refs[15:]
-    copies = plane_copies(rank_ref[0], own, halo, planes, 0, sems)
-    for copy in copies:
-        copy.start()
+def cost_kernel(left_ref, *refs):
+    panels = panel_places(refs[0:PANELS])
+    volume, left_rolls, wide = refs[PANELS:]
     widen(left_ref, panels, left_rolls, wide)
     volume[0:2] = jnp.zeros((2, 240, 128), BF16)
     volume[50:52] = jnp.zeros((2, 240, 128), BF16)
@@ -139,21 +160,25 @@
         return carry
 
     lax.fori_loop(0, 5, groups, 0)
-    for copy in copies:
-        copy.wait()
+
+def filter_kernel(rank_ref, volume, mask_ref, sum_ref, *refs):
+    slabs, (out_ref, planes, total, sems) = refs[0:SLABS], refs[SLABS:]
+    load = PlaneLoad(rank_ref[0], slabs, planes, 0, sems)
+    load.start()
     total[...] = jnp.zeros_like(total)
+    load.wait()
 
     def chunk(index, carry):
-        d = index * 8
-        cot = jnp.concatenate([planes[d + j] for j in range(8)], axis=1)
+        d = index * 16
+        cot = jnp.concatenate([planes[d + j] for j in range(16)], axis=1)
         for a in range(3):
-            cost = jnp.concatenate([volume[d + j + 2 * a] for j in range(8)], axis=1)
+            cost = jnp.concatenate([volume[d + j + 2 * a] for j in range(16)], axis=1)
             total[a] += lax.dot_general(
                 cost, cot, (((1,), (1,)), ((), ())), preferred_element_type=F32
             )
         return carry
 
-    lax.fori_loop(0, 6, chunk, 0)
+    lax.fori_loop(0, DISP // 16, chunk, 0)
     out_ref[...] = jnp.zeros_like(out_ref)
     for a in range(3):
         terms = total[a].reshape(30, 8, ROWS)
@@ -165,10 +190,10 @@
 
 
 def grad_kernel(left_ref, *refs):
-    panels = refs[0:7]
-    grad_ref, shift_ref, valid_ref = refs[7:10]
-    left_out, right_out = refs[10], refs[11:18]
-    left_rolls, wide, chosen, counts, weights = refs[18:]
+    panels = panel_places(refs[0:PANELS])
+    grad_ref, shift_ref, valid_ref = refs[PANELS : PANELS + 3]
+    left_out, right_out = refs[PANELS + 3], refs[PANELS + 4 : PANELS + 11]
+    left_rolls, wide, chosen, counts, weights = refs[PANELS + 11 :]
     widen(left_ref, panels, left_rolls, wide)
     row = lax.broadcasted_iota(jnp.int32, (8, 128), 0)
     valid = valid_ref[...].astype(F32)
@@ -242,42 +267,63 @@
 ANY = pl.BlockSpec(memory_space=pl.ANY)
 
 
-def run_conv(rank, kernel, own, halo):
+def cost_of(flops, size):
+    return pl.CostEstimate(flops=flops, bytes_accessed=size, transcendentals=0)
+
+
+def run_conv(rank, kernel, slabs):
     return pl.pallas_call(
         conv_kernel,
         out_shape=jax.ShapeDtypeStruct((DISP, 80, 128), BF16),
-        in_specs=[SMEM, VMEM] + [ANY] * 8,
+        in_specs=[SMEM, VMEM] + [ANY] * SLABS,
         out_specs=VMEM,
         scratch_shapes=[pltpu.VMEM((52, ROWS, 128), BF16), pltpu.SemaphoreType.DMA((8,))],
-        compiler_params=pltpu.CompilerParams(vmem_limit_bytes=20 * MIB),
-        cost_estimate=pl.CostEstimate(flops=15_000_000_000, bytes_accessed=8_000_000, transcendentals=0),
+        compiler_params=pltpu.CompilerParams(vmem_limit_bytes=16 * MIB),
+        cost_estimate=cost_of(7_000_000_000, 6_000_000),
         name="filter_transpose",
-    )(rank, kernel, *own, *halo)
-
-
-def run_cost(rank, left, panels, own, halo):
+    )(rank, kernel, *slabs)
+
+
+def run_cost(left, panels):
+    return pl.pallas_call(
+        cost_kernel,
+        out_shape=jax.ShapeDtypeStruct((52, 240, 128), BF16),
+        in_specs=[VMEM] * (1 + PANELS),
+        out_specs=VMEM,
+        scratch_shapes=[
+            pltpu.VMEM((8, 640, 128), F32),
+            pltpu.VMEM((BLOCKS, 640, 128), F32),
+        ],
+        compiler_params=pltpu.CompilerParams(vmem_limit_bytes=16 * MIB),
+        cost_estimate=cost_of(5_000_000_000, 4_000_000),
+        name="cost_volume",
+    )(left, *panels)
+
+
+def picking():
     column, channel = filter_column()
     w = np.arange(8)[None, :, None]
     b = np.arange(3)[:, None, None]
     mask = (w == column[None, None, :] + 2 * b - 2).astype(np.float32)
     summing = (channel[:, None] == np.arange(OUTC)[None]).astype(np.float32)
+    return jnp.asarray(mask), jnp.asarray(summing)
+
+
+def run_filter(rank, volume, slabs):
     return pl.pallas_call(
-        cost_kernel,
+        filter_kernel,
         out_shape=jax.ShapeDtypeStruct((96, 128), F32),
-        in_specs=[SMEM, VMEM] + [VMEM] * 7 + [ANY] * 8 + [VMEM] * 2,
+        in_specs=[SMEM] + [VMEM] * 3 + [ANY] * SLABS,
         out_specs=VMEM,
         scratch_shapes=[
-            pltpu.VMEM((8, 640, 128), F32),
-            pltpu.VMEM((BLOCKS, 640, 128), F32),
             pltpu.VMEM((DISP, ROWS, 128), BF16),
-            pltpu.VMEM((52, 240, 128), BF16),
             pltpu.VMEM((3, 240, ROWS), F32),
             pltpu.SemaphoreType.DMA((8,)),
         ],
-        compiler_params=pltpu.CompilerParams(vmem_limit_bytes=32 * MIB),
-        cost_estimate=pl.CostEstimate(flops=15_000_000_000, bytes_accessed=8_000_000, transcendentals=0),
-        name="cost_and_filter_grad",
-    )(rank, left, *panels, *own, *halo, jnp.asarray(mask), jnp.asarray(summing))
+        compiler_params=pltpu.CompilerParams(vmem_limit_bytes=20 * MIB),
+        cost_estimate=cost_of(8_000_000_000, 4_000_000),
+        name="filter_grad",
+    )(rank, volume, *picking(), *slabs)
 
 
 def run_grad(left, panels, grad_cost, shift, valid):
@@ -286,7 +332,7 @@
         out_shape=[jax.ShapeDtypeStruct((640, 128), F32)]
         + [jax.ShapeDtypeStruct((640, 128), BF16)] * 6
         + [jax.ShapeDtypeStruct((640, 128), F32)],
-        in_specs=[VMEM] * 11,
+        in_specs=[VMEM] * (4 + PANELS),
         out_specs=[VMEM] * 8,
         scratch_shapes=[
             pltpu.VMEM((8, 640, 128), F32),
@@ -295,8 +341,8 @@
             pltpu.VMEM((BLOCKS, 8, 128), F32),
             pltpu.VMEM((2, BLOCKS, 8, 8, 128), F32),
         ],
-        compiler_params=pltpu.CompilerParams(vmem_limit_bytes=32 * MIB),
-        cost_estimate=pl.CostEstimate(flops=8_000_000_000, bytes_accessed=4_000_000, transcendentals=0),
+        compiler_params=pltpu.CompilerParams(vmem_limit_bytes=24 * MIB),
+        cost_estimate=cost_of(5_000_000_000, 4_000_000),
         name="feature_grads",
     )(left, *panels, grad_cost, shift, valid)
 
@@ -336,34 +382,41 @@
 
 
 def summed_over_lon(value):
-    total = value
-    for k in range(1, 4):
-        total = total + moved(value, "lon", lambda i: i - i % 4 + (i + k) % 4)
-    value = total
-    for k in range(1, 8):
-        total = total + moved(value, "lon", lambda i: i - i % 32 + (i + 4 * k) % 32)
-    return total + moved(total, "lon", lambda i: i ^ 32)
+    for unit in (1, 4, 16):
+        value = value + sum(moved(value, "lon", lambda i: i ^ (unit * k)) for k in (1, 2, 3))
+    return value
+
+
+def together(value, other):
+    return lax.optimization_barrier((value, other))[0]
 
 
 def shards(left_feat, right_feat, conv_cot, conv_weight, disparity_shift, valid_mask):
     rank = lax.axis_index("grp")
     rank_array = rank.astype(jnp.int32).reshape(1)
-    panels = [along(right_feat, k).reshape(640, 128) for k in range(6, 0, -1)]
-    panels.append(right_feat.reshape(640, 128))
+    right = right_feat.reshape(640, 128)
     left = left_feat.reshape(640, 128)
-
     own = conv_cot.reshape(12, 256, 128)
+
     own_far = across(own, 2)
-    before = along(conv_cot[:, :, 6:].reshape(12, 64, 128), 1)
+    one = along(jnp.concatenate([right, conv_cot[:, :, 6:].reshape(768, 128)]), 1)
     after = along(conv_cot[:, :, :2].reshape(12, 64, 128), -1)
-    halo = jnp.concatenate([before, after], axis=1)
+    halo = jnp.concatenate([one[640:].reshape(12, 64, 128), after], axis=1)
     halo_far = across(halo, 2)
-    owns = [own, across(own, 1), own_far, across(own_far, 1)]
-    halos = [halo, across(halo, 1), halo_far, across(halo_far, 1)]
-
-    grad_cost = run_conv(rank_array, conv_matrix(conv_weight, rank), owns, halos)
-    filter_part = run_cost(rank_array, left, panels, owns, halos)
-    outs = run_grad(left, panels, grad_cost, disparity_shift, valid_mask)
+    later = together(right, after)
+    two, three, four = (along(later, k) for k in (2, 3, 4))
+    pair = along(jnp.concatenate([one[:640], two]), 4)
+    panels = [one, two, three, four, pair, right]
+    own_later = together(own, after)
+    slabs = [own, across(own_later, 1), own_far, across(own_far, 1)]
+    slabs += [halo, across(halo, 1), halo_far, across(halo_far, 1)]
+
+    grad_cost = run_conv(rank_array, conv_matrix(conv_weight, rank), slabs)
+    volume = run_cost(together(left, grad_cost), panels)
+    filter_part = run_filter(rank_array, volume, slabs)
+    outs = run_grad(
+        together(left, filter_part), panels, grad_cost, disparity_shift, valid_mask
+    )
     left_grad = outs[0].reshape(80, 8, 128)
     right_grad = outs[7]
     for k in range(1, 7):

time: 149 us -> 126 us (0.85)
  the two profiles are of different devices: /device:TPU:69 before, /device:TPU:4 now
where the time goes in v2:
time: 126 us
  waiting for transfers between devices  59.2 us (47%)
  starting transfers between devices  38.8 us (31%)
  Pallas kernels  20.2 us (16%)
  local copies, waits for them, and re-layouts  3.94 us (3%)
  other arithmetic  2.49 us (2%)
    ppermute x30, waiting for transfers between devices, moved(): return lax.ppermute(value, axis, pairs)  59.2 us
    ppermute x30, starting transfers between devices, moved(): return lax.ppermute(value, axis, pairs)  38.8 us
    pallas_call x1, Pallas kernels, run_filter(): pl.pallas_call(filter_kernel, out_shape=jax.ShapeDtypeStruct((96, 128), F...  7.57 us
    pallas_call x1, Pallas kernels, run_conv(): pl.pallas_call(conv_kernel, out_shape=jax.ShapeDtypeStruct((DISP, 80, 128...  5.92 us
    pallas_call x1, Pallas kernels, run_grad(): pl.pallas_call(grad_kernel, out_shape=[jax.ShapeDtypeStruct((640, 128), F...  4.26 us
  transfers between devices with their start and end apart: 30, of which 13 were waited for; matrix products, arithmetic and copies ran while one was open for 4% of the time, Pallas kernels for 8%

profile of v2, /device:TPU:4, one launch (start us, length us, event | category | flops | bytes accessed | tf_op | source)
XLA Modules:
  0.0 125.8 jit_solution(8044501093373046321)
XLA Ops:
  0.7 3.3 %collective-permute-start.2 = (bf16[12,256,128]{2,1,0:T(8,128)(2,1)}, bf16[12,256,128]{2,1,0:T(8,128)(2,1)S(1)}, u32[]{:S(2)}, u32[]{:S(2)}) collective-permute-start(bf16[12,256,128]{2,1,0:T(8,128)(2,1)} %bitcast.39), channel_id=1, source_target_pairs={{0,2},{1,3},{2,0},{3,1},{4,6},{5,7},{6,4},{7,5},{8,10},{9,11},{10,... | collective-permute-start | bytes 2359304 | tf_op jit(solution)/shard_map/ppermute | solution.py:372
  4.0 1.9 %fusion.2 = (bf16[12,32,2,128]{3,2,1,0:T(2,128)(2,1)S(1)}, bf16[12,32,2,128]{3,2,1,0:T(2,128)(2,1)S(1)}) fusion(bf16[12,32,8,128]{3,2,1,0:T(8,128)(2,1)} %param.14), kind=kLoop, calls=%fused_computation.27 | loop fusion | bytes 786432 | tf_op jit(solution)/shard_map/slice | solution.py:402
  5.9 1.0 pad_maximum_fusion.1
  6.9 1.3 %collective-permute-start.4 = (bf16[1408,128]{1,0:T(8,128)(2,1)S(1)}, bf16[1408,128]{1,0:T(8,128)(2,1)S(1)}, u32[]{:S(2)}, u32[]{:S(2)}) collective-permute-start(bf16[1408,128]{1,0:T(8,128)(2,1)S(1)} %pad_maximum_fusion.1), channel_id=1, source_target_pairs={{0,4},{4,8},{8,12},{12,16},{16,20},{20,24},{24,28},{28,32},{32,36}... | collective-permute-start | bytes 1081352 | tf_op jit(solution)/shard_map/ppermute | solution.py:372
  8.1 0.8 collective-permute-start
  9.0 0.1 constant_dynamic-slice_fusion
  9.1 0.2 copy.27
  9.4 5.0 %collective-permute-done = bf16[12,64,128]{2,1,0:T(8,128)(2,1)S(1)} collective-permute-done((bf16[12,64,128]{2,1,0:T(8,128)(2,1)S(1)}, bf16[12,64,128]{2,1,0:T(8,128)(2,1)S(1)}, u32[]{:S(2)}, u32[]{:S(2)}) %collective-permute-start) | collective-permute-done | bytes 196640 | tf_op jit(solution)/shard_map/ppermute | solution.py:372
  14.3 2.5 %collective-permute-done.4.refs_0_ = bf16[1408,128]{1,0:T(8,128)(2,1)S(1)} collective-permute-done((bf16[1408,128]{1,0:T(8,128)(2,1)S(1)}, bf16[1408,128]{1,0:T(8,128)(2,1)S(1)}, u32[]{:S(2)}, u32[]{:S(2)}) %collective-permute-start.4) | collective-permute-done | bytes 360480 | tf_op jit(solution)/shard_map/ppermute | solution.py:372
  16.9 0.4 collective-permute-start.6
  17.3 5.6 %collective-permute-done.2.refs_2_ = bf16[12,256,128]{2,1,0:T(8,128)(2,1)S(1)} collective-permute-done((bf16[12,256,128]{2,1,0:T(8,128)(2,1)}, bf16[12,256,128]{2,1,0:T(8,128)(2,1)S(1)}, u32[]{:S(2)}, u32[]{:S(2)}) %collective-permute-start.2) | collective-permute-done | bytes 786464 | tf_op jit(solution)/shard_map/ppermute | solution.py:372
  22.9 0.2 fusion
  23.4 1.3 %collective-permute-start.8 = (bf16[640,128]{1,0:T(8,128)(2,1)S(1)}, bf16[640,128]{1,0:T(8,128)(2,1)S(1)}, u32[]{:S(2)}, u32[]{:S(2)}) collective-permute-start(bf16[640,128]{1,0:T(8,128)(2,1)S(1)} %bitcast.44), channel_id=1, source_target_pairs={{0,8},{4,12},{8,16},{12,20},{16,24},{20,28},{24,32},{28,36},{32,40... | collective-permute-start | bytes 491528 | tf_op jit(solution)/shard_map/ppermute | solution.py:372
  24.6 0.2 collective-permute-start.5
  24.9 5.4 %collective-permute-done.6.refs_6_ = bf16[12,128,128]{2,1,0:T(8,128)(2,1)S(1)} collective-permute-done((bf16[12,128,128]{2,1,0:T(8,128)(2,1)S(1)}, bf16[12,128,128]{2,1,0:T(8,128)(2,1)S(1)}, u32[]{:S(2)}, u32[]{:S(2)}) %collective-permute-start.6) | collective-permute-done | bytes 393248 | tf_op jit(solution)/shard_map/ppermute | solution.py:372
  30.2 0.3 select_add_fusion
  30.6 7.8 %collective-permute-done.8.refs_1_ = bf16[640,128]{1,0:T(8,128)(2,1)S(1)} collective-permute-done((bf16[640,128]{1,0:T(8,128)(2,1)S(1)}, bf16[640,128]{1,0:T(8,128)(2,1)S(1)}, u32[]{:S(2)}, u32[]{:S(2)}) %collective-permute-start.8) | collective-permute-done | bytes 163872 | tf_op jit(solution)/shard_map/ppermute | solution.py:372
  38.5 0.3 collective-permute-start.11
  38.8 5.9 %filter_transpose.1.refs_6_ = bf16[48,80,128]{2,1,0:T(8,128)(2,1)S(1)} custom-call(s32[1]{0:T(128)} %bitcast.1.rank_ref, bf16[240,1152]{1,0:T(8,128)(2,1)S(1)} %bitcast.38, bf16[12,256,128]{2,1,0:T(8,128)(2,1)S(1)} %bitcast.41, bf16[12,256,128]{2,1,0:T(8,128)(2,1)S(1)} %collective-permute-done.1.refs_1_, ...), custom_call_target="tpu_custom_call" | custom-call | flops 7000000000 | bytes 6000000 | tf_op jit(solution)/shard_map/filter_transpose/pallas_call | solution.py:275
  44.8 2.4 %collective-permute-done.10.refs_3_ = bf16[640,128]{1,0:T(8,128)(2,1)S(1)} collective-permute-done((bf16[640,128]{1,0:T(8,128)(2,1)S(1)}, bf16[640,128]{1,0:T(8,128)(2,1)S(1)}, u32[]{:S(2)}, u32[]{:S(2)}) %collective-permute-start.10) | collective-permute-done | bytes 163872 | tf_op jit(solution)/shard_map/ppermute | solution.py:372
  47.2 5.6 %collective-permute-done.9.refs_2_ = bf16[640,128]{1,0:T(8,128)(2,1)S(1)} collective-permute-done((bf16[640,128]{1,0:T(8,128)(2,1)S(1)}, bf16[640,128]{1,0:T(8,128)(2,1)S(1)}, u32[]{:S(2)}, u32[]{:S(2)}) %collective-permute-start.9) | collective-permute-done | bytes 163872 | tf_op jit(solution)/shard_map/ppermute | solution.py:372
  52.8 5.2 %collective-permute-done.11.refs_4_ = bf16[1280,128]{1,0:T(8,128)(2,1)S(1)} collective-permute-done((bf16[1280,128]{1,0:T(8,128)(2,1)S(1)}, bf16[1280,128]{1,0:T(8,128)(2,1)S(1)}, u32[]{:S(2)}, u32[]{:S(2)}) %collective-permute-start.11) | collective-permute-done | bytes 327712 | tf_op jit(solution)/shard_map/ppermute | solution.py:372
  57.9 2.4 %cost_volume.1.volume = bf16[52,240,128]{2,1,0:T(8,128)(2,1)S(1)} custom-call(bf16[640,128]{1,0:T(8,128)(2,1)S(1)} %bitcast.49, bf16[1408,128]{1,0:T(8,128)(2,1)S(1)} %collective-permute-done.4.refs_0_, bf16[640,128]{1,0:T(8,128)(2,1)S(1)} %collective-permute-done.8.refs_1_, bf16[640,128]{1,0:T(8,128)(2,1)S(1)} %collective-permute-done.9.refs_2_, ...), custom_call_target="tpu_custom_call" | custom-call | flops 5000000000 | bytes 4000000 | tf_op jit(solution)/shard_map/cost_volume/pallas_call | solution.py:288
  60.4 7.6 %filter_grad.1 = f32[96,128]{1,0:T(8,128)S(1)} custom-call(s32[1]{0:T(128)} %bitcast.1.rank_ref, bf16[52,240,128]{2,1,0:T(8,128)(2,1)S(1)} %cost_volume.1.volume, f32[3,8,384]{2,1,0:T(8,128)S(1)} %copy-done.7, f32[384,32]{1,0:T(8,128)S(1)} %copy-done.6, bf16[12,256,128]{2,1,0:T(8,128)(2,1)S(1)} %bitcast.42, ...), custom_call_target="tpu_custom_call" | custom-call | flops 8000000000 | bytes 4000000 | tf_op jit(solution)/shard_map/filter_grad/pallas_call | solution.py:313
  68.0 0.7 collective-permute-start.18
  68.6 4.7 %collective-permute-start.19 = (f32[96,128]{1,0:T(8,128)S(1)}, f32[96,128]{1,0:T(8,128)S(1)}, u32[]{:S(2)}, u32[]{:S(2)}) collective-permute-start(f32[96,128]{1,0:T(8,128)S(1)} %filter_grad.1), channel_id=1, source_target_pairs={{0,8},{4,12},{8,0},{12,4},{16,24},{20,28},{24,16},{28,20},{32,40},... | collective-permute-start | bytes 147464 | tf_op jit(solution)/shard_map/ppermute | solution.py:372
  73.3 0.5 collective-permute-start.20
  73.7 2.0 %collective-permute-done.19 = f32[96,128]{1,0:T(8,128)S(1)} collective-permute-done((f32[96,128]{1,0:T(8,128)S(1)}, f32[96,128]{1,0:T(8,128)S(1)}, u32[]{:S(2)}, u32[]{:S(2)}) %collective-permute-start.19) | collective-permute-done | bytes 49184 | tf_op jit(solution)/shard_map/ppermute | solution.py:372
  75.8 1.6 %collective-permute-done.20 = f32[96,128]{1,0:T(8,128)S(1)} collective-permute-done((f32[96,128]{1,0:T(8,128)S(1)}, f32[96,128]{1,0:T(8,128)S(1)}, u32[]{:S(2)}, u32[]{:S(2)}) %collective-permute-start.20) | collective-permute-done | bytes 49184 | tf_op jit(solution)/shard_map/ppermute | solution.py:372
  77.4 0.1 collective-permute-start.21
  77.5 0.1 collective-permute-start.22
  77.6 4.3 %collective-permute-start.23 = (f32[96,128]{1,0:T(8,128)S(1)}, f32[96,128]{1,0:T(8,128)S(1)}, u32[]{:S(2)}, u32[]{:S(2)}) collective-permute-start(f32[96,128]{1,0:T(8,128)S(1)} %add_add_fusion.2), channel_id=1, source_target_pairs={{0,48},{4,52},{8,56},{12,60},{16,32},{20,36},{24,40},{28,44},{32,1... | collective-permute-start | bytes 147464 | tf_op jit(solution)/shard_map/ppermute | solution.py:372
  81.9 4.3 %feature_grads.1 = (f32[640,128]{1,0:T(8,128)}, bf16[640,128]{1,0:T(8,128)(2,1)S(1)}, bf16[640,128]{1,0:T(8,128)(2,1)S(1)}, bf16[640,128]{1,0:T(8,128)(2,1)S(1)}...) custom-call(bf16[640,128]{1,0:T(8,128)(2,1)S(1)} %bitcast.50, ...), custom_call_target="tpu_custom_call" | custom-call | flops 5000000000 | bytes 4000000 | tf_op jit(solution)/shard_map/feature_grads/pallas_call | solution.py:330
  86.1 2.0 %collective-permute-start.12 = (bf16[640,128]{1,0:T(8,128)(2,1)S(1)}, bf16[640,128]{1,0:T(8,128)(2,1)S(1)}, u32[]{:S(2)}, u32[]{:S(2)}) collective-permute-start(bf16[640,128]{1,0:T(8,128)(2,1)S(1)} %get-tuple-element.21), channel_id=1, source_target_pairs={{0,252},{4,0},{8,4},{12,8},{16,12},{20,16},{24,20},{28,24},{32,28}... | collective-permute-start | bytes 491528 | tf_op jit(solution)/shard_map/ppermute | solution.py:372
  88.1 0.1 collective-permute-start.24
  88.3 7.3 %collective-permute-start.26 = (f32[96,128]{1,0:T(8,128)S(1)}, f32[96,128]{1,0:T(8,128)S(1)}, u32[]{:S(2)}, u32[]{:S(2)}) collective-permute-start(f32[96,128]{1,0:T(8,128)S(1)} %add_add_fusion.1), channel_id=1, source_target_pairs={{0,192},{4,196},{8,200},{12,204},{16,208},{20,212},{24,216},{28,22... | collective-permute-start | bytes 147464 | tf_op jit(solution)/shard_map/ppermute | solution.py:372
  95.6 2.8 %collective-permute-start.13 = (bf16[640,128]{1,0:T(8,128)(2,1)S(1)}, bf16[640,128]{1,0:T(8,128)(2,1)S(1)}, u32[]{:S(2)}, u32[]{:S(2)}) collective-permute-start(bf16[640,128]{1,0:T(8,128)(2,1)S(1)} %get-tuple-element.22), channel_id=1, source_target_pairs={{0,248},{4,252},{8,0},{12,4},{16,8},{20,12},{24,16},{28,20},{32,24... | collective-permute-start | bytes 491528 | tf_op jit(solution)/shard_map/ppermute | solution.py:372
  98.5 4.9 %collective-permute-start.16 = (bf16[640,128]{1,0:T(8,128)(2,1)S(1)}, bf16[640,128]{1,0:T(8,128)(2,1)S(1)}, u32[]{:S(2)}, u32[]{:S(2)}) collective-permute-start(bf16[640,128]{1,0:T(8,128)(2,1)S(1)} %get-tuple-element.25), channel_id=1, source_target_pairs={{0,236},{4,240},{8,244},{12,248},{16,252},{20,0},{24,4},{28,8},{32... | collective-permute-start | bytes 491528 | tf_op jit(solution)/shard_map/ppermute | solution.py:372
  103.4 2.3 %collective-permute-start.17 = (bf16[640,128]{1,0:T(8,128)(2,1)S(1)}, bf16[640,128]{1,0:T(8,128)(2,1)S(1)}, u32[]{:S(2)}, u32[]{:S(2)}) collective-permute-start(bf16[640,128]{1,0:T(8,128)(2,1)S(1)} %get-tuple-element.26), channel_id=1, source_target_pairs={{0,232},{4,236},{8,240},{12,244},{16,248},{20,252},{24,0},{28,4},{... | collective-permute-start | bytes 491528 | tf_op jit(solution)/shard_map/ppermute | solution.py:372
  105.7 0.9 collective-permute-done.13
  106.6 2.4 %collective-permute-done.14 = bf16[640,128]{1,0:T(8,128)(2,1)S(1)} collective-permute-done((bf16[640,128]{1,0:T(8,128)(2,1)S(1)}, bf16[640,128]{1,0:T(8,128)(2,1)S(1)}, u32[]{:S(2)}, u32[]{:S(2)}) %collective-permute-start.14) | collective-permute-done | bytes 163872 | tf_op jit(solution)/shard_map/ppermute | solution.py:372
  109.0 1.4 %collective-permute-start.28 = (f32[96,128]{1,0:T(8,128)S(1)}, f32[96,128]{1,0:T(8,128)S(1)}, u32[]{:S(2)}, u32[]{:S(2)}) collective-permute-start(f32[96,128]{1,0:T(8,128)S(1)} %add_add_fusion), channel_id=1, source_target_pairs={{0,2},{1,3},{2,0},{3,1},{4,6},{5,7},{6,4},{7,5},{8,10},{9,11},{10,... | collective-permute-start | bytes 147464 | tf_op jit(solution)/shard_map/ppermute | solution.py:372
  110.4 12.8 %collective-permute-done.17 = bf16[640,128]{1,0:T(8,128)(2,1)S(1)} collective-permute-done((bf16[640,128]{1,0:T(8,128)(2,1)S(1)}, bf16[640,128]{1,0:T(8,128)(2,1)S(1)}, u32[]{:S(2)}, u32[]{:S(2)}) %collective-permute-start.17) | collective-permute-done | bytes 163872 | tf_op jit(solution)/shard_map/ppermute | solution.py:372
  123.2 0.9 add_bitcast_fusion
  124.2 0.3 reshape.72
  124.5 0.2 slice_multiply_fusion
  124.7 0.1 copy.29
  124.9 1.0 copy.25
  (65 shorter events, 0.8 us)
Async XLA Ops:
  0.6 8.4 %copy-start = (bf16[32,40,3,3,3]{1,0,4,3,2:T(8,128)(2,1)S(1)}, bf16[32,40,3,3,3]{1,0,4,3,2:T(8,128)(2,1)}, u32[]{:S(2)}) copy-start(bf16[32,40,3,3,3]{1,0,4,3,2:T(8,128)(2,1)} %param.15) | copy-start | bytes 207364
  0.6 22.3 %copy-start.8 = (bf16[32,384,1,1,1]{1,0,4,3,2:T(8,128)(2,1)S(1)}, bf16[32,384,1,1,1]{1,0,4,3,2:T(8,128)(2,1)}, u32[]{:S(2)}) copy-start(bf16[32,384,1,1,1]{1,0,4,3,2:T(8,128)(2,1)} %constant.41) | copy-start | bytes 73732
  0.7 29.6 %copy-start.9 = (pred[8,384]{1,0:T(8,128)(4,1)S(1)}, pred[8,384]{1,0:T(8,128)(4,1)}, u32[]{:S(2)}) copy-start(pred[8,384]{1,0:T(8,128)(4,1)} %constant.31.clone) | copy-start | bytes 9220
  0.7 29.6 %copy-start.10 = (pred[8,384]{1,0:T(8,128)(4,1)S(1)}, pred[8,384]{1,0:T(8,128)(4,1)}, u32[]{:S(2)}) copy-start(pred[8,384]{1,0:T(8,128)(4,1)} %constant.32.clone) | copy-start | bytes 9220
  0.7 29.5 %copy-start.11 = (pred[8,384]{1,0:T(8,128)(4,1)S(1)}, pred[8,384]{1,0:T(8,128)(4,1)}, u32[]{:S(2)}) copy-start(pred[8,384]{1,0:T(8,128)(4,1)} %constant.33.clone) | copy-start | bytes 9220
  0.7 22.7 %copy-start.2 = (bf16[80,8,128]{2,1,0:T(8,128)(2,1)S(1)}, bf16[80,8,128]{2,1,0:T(8,128)(2,1)}, u32[]{:S(2)}) copy-start(bf16[80,8,128]{2,1,0:T(8,128)(2,1)} %param.13) | copy-start | bytes 491524
  0.7 22.2 %collective-permute-start.2 = (bf16[12,256,128]{2,1,0:T(8,128)(2,1)}, bf16[12,256,128]{2,1,0:T(8,128)(2,1)S(1)}, u32[]{:S(2)}, u32[]{:S(2)}) collective-permute-start(bf16[12,256,128]{2,1,0:T(8,128)(2,1)} %bitcast.39), channel_id=1, source_target_pairs={{0,2},{1,3},{2,0},{3,1},{4,6},{5,7},{6,4},{7,5},{8,10},{9,11},{10,... | collective-permute-start | bytes 2359304 | tf_op jit(solution)/shard_map/ppermute | solution.py:372
  5.8 32.9 %copy-start.1 = (bf16[12,32,8,128]{3,2,1,0:T(8,128)(2,1)S(1)}, bf16[12,32,8,128]{3,2,1,0:T(8,128)(2,1)}, u32[]{:S(2)}) copy-start(bf16[12,32,8,128]{3,2,1,0:T(8,128)(2,1)} %param.14) | copy-start | bytes 2359300
  6.9 9.9 %collective-permute-start.4 = (bf16[1408,128]{1,0:T(8,128)(2,1)S(1)}, bf16[1408,128]{1,0:T(8,128)(2,1)S(1)}, u32[]{:S(2)}, u32[]{:S(2)}) collective-permute-start(bf16[1408,128]{1,0:T(8,128)(2,1)S(1)} %pad_maximum_fusion.1), channel_id=1, source_target_pairs={{0,4},{4,8},{8,12},{12,16},{16,20},{20,24},{24,28},{28,32},{32,36}... | collective-permute-start | bytes 1081352 | tf_op jit(solution)/shard_map/ppermute | solution.py:372
  8.1 6.2 %collective-permute-start = (bf16[12,64,128]{2,1,0:T(8,128)(2,1)S(1)}, bf16[12,64,128]{2,1,0:T(8,128)(2,1)S(1)}, u32[]{:S(2)}, u32[]{:S(2)}) collective-permute-start(bf16[12,64,128]{2,1,0:T(8,128)(2,1)S(1)} %bitcast.55), channel_id=1, source_target_pairs={{0,252},{4,0},{8,4},{12,8},{16,12},{20,16},{24,20},{28,24},{32,28}... | collective-permute-start | bytes 589832 | tf_op jit(solution)/shard_map/ppermute | solution.py:372
  14.3 24.2 %collective-permute-start.1 = (bf16[12,256,128]{2,1,0:T(8,128)(2,1)}, bf16[12,256,128]{2,1,0:T(8,128)(2,1)S(1)}, u32[]{:S(2)}, u32[]{:S(2)}) collective-permute-start(bf16[12,256,128]{2,1,0:T(8,128)(2,1)} %bitcast.40), channel_id=1, source_target_pairs={{0,1},{1,0},{2,3},{3,2},{4,5},{5,4},{6,7},{7,6},{8,9},{9,8},{10,11... | collective-permute-start | bytes 2359304 | tf_op jit(solution)/shard_map/ppermute | solution.py:372
  16.9 13.3 %collective-permute-start.6 = (bf16[12,128,128]{2,1,0:T(8,128)(2,1)S(1)}, bf16[12,128,128]{2,1,0:T(8,128)(2,1)S(1)}, u32[]{:S(2)}, u32[]{:S(2)}) collective-permute-start(bf16[12,128,128]{2,1,0:T(8,128)(2,1)S(1)} %pad_maximum_fusion.refs_4_), channel_id=1, source_target_pairs={{0,2},{1,3},{2,0},{3,1},{4,6},{5,7},{6,4},{7,5},{8,10},{9,11},{10,... | collective-permute-start | bytes 1179656 | tf_op jit(solution)/shard_map/ppermute | solution.py:372
  22.9 15.8 %collective-permute-start.3 = (bf16[12,256,128]{2,1,0:T(8,128)(2,1)S(1)}, bf16[12,256,128]{2,1,0:T(8,128)(2,1)S(1)}, u32[]{:S(2)}, u32[]{:S(2)}) collective-permute-start(bf16[12,256,128]{2,1,0:T(8,128)(2,1)S(1)} %collective-permute-done.2.refs_2_), channel_id=1, source_target_pairs={{0,1},{1,0},{2,3},{3,2},{4,5},{5,4},{6,7},{7,6},{8,9},{9,8},{10,11... | collective-permute-start | bytes 2359304 | tf_op jit(solution)/shard_map/ppermute | solution.py:372
  23.4 15.0 %collective-permute-start.8 = (bf16[640,128]{1,0:T(8,128)(2,1)S(1)}, bf16[640,128]{1,0:T(8,128)(2,1)S(1)}, u32[]{:S(2)}, u32[]{:S(2)}) collective-permute-start(bf16[640,128]{1,0:T(8,128)(2,1)S(1)} %bitcast.44), channel_id=1, source_target_pairs={{0,8},{4,12},{8,16},{12,20},{16,24},{20,28},{24,32},{28,36},{32,40... | collective-permute-start | bytes 491528 | tf_op jit(solution)/shard_map/ppermute | solution.py:372
  24.6 13.7 %collective-permute-start.5 = (bf16[12,128,128]{2,1,0:T(8,128)(2,1)S(1)}, bf16[12,128,128]{2,1,0:T(8,128)(2,1)S(1)}, u32[]{:S(2)}, u32[]{:S(2)}) collective-permute-start(bf16[12,128,128]{2,1,0:T(8,128)(2,1)S(1)} %pad_maximum_fusion.refs_4_), channel_id=1, source_target_pairs={{0,1},{1,0},{2,3},{3,2},{4,5},{5,4},{6,7},{7,6},{8,9},{9,8},{10,11... | collective-permute-start | bytes 1179656 | tf_op jit(solution)/shard_map/ppermute | solution.py:372
  30.2 8.5 %collective-permute-start.7 = (bf16[12,128,128]{2,1,0:T(8,128)(2,1)S(1)}, bf16[12,128,128]{2,1,0:T(8,128)(2,1)S(1)}, u32[]{:S(2)}, u32[]{:S(2)}) collective-permute-start(bf16[12,128,128]{2,1,0:T(8,128)(2,1)S(1)} %collective-permute-done.6.refs_6_), channel_id=1, source_target_pairs={{0,1},{1,0},{2,3},{3,2},{4,5},{5,4},{6,7},{7,6},{8,9},{9,8},{10,11... | collective-permute-start | bytes 1179656 | tf_op jit(solution)/shard_map/ppermute | solution.py:372
  38.3 8.8 %collective-permute-start.10 = (bf16[640,128]{1,0:T(8,128)(2,1)S(1)}, bf16[640,128]{1,0:T(8,128)(2,1)S(1)}, u32[]{:S(2)}, u32[]{:S(2)}) collective-permute-start(bf16[640,128]{1,0:T(8,128)(2,1)S(1)} %bitcast.45), channel_id=1, source_target_pairs={{0,16},{4,20},{8,24},{12,28},{16,32},{20,36},{24,40},{28,44},{32,4... | collective-permute-start | bytes 491528 | tf_op jit(solution)/shard_map/ppermute | solution.py:372
  38.4 14.4 %collective-permute-start.9 = (bf16[640,128]{1,0:T(8,128)(2,1)S(1)}, bf16[640,128]{1,0:T(8,128)(2,1)S(1)}, u32[]{:S(2)}, u32[]{:S(2)}) collective-permute-start(bf16[640,128]{1,0:T(8,128)(2,1)S(1)} %bitcast.46), channel_id=1, source_target_pairs={{0,12},{4,16},{8,20},{12,24},{16,28},{20,32},{24,36},{28,40},{32,4... | collective-permute-start | bytes 491528 | tf_op jit(solution)/shard_map/ppermute | solution.py:372
  38.5 19.4 %collective-permute-start.11 = (bf16[1280,128]{1,0:T(8,128)(2,1)S(1)}, bf16[1280,128]{1,0:T(8,128)(2,1)S(1)}, u32[]{:S(2)}, u32[]{:S(2)}) collective-permute-start(bf16[1280,128]{1,0:T(8,128)(2,1)S(1)} %pad_maximum_fusion.2), channel_id=1, source_target_pairs={{0,16},{4,20},{8,24},{12,28},{16,32},{20,36},{24,40},{28,44},{32,4... | collective-permute-start | bytes 983048 | tf_op jit(solution)/shard_map/ppermute | solution.py:372
  38.8 19.1 %copy-start.3 = (bf16[80,8,128]{2,1,0:T(8,128)(2,1)S(1)}, bf16[80,8,128]{2,1,0:T(8,128)(2,1)}, u32[]{:S(2)}) copy-start(bf16[80,8,128]{2,1,0:T(8,128)(2,1)} %param.12) | copy-start | bytes 491524
  44.7 15.6 %copy-start.6 = (f32[384,32]{1,0:T(8,128)S(1)}, f32[384,32]{1,0:T(8,128)}, u32[]{:S(2)}) copy-start(f32[384,32]{1,0:T(8,128)} %constant.35.clone.sum_ref) | copy-start | bytes 147460
  44.7 15.6 %copy-start.7 = (f32[3,8,384]{2,1,0:T(8,128)S(1)}, f32[3,8,384]{2,1,0:T(8,128)}, u32[]{:S(2)}) copy-start(f32[3,8,384]{2,1,0:T(8,128)} %constant.34.clone.mask_ref) | copy-start | bytes 110596
  60.4 21.5 %copy-start.4 = (s32[8,128]{1,0:T(8,128)S(1)}, s32[8,128]{1,0:T(8,128)}, u32[]{:S(2)}) copy-start(s32[8,128]{1,0:T(8,128)} %refs_7_.1) | copy-start | bytes 12292
  60.4 21.5 %copy-start.5 = (s32[8,128]{1,0:T(8,128)S(1)}, s32[8,128]{1,0:T(8,128)}, u32[]{:S(2)}) copy-start(s32[8,128]{1,0:T(8,128)} %refs_8_.1) | copy-start | bytes 12292
  68.0 5.8 %collective-permute-start.18 = (f32[96,128]{1,0:T(8,128)S(1)}, f32[96,128]{1,0:T(8,128)S(1)}, u32[]{:S(2)}, u32[]{:S(2)}) collective-permute-start(f32[96,128]{1,0:T(8,128)S(1)} %filter_grad.1), channel_id=1, source_target_pairs={{0,4},{4,0},{8,12},{12,8},{16,20},{20,16},{24,28},{28,24},{32,36},... | collective-permute-start | bytes 147464 | tf_op jit(solution)/shard_map/ppermute | solution.py:372
  68.6 7.2 %collective-permute-start.19 = (f32[96,128]{1,0:T(8,128)S(1)}, f32[96,128]{1,0:T(8,128)S(1)}, u32[]{:S(2)}, u32[]{:S(2)}) collective-permute-start(f32[96,128]{1,0:T(8,128)S(1)} %filter_grad.1), channel_id=1, source_target_pairs={{0,8},{4,12},{8,0},{12,4},{16,24},{20,28},{24,16},{28,20},{32,40},... | collective-permute-start | bytes 147464 | tf_op jit(solution)/shard_map/ppermute | solution.py:372
  73.3 4.1 %collective-permute-start.20 = (f32[96,128]{1,0:T(8,128)S(1)}, f32[96,128]{1,0:T(8,128)S(1)}, u32[]{:S(2)}, u32[]{:S(2)}) collective-permute-start(f32[96,128]{1,0:T(8,128)S(1)} %filter_grad.1), channel_id=1, source_target_pairs={{0,12},{4,8},{8,4},{12,0},{16,28},{20,24},{24,20},{28,16},{32,44},... | collective-permute-start | bytes 147464 | tf_op jit(solution)/shard_map/ppermute | solution.py:372
  77.4 10.7 %collective-permute-start.21 = (f32[96,128]{1,0:T(8,128)S(1)}, f32[96,128]{1,0:T(8,128)S(1)}, u32[]{:S(2)}, u32[]{:S(2)}) collective-permute-start(f32[96,128]{1,0:T(8,128)S(1)} %add_add_fusion.2), channel_id=1, source_target_pairs={{0,16},{4,20},{8,24},{12,28},{16,0},{20,4},{24,8},{28,12},{32,48},... | collective-permute-start | bytes 147464 | tf_op jit(solution)/shard_map/ppermute | solution.py:372
  77.5 10.6 %collective-permute-start.22 = (f32[96,128]{1,0:T(8,128)S(1)}, f32[96,128]{1,0:T(8,128)S(1)}, u32[]{:S(2)}, u32[]{:S(2)}) collective-permute-start(f32[96,128]{1,0:T(8,128)S(1)} %add_add_fusion.2), channel_id=1, source_target_pairs={{0,32},{4,36},{8,40},{12,44},{16,48},{20,52},{24,56},{28,60},{32,0... | collective-permute-start | bytes 147464 | tf_op jit(solution)/shard_map/ppermute | solution.py:372
  77.6 10.5 %collective-permute-start.23 = (f32[96,128]{1,0:T(8,128)S(1)}, f32[96,128]{1,0:T(8,128)S(1)}, u32[]{:S(2)}, u32[]{:S(2)}) collective-permute-start(f32[96,128]{1,0:T(8,128)S(1)} %add_add_fusion.2), channel_id=1, source_target_pairs={{0,48},{4,52},{8,56},{12,60},{16,32},{20,36},{24,40},{28,44},{32,1... | collective-permute-start | bytes 147464 | tf_op jit(solution)/shard_map/ppermute | solution.py:372
  86.1 17.3 %collective-permute-start.12 = (bf16[640,128]{1,0:T(8,128)(2,1)S(1)}, bf16[640,128]{1,0:T(8,128)(2,1)S(1)}, u32[]{:S(2)}, u32[]{:S(2)}) collective-permute-start(bf16[640,128]{1,0:T(8,128)(2,1)S(1)} %get-tuple-element.21), channel_id=1, source_target_pairs={{0,252},{4,0},{8,4},{12,8},{16,12},{20,16},{24,20},{28,24},{32,28}... | collective-permute-start | bytes 491528 | tf_op jit(solution)/shard_map/ppermute | solution.py:372
  88.1 10.3 %collective-permute-start.24 = (f32[96,128]{1,0:T(8,128)S(1)}, f32[96,128]{1,0:T(8,128)S(1)}, u32[]{:S(2)}, u32[]{:S(2)}) collective-permute-start(f32[96,128]{1,0:T(8,128)S(1)} %add_add_fusion.1), channel_id=1, source_target_pairs={{0,64},{4,68},{8,72},{12,76},{16,80},{20,84},{24,88},{28,92},{32,9... | collective-permute-start | bytes 147464 | tf_op jit(solution)/shard_map/ppermute | solution.py:372
  88.2 10.2 %collective-permute-start.25 = (f32[96,128]{1,0:T(8,128)S(1)}, f32[96,128]{1,0:T(8,128)S(1)}, u32[]{:S(2)}, u32[]{:S(2)}) collective-permute-start(f32[96,128]{1,0:T(8,128)S(1)} %add_add_fusion.1), channel_id=1, source_target_pairs={{0,128},{4,132},{8,136},{12,140},{16,144},{20,148},{24,152},{28,15... | collective-permute-start | bytes 147464 | tf_op jit(solution)/shard_map/ppermute | solution.py:372
  88.3 10.2 %collective-permute-start.26 = (f32[96,128]{1,0:T(8,128)S(1)}, f32[96,128]{1,0:T(8,128)S(1)}, u32[]{:S(2)}, u32[]{:S(2)}) collective-permute-start(f32[96,128]{1,0:T(8,128)S(1)} %add_add_fusion.1), channel_id=1, source_target_pairs={{0,192},{4,196},{8,200},{12,204},{16,208},{20,212},{24,216},{28,22... | collective-permute-start | bytes 147464 | tf_op jit(solution)/shard_map/ppermute | solution.py:372
  95.6 11.0 %collective-permute-start.13 = (bf16[640,128]{1,0:T(8,128)(2,1)S(1)}, bf16[640,128]{1,0:T(8,128)(2,1)S(1)}, u32[]{:S(2)}, u32[]{:S(2)}) collective-permute-start(bf16[640,128]{1,0:T(8,128)(2,1)S(1)} %get-tuple-element.22), channel_id=1, source_target_pairs={{0,248},{4,252},{8,0},{12,4},{16,8},{20,12},{24,16},{28,20},{32,24... | collective-permute-start | bytes 491528 | tf_op jit(solution)/shard_map/ppermute | solution.py:372
  98.4 10.6 %collective-permute-start.14 = (bf16[640,128]{1,0:T(8,128)(2,1)S(1)}, bf16[640,128]{1,0:T(8,128)(2,1)S(1)}, u32[]{:S(2)}, u32[]{:S(2)}) collective-permute-start(bf16[640,128]{1,0:T(8,128)(2,1)S(1)} %get-tuple-element.23), channel_id=1, source_target_pairs={{0,244},{4,248},{8,252},{12,0},{16,4},{20,8},{24,12},{28,16},{32,2... | collective-permute-start | bytes 491528 | tf_op jit(solution)/shard_map/ppermute | solution.py:372
  98.4 12.0 %collective-permute-start.15 = (bf16[640,128]{1,0:T(8,128)(2,1)S(1)}, bf16[640,128]{1,0:T(8,128)(2,1)S(1)}, u32[]{:S(2)}, u32[]{:S(2)}) collective-permute-start(bf16[640,128]{1,0:T(8,128)(2,1)S(1)} %get-tuple-element.24), channel_id=1, source_target_pairs={{0,240},{4,244},{8,248},{12,252},{16,0},{20,4},{24,8},{28,12},{32,... | collective-permute-start | bytes 491528 | tf_op jit(solution)/shard_map/ppermute | solution.py:372
  98.5 11.9 %collective-permute-start.16 = (bf16[640,128]{1,0:T(8,128)(2,1)S(1)}, bf16[640,128]{1,0:T(8,128)(2,1)S(1)}, u32[]{:S(2)}, u32[]{:S(2)}) collective-permute-start(bf16[640,128]{1,0:T(8,128)(2,1)S(1)} %get-tuple-element.25), channel_id=1, source_target_pairs={{0,236},{4,240},{8,244},{12,248},{16,252},{20,0},{24,4},{28,8},{32... | collective-permute-start | bytes 491528 | tf_op jit(solution)/shard_map/ppermute | solution.py:372
  103.4 19.8 %collective-permute-start.17 = (bf16[640,128]{1,0:T(8,128)(2,1)S(1)}, bf16[640,128]{1,0:T(8,128)(2,1)S(1)}, u32[]{:S(2)}, u32[]{:S(2)}) collective-permute-start(bf16[640,128]{1,0:T(8,128)(2,1)S(1)} %get-tuple-element.26), channel_id=1, source_target_pairs={{0,232},{4,236},{8,240},{12,244},{16,248},{20,252},{24,0},{28,4},{... | collective-permute-start | bytes 491528 | tf_op jit(solution)/shard_map/ppermute | solution.py:372
  106.6 17.5 %collective-permute-start.27 = (f32[96,128]{1,0:T(8,128)S(1)}, f32[96,128]{1,0:T(8,128)S(1)}, u32[]{:S(2)}, u32[]{:S(2)}) collective-permute-start(f32[96,128]{1,0:T(8,128)S(1)} %add_add_fusion), channel_id=1, source_target_pairs={{0,3},{1,2},{2,1},{3,0},{4,7},{5,6},{6,5},{7,4},{8,11},{9,10},{10,... | collective-permute-start | bytes 147464 | tf_op jit(solution)/shard_map/ppermute | solution.py:372
  109.0 15.1 %collective-permute-start.28 = (f32[96,128]{1,0:T(8,128)S(1)}, f32[96,128]{1,0:T(8,128)S(1)}, u32[]{:S(2)}, u32[]{:S(2)}) collective-permute-start(f32[96,128]{1,0:T(8,128)S(1)} %add_add_fusion), channel_id=1, source_target_pairs={{0,2},{1,3},{2,0},{3,1},{4,6},{5,7},{6,4},{7,5},{8,10},{9,11},{10,... | collective-permute-start | bytes 147464 | tf_op jit(solution)/shard_map/ppermute | solution.py:372
  110.4 13.7 %collective-permute-start.29 = (f32[96,128]{1,0:T(8,128)S(1)}, f32[96,128]{1,0:T(8,128)S(1)}, u32[]{:S(2)}, u32[]{:S(2)}) collective-permute-start(f32[96,128]{1,0:T(8,128)S(1)} %add_add_fusion), channel_id=1, source_target_pairs={{0,1},{1,0},{2,3},{3,2},{4,5},{5,4},{6,7},{7,6},{8,9},{9,8},{10,11... | collective-permute-start | bytes 147464 | tf_op jit(solution)/shard_map/ppermute | solution.py:372

commit v3 on v2

--- a/solution.py
+++ b/solution.py
@@ -381,14 +381,17 @@
     return moved(value, "grp", lambda i: i ^ bits)
 
 
-def summed_over_lon(value):
-    for unit in (1, 4, 16):
-        value = value + sum(moved(value, "lon", lambda i: i ^ (unit * k)) for k in (1, 2, 3))
-    return value
-
-
 def together(value, other):
     return lax.optimization_barrier((value, other))[0]
+
+
+def summed_over_lon(value, gates):
+    for unit, gate in zip((1, 4, 16), gates):
+        parts = [moved(value, "lon", lambda i: i ^ (unit * k)) for k in (1, 2, 3)]
+        value = value + parts[0] + parts[1] + parts[2]
+        if gate is not None:
+            value = together(value, gate)
+    return value
 
 
 def shards(left_feat, right_feat, conv_cot, conv_weight, disparity_shift, valid_mask):
@@ -414,16 +417,15 @@
     grad_cost = run_conv(rank_array, conv_matrix(conv_weight, rank), slabs)
     volume = run_cost(together(left, grad_cost), panels)
     filter_part = run_filter(rank_array, volume, slabs)
-    outs = run_grad(
-        together(left, filter_part), panels, grad_cost, disparity_shift, valid_mask
-    )
+    outs = run_grad(together(left, filter_part), panels, grad_cost, disparity_shift, valid_mask)
     left_grad = outs[0].reshape(80, 8, 128)
+    back = {k: along(outs[7 - k], -k) for k in (6, 5, 4, 3, 2, 1)}
     right_grad = outs[7]
     for k in range(1, 7):
-        right_grad = right_grad + along(outs[1 + 6 - k], -k).astype(F32)
+        right_grad = right_grad + back[k].astype(F32)
     right_grad = right_grad.reshape(80, 8, 128)
-
-    total = summed_over_lon(filter_part)
+    total = summed_over_lon(filter_part, (outs[7], None, None))
+
     pieces = [total] + [across(total, k) for k in range(1, 4)]
     odd, high = (rank & 1) == 1, (rank & 2) == 2
     pieces = [jnp.where(odd, pieces[k ^ 1], pieces[k]) for k in range(4)]

time: 126 us -> 124 us (0.984)
  waiting for transfers between devices: 59.2 us -> 53.2 us
  starting transfers between devices: 38.8 us -> 41.6 us
    ppermute x30, waiting for transfers between devices: 59.2 us -> 53.2 us  [moved(): return lax.ppermute(value, axis, pairs)]
    ppermute x30, starting transfers between devices: 38.8 us -> 41.6 us  [moved(): return lax.ppermute(value, axis, pairs)]
  transfers between devices with their start and end apart: 30 -> 30, of which waited for: 13 -> 12; matrix products, arithmetic and copies ran while one was open for 4% -> 4% of each run, Pallas kernels for 8% -> 8%
where the time goes in v3:
time: 124 us; the launch traced here: 123 us
  waiting for transfers between devices  53.2 us (43%)
  starting transfers between devices  41.6 us (34%)
  Pallas kernels  20.2 us (16%)
  local copies, waits for them, and re-layouts  3.94 us (3%)
  other arithmetic  2.49 us (2%)
    ppermute x30, waiting for transfers between devices, moved(): return lax.ppermute(value, axis, pairs)  53.2 us
    ppermute x30, starting transfers between devices, moved(): return lax.ppermute(value, axis, pairs)  41.6 us
    pallas_call x1, Pallas kernels, run_filter(): pl.pallas_call(filter_kernel, out_shape=jax.ShapeDtypeStruct((96, 128), F...  7.57 us
    pallas_call x1, Pallas kernels, run_conv(): pl.pallas_call(conv_kernel, out_shape=jax.ShapeDtypeStruct((DISP, 80, 128...  5.92 us
    pallas_call x1, Pallas kernels, run_grad(): pl.pallas_call(grad_kernel, out_shape=[jax.ShapeDtypeStruct((640, 128), F...  4.26 us
  transfers between devices with their start and end apart: 30, of which 12 were waited for; matrix products, arithmetic and copies ran while one was open for 4% of the time, Pallas kernels for 8%

profile of v3, /device:TPU:4, one launch (start us, length us, event | category | flops | bytes accessed | tf_op | source)
XLA Modules:
  0.0 122.6 jit_solution(10566824360706179072)
XLA Ops:
  0.7 3.3 %collective-permute-start.2 = (bf16[12,256,128]{2,1,0:T(8,128)(2,1)}, bf16[12,256,128]{2,1,0:T(8,128)(2,1)S(1)}, u32[]{:S(2)}, u32[]{:S(2)}) collective-permute-start(bf16[12,256,128]{2,1,0:T(8,128)(2,1)} %bitcast.39), channel_id=1, source_target_pairs={{0,2},{1,3},{2,0},{3,1},{4,6},{5,7},{6,4},{7,5},{8,10},{9,11},{10,... | collective-permute-start | bytes 2359304 | tf_op jit(solution)/shard_map/ppermute | solution.py:372
  4.0 1.9 %fusion.2 = (bf16[12,32,2,128]{3,2,1,0:T(2,128)(2,1)S(1)}, bf16[12,32,2,128]{3,2,1,0:T(2,128)(2,1)S(1)}) fusion(bf16[12,32,8,128]{3,2,1,0:T(8,128)(2,1)} %param.14), kind=kLoop, calls=%fused_computation.27 | loop fusion | bytes 786432 | tf_op jit(solution)/shard_map/slice | solution.py:405
  5.9 1.0 pad_maximum_fusion.1
  6.9 1.3 %collective-permute-start.4 = (bf16[1408,128]{1,0:T(8,128)(2,1)S(1)}, bf16[1408,128]{1,0:T(8,128)(2,1)S(1)}, u32[]{:S(2)}, u32[]{:S(2)}) collective-permute-start(bf16[1408,128]{1,0:T(8,128)(2,1)S(1)} %pad_maximum_fusion.1), channel_id=1, source_target_pairs={{0,4},{4,8},{8,12},{12,16},{16,20},{20,24},{24,28},{28,32},{32,36}... | collective-permute-start | bytes 1081352 | tf_op jit(solution)/shard_map/ppermute | solution.py:372
  8.1 0.8 collective-permute-start
  9.0 0.1 constant_dynamic-slice_fusion
  9.1 0.2 copy.27
  9.4 5.0 %collective-permute-done = bf16[12,64,128]{2,1,0:T(8,128)(2,1)S(1)} collective-permute-done((bf16[12,64,128]{2,1,0:T(8,128)(2,1)S(1)}, bf16[12,64,128]{2,1,0:T(8,128)(2,1)S(1)}, u32[]{:S(2)}, u32[]{:S(2)}) %collective-permute-start) | collective-permute-done | bytes 196640 | tf_op jit(solution)/shard_map/ppermute | solution.py:372
  14.3 2.5 %collective-permute-done.4.refs_0_ = bf16[1408,128]{1,0:T(8,128)(2,1)S(1)} collective-permute-done((bf16[1408,128]{1,0:T(8,128)(2,1)S(1)}, bf16[1408,128]{1,0:T(8,128)(2,1)S(1)}, u32[]{:S(2)}, u32[]{:S(2)}) %collective-permute-start.4) | collective-permute-done | bytes 360480 | tf_op jit(solution)/shard_map/ppermute | solution.py:372
  16.9 0.4 collective-permute-start.6
  17.3 5.6 %collective-permute-done.2.refs_2_ = bf16[12,256,128]{2,1,0:T(8,128)(2,1)S(1)} collective-permute-done((bf16[12,256,128]{2,1,0:T(8,128)(2,1)}, bf16[12,256,128]{2,1,0:T(8,128)(2,1)S(1)}, u32[]{:S(2)}, u32[]{:S(2)}) %collective-permute-start.2) | collective-permute-done | bytes 786464 | tf_op jit(solution)/shard_map/ppermute | solution.py:372
  22.9 0.2 fusion
  23.4 1.3 %collective-permute-start.8 = (bf16[640,128]{1,0:T(8,128)(2,1)S(1)}, bf16[640,128]{1,0:T(8,128)(2,1)S(1)}, u32[]{:S(2)}, u32[]{:S(2)}) collective-permute-start(bf16[640,128]{1,0:T(8,128)(2,1)S(1)} %bitcast.44), channel_id=1, source_target_pairs={{0,8},{4,12},{8,16},{12,20},{16,24},{20,28},{24,32},{28,36},{32,40... | collective-permute-start | bytes 491528 | tf_op jit(solution)/shard_map/ppermute | solution.py:372
  24.6 0.2 collective-permute-start.5
  24.9 5.4 %collective-permute-done.6.refs_6_ = bf16[12,128,128]{2,1,0:T(8,128)(2,1)S(1)} collective-permute-done((bf16[12,128,128]{2,1,0:T(8,128)(2,1)S(1)}, bf16[12,128,128]{2,1,0:T(8,128)(2,1)S(1)}, u32[]{:S(2)}, u32[]{:S(2)}) %collective-permute-start.6) | collective-permute-done | bytes 393248 | tf_op jit(solution)/shard_map/ppermute | solution.py:372
  30.2 0.3 select_add_fusion
  30.6 7.8 %collective-permute-done.8.refs_1_ = bf16[640,128]{1,0:T(8,128)(2,1)S(1)} collective-permute-done((bf16[640,128]{1,0:T(8,128)(2,1)S(1)}, bf16[640,128]{1,0:T(8,128)(2,1)S(1)}, u32[]{:S(2)}, u32[]{:S(2)}) %collective-permute-start.8) | collective-permute-done | bytes 163872 | tf_op jit(solution)/shard_map/ppermute | solution.py:372
  38.5 0.3 collective-permute-start.11
  38.8 5.9 %filter_transpose.1.refs_6_ = bf16[48,80,128]{2,1,0:T(8,128)(2,1)S(1)} custom-call(s32[1]{0:T(128)} %bitcast.1.rank_ref, bf16[240,1152]{1,0:T(8,128)(2,1)S(1)} %bitcast.38, bf16[12,256,128]{2,1,0:T(8,128)(2,1)S(1)} %bitcast.41, bf16[12,256,128]{2,1,0:T(8,128)(2,1)S(1)} %collective-permute-done.1.refs_1_, ...), custom_call_target="tpu_custom_call" | custom-call | flops 7000000000 | bytes 6000000 | tf_op jit(solution)/shard_map/filter_transpose/pallas_call | solution.py:275
  44.8 2.4 %collective-permute-done.10.refs_3_ = bf16[640,128]{1,0:T(8,128)(2,1)S(1)} collective-permute-done((bf16[640,128]{1,0:T(8,128)(2,1)S(1)}, bf16[640,128]{1,0:T(8,128)(2,1)S(1)}, u32[]{:S(2)}, u32[]{:S(2)}) %collective-permute-start.10) | collective-permute-done | bytes 163872 | tf_op jit(solution)/shard_map/ppermute | solution.py:372
  47.2 5.6 %collective-permute-done.9.refs_2_ = bf16[640,128]{1,0:T(8,128)(2,1)S(1)} collective-permute-done((bf16[640,128]{1,0:T(8,128)(2,1)S(1)}, bf16[640,128]{1,0:T(8,128)(2,1)S(1)}, u32[]{:S(2)}, u32[]{:S(2)}) %collective-permute-start.9) | collective-permute-done | bytes 163872 | tf_op jit(solution)/shard_map/ppermute | solution.py:372
  52.8 5.2 %collective-permute-done.11.refs_4_ = bf16[1280,128]{1,0:T(8,128)(2,1)S(1)} collective-permute-done((bf16[1280,128]{1,0:T(8,128)(2,1)S(1)}, bf16[1280,128]{1,0:T(8,128)(2,1)S(1)}, u32[]{:S(2)}, u32[]{:S(2)}) %collective-permute-start.11) | collective-permute-done | bytes 327712 | tf_op jit(solution)/shard_map/ppermute | solution.py:372
  57.9 2.4 %cost_volume.1.volume = bf16[52,240,128]{2,1,0:T(8,128)(2,1)S(1)} custom-call(bf16[640,128]{1,0:T(8,128)(2,1)S(1)} %bitcast.49, bf16[1408,128]{1,0:T(8,128)(2,1)S(1)} %collective-permute-done.4.refs_0_, bf16[640,128]{1,0:T(8,128)(2,1)S(1)} %collective-permute-done.8.refs_1_, bf16[640,128]{1,0:T(8,128)(2,1)S(1)} %collective-permute-done.9.refs_2_, ...), custom_call_target="tpu_custom_call" | custom-call | flops 5000000000 | bytes 4000000 | tf_op jit(solution)/shard_map/cost_volume/pallas_call | solution.py:288
  60.4 7.6 %filter_grad.1 = f32[96,128]{1,0:T(8,128)S(1)} custom-call(s32[1]{0:T(128)} %bitcast.1.rank_ref, bf16[52,240,128]{2,1,0:T(8,128)(2,1)S(1)} %cost_volume.1.volume, f32[3,8,384]{2,1,0:T(8,128)S(1)} %copy-done.7, f32[384,32]{1,0:T(8,128)S(1)} %copy-done.6, bf16[12,256,128]{2,1,0:T(8,128)(2,1)S(1)} %bitcast.42, ...), custom_call_target="tpu_custom_call" | custom-call | flops 8000000000 | bytes 4000000 | tf_op jit(solution)/shard_map/filter_grad/pallas_call | solution.py:313
  68.0 0.7 collective-permute-start.18
  68.6 4.7 %collective-permute-start.19 = (f32[96,128]{1,0:T(8,128)S(1)}, f32[96,128]{1,0:T(8,128)S(1)}, u32[]{:S(2)}, u32[]{:S(2)}) collective-permute-start(f32[96,128]{1,0:T(8,128)S(1)} %filter_grad.1), channel_id=1, source_target_pairs={{0,8},{4,12},{8,0},{12,4},{16,24},{20,28},{24,16},{28,20},{32,40},... | collective-permute-start | bytes 147464 | tf_op jit(solution)/shard_map/ppermute | solution.py:372
  73.3 0.5 collective-permute-start.20
  73.7 4.3 %feature_grads.1 = (f32[640,128]{1,0:T(8,128)}, bf16[640,128]{1,0:T(8,128)(2,1)S(1)}, bf16[640,128]{1,0:T(8,128)(2,1)S(1)}, bf16[640,128]{1,0:T(8,128)(2,1)S(1)}...) custom-call(bf16[640,128]{1,0:T(8,128)(2,1)S(1)} %bitcast.50, ...), custom_call_target="tpu_custom_call" | custom-call | flops 5000000000 | bytes 4000000 | tf_op jit(solution)/shard_map/feature_grads/pallas_call | solution.py:330
  78.0 0.1 collective-permute-start.21
  78.2 4.3 %collective-permute-start.23 = (f32[96,128]{1,0:T(8,128)S(1)}, f32[96,128]{1,0:T(8,128)S(1)}, u32[]{:S(2)}, u32[]{:S(2)}) collective-permute-start(f32[96,128]{1,0:T(8,128)S(1)} %add_add_fusion.2), channel_id=1, source_target_pairs={{0,48},{4,52},{8,56},{12,60},{16,32},{20,36},{24,40},{28,44},{32,1... | collective-permute-start | bytes 147464 | tf_op jit(solution)/shard_map/ppermute | solution.py:372
  82.5 1.6 %collective-permute-start.12 = (bf16[640,128]{1,0:T(8,128)(2,1)S(1)}, bf16[640,128]{1,0:T(8,128)(2,1)S(1)}, u32[]{:S(2)}, u32[]{:S(2)}) collective-permute-start(bf16[640,128]{1,0:T(8,128)(2,1)S(1)} %get-tuple-element.22), channel_id=1, source_target_pairs={{0,252},{4,0},{8,4},{12,8},{16,12},{20,16},{24,20},{28,24},{32,28}... | collective-permute-start | bytes 491528 | tf_op jit(solution)/shard_map/ppermute | solution.py:372
  84.1 1.0 collective-permute-done.23
  85.1 0.7 collective-permute-start.24
  85.8 2.2 %collective-permute-start.25 = (f32[96,128]{1,0:T(8,128)S(1)}, f32[96,128]{1,0:T(8,128)S(1)}, u32[]{:S(2)}, u32[]{:S(2)}) collective-permute-start(f32[96,128]{1,0:T(8,128)S(1)} %add_add_fusion.1), channel_id=1, source_target_pairs={{0,128},{4,132},{8,136},{12,140},{16,144},{20,148},{24,152},{28,15... | collective-permute-start | bytes 147464 | tf_op jit(solution)/shard_map/ppermute | solution.py:372
  88.0 4.6 %collective-permute-start.26 = (f32[96,128]{1,0:T(8,128)S(1)}, f32[96,128]{1,0:T(8,128)S(1)}, u32[]{:S(2)}, u32[]{:S(2)}) collective-permute-start(f32[96,128]{1,0:T(8,128)S(1)} %add_add_fusion.1), channel_id=1, source_target_pairs={{0,192},{4,196},{8,200},{12,204},{16,208},{20,212},{24,216},{28,22... | collective-permute-start | bytes 147464 | tf_op jit(solution)/shard_map/ppermute | solution.py:372
  92.6 4.3 %collective-permute-start.13 = (bf16[640,128]{1,0:T(8,128)(2,1)S(1)}, bf16[640,128]{1,0:T(8,128)(2,1)S(1)}, u32[]{:S(2)}, u32[]{:S(2)}) collective-permute-start(bf16[640,128]{1,0:T(8,128)(2,1)S(1)} %get-tuple-element.23), channel_id=1, source_target_pairs={{0,248},{4,252},{8,0},{12,4},{16,8},{20,12},{24,16},{28,20},{32,24... | collective-permute-start | bytes 491528 | tf_op jit(solution)/shard_map/ppermute | solution.py:372
  97.0 0.4 collective-permute-done.26
  97.4 5.7 %collective-permute-start.16 = (bf16[640,128]{1,0:T(8,128)(2,1)S(1)}, bf16[640,128]{1,0:T(8,128)(2,1)S(1)}, u32[]{:S(2)}, u32[]{:S(2)}) collective-permute-start(bf16[640,128]{1,0:T(8,128)(2,1)S(1)} %get-tuple-element.26), channel_id=1, source_target_pairs={{0,236},{4,240},{8,244},{12,248},{16,252},{20,0},{24,4},{28,8},{32... | collective-permute-start | bytes 491528 | tf_op jit(solution)/shard_map/ppermute | solution.py:372
  103.1 2.6 %collective-permute-start.17 = (bf16[640,128]{1,0:T(8,128)(2,1)S(1)}, bf16[640,128]{1,0:T(8,128)(2,1)S(1)}, u32[]{:S(2)}, u32[]{:S(2)}) collective-permute-start(bf16[640,128]{1,0:T(8,128)(2,1)S(1)} %get-tuple-element.27), channel_id=1, source_target_pairs={{0,232},{4,236},{8,240},{12,244},{16,248},{20,252},{24,0},{28,4},{... | collective-permute-start | bytes 491528 | tf_op jit(solution)/shard_map/ppermute | solution.py:372
  105.8 1.5 %collective-permute-done.14 = bf16[640,128]{1,0:T(8,128)(2,1)S(1)} collective-permute-done((bf16[640,128]{1,0:T(8,128)(2,1)S(1)}, bf16[640,128]{1,0:T(8,128)(2,1)S(1)}, u32[]{:S(2)}, u32[]{:S(2)}) %collective-permute-start.14) | collective-permute-done | bytes 163872 | tf_op jit(solution)/shard_map/ppermute | solution.py:372
  107.3 1.5 %collective-permute-start.28 = (f32[96,128]{1,0:T(8,128)S(1)}, f32[96,128]{1,0:T(8,128)S(1)}, u32[]{:S(2)}, u32[]{:S(2)}) collective-permute-start(f32[96,128]{1,0:T(8,128)S(1)} %add_add_fusion), channel_id=1, source_target_pairs={{0,2},{1,3},{2,0},{3,1},{4,6},{5,7},{6,4},{7,5},{8,10},{9,11},{10,... | collective-permute-start | bytes 147464 | tf_op jit(solution)/shard_map/ppermute | solution.py:372
  108.8 0.4 collective-permute-start.29
  109.2 10.8 %collective-permute-done.17 = bf16[640,128]{1,0:T(8,128)(2,1)S(1)} collective-permute-done((bf16[640,128]{1,0:T(8,128)(2,1)S(1)}, bf16[640,128]{1,0:T(8,128)(2,1)S(1)}, u32[]{:S(2)}, u32[]{:S(2)}) %collective-permute-start.17) | collective-permute-done | bytes 163872 | tf_op jit(solution)/shard_map/ppermute | solution.py:372
  120.0 0.9 add_bitcast_fusion
  121.0 0.3 reshape.72
  121.3 0.2 slice_multiply_fusion
  121.5 0.1 copy.29
  121.7 1.0 copy.25
  (65 shorter events, 0.9 us)
Async XLA Ops:
  0.6 8.4 %copy-start = (bf16[32,40,3,3,3]{1,0,4,3,2:T(8,128)(2,1)S(1)}, bf16[32,40,3,3,3]{1,0,4,3,2:T(8,128)(2,1)}, u32[]{:S(2)}) copy-start(bf16[32,40,3,3,3]{1,0,4,3,2:T(8,128)(2,1)} %param.15) | copy-start | bytes 207364
  0.6 22.3 %copy-start.8 = (bf16[32,384,1,1,1]{1,0,4,3,2:T(8,128)(2,1)S(1)}, bf16[32,384,1,1,1]{1,0,4,3,2:T(8,128)(2,1)}, u32[]{:S(2)}) copy-start(bf16[32,384,1,1,1]{1,0,4,3,2:T(8,128)(2,1)} %constant.41) | copy-start | bytes 73732
  0.7 29.6 %copy-start.9 = (pred[8,384]{1,0:T(8,128)(4,1)S(1)}, pred[8,384]{1,0:T(8,128)(4,1)}, u32[]{:S(2)}) copy-start(pred[8,384]{1,0:T(8,128)(4,1)} %constant.31.clone) | copy-start | bytes 9220
  0.7 29.6 %copy-start.10 = (pred[8,384]{1,0:T(8,128)(4,1)S(1)}, pred[8,384]{1,0:T(8,128)(4,1)}, u32[]{:S(2)}) copy-start(pred[8,384]{1,0:T(8,128)(4,1)} %constant.32.clone) | copy-start | bytes 9220
  0.7 29.5 %copy-start.11 = (pred[8,384]{1,0:T(8,128)(4,1)S(1)}, pred[8,384]{1,0:T(8,128)(4,1)}, u32[]{:S(2)}) copy-start(pred[8,384]{1,0:T(8,128)(4,1)} %constant.33.clone) | copy-start | bytes 9220
  0.7 22.7 %copy-start.2 = (bf16[80,8,128]{2,1,0:T(8,128)(2,1)S(1)}, bf16[80,8,128]{2,1,0:T(8,128)(2,1)}, u32[]{:S(2)}) copy-start(bf16[80,8,128]{2,1,0:T(8,128)(2,1)} %param.13) | copy-start | bytes 491524
  0.7 22.2 %collective-permute-start.2 = (bf16[12,256,128]{2,1,0:T(8,128)(2,1)}, bf16[12,256,128]{2,1,0:T(8,128)(2,1)S(1)}, u32[]{:S(2)}, u32[]{:S(2)}) collective-permute-start(bf16[12,256,128]{2,1,0:T(8,128)(2,1)} %bitcast.39), channel_id=1, source_target_pairs={{0,2},{1,3},{2,0},{3,1},{4,6},{5,7},{6,4},{7,5},{8,10},{9,11},{10,... | collective-permute-start | bytes 2359304 | tf_op jit(solution)/shard_map/ppermute | solution.py:372
  5.8 32.9 %copy-start.1 = (bf16[12,32,8,128]{3,2,1,0:T(8,128)(2,1)S(1)}, bf16[12,32,8,128]{3,2,1,0:T(8,128)(2,1)}, u32[]{:S(2)}) copy-start(bf16[12,32,8,128]{3,2,1,0:T(8,128)(2,1)} %param.14) | copy-start | bytes 2359300
  6.9 9.9 %collective-permute-start.4 = (bf16[1408,128]{1,0:T(8,128)(2,1)S(1)}, bf16[1408,128]{1,0:T(8,128)(2,1)S(1)}, u32[]{:S(2)}, u32[]{:S(2)}) collective-permute-start(bf16[1408,128]{1,0:T(8,128)(2,1)S(1)} %pad_maximum_fusion.1), channel_id=1, source_target_pairs={{0,4},{4,8},{8,12},{12,16},{16,20},{20,24},{24,28},{28,32},{32,36}... | collective-permute-start | bytes 1081352 | tf_op jit(solution)/shard_map/ppermute | solution.py:372
  8.1 6.2 %collective-permute-start = (bf16[12,64,128]{2,1,0:T(8,128)(2,1)S(1)}, bf16[12,64,128]{2,1,0:T(8,128)(2,1)S(1)}, u32[]{:S(2)}, u32[]{:S(2)}) collective-permute-start(bf16[12,64,128]{2,1,0:T(8,128)(2,1)S(1)} %bitcast.55), channel_id=1, source_target_pairs={{0,252},{4,0},{8,4},{12,8},{16,12},{20,16},{24,20},{28,24},{32,28}... | collective-permute-start | bytes 589832 | tf_op jit(solution)/shard_map/ppermute | solution.py:372
  14.3 24.2 %collective-permute-start.1 = (bf16[12,256,128]{2,1,0:T(8,128)(2,1)}, bf16[12,256,128]{2,1,0:T(8,128)(2,1)S(1)}, u32[]{:S(2)}, u32[]{:S(2)}) collective-permute-start(bf16[12,256,128]{2,1,0:T(8,128)(2,1)} %bitcast.40), channel_id=1, source_target_pairs={{0,1},{1,0},{2,3},{3,2},{4,5},{5,4},{6,7},{7,6},{8,9},{9,8},{10,11... | collective-permute-start | bytes 2359304 | tf_op jit(solution)/shard_map/ppermute | solution.py:372
  16.9 13.3 %collective-permute-start.6 = (bf16[12,128,128]{2,1,0:T(8,128)(2,1)S(1)}, bf16[12,128,128]{2,1,0:T(8,128)(2,1)S(1)}, u32[]{:S(2)}, u32[]{:S(2)}) collective-permute-start(bf16[12,128,128]{2,1,0:T(8,128)(2,1)S(1)} %pad_maximum_fusion.refs_4_), channel_id=1, source_target_pairs={{0,2},{1,3},{2,0},{3,1},{4,6},{5,7},{6,4},{7,5},{8,10},{9,11},{10,... | collective-permute-start | bytes 1179656 | tf_op jit(solution)/shard_map/ppermute | solution.py:372
  22.9 15.8 %collective-permute-start.3 = (bf16[12,256,128]{2,1,0:T(8,128)(2,1)S(1)}, bf16[12,256,128]{2,1,0:T(8,128)(2,1)S(1)}, u32[]{:S(2)}, u32[]{:S(2)}) collective-permute-start(bf16[12,256,128]{2,1,0:T(8,128)(2,1)S(1)} %collective-permute-done.2.refs_2_), channel_id=1, source_target_pairs={{0,1},{1,0},{2,3},{3,2},{4,5},{5,4},{6,7},{7,6},{8,9},{9,8},{10,11... | collective-permute-start | bytes 2359304 | tf_op jit(solution)/shard_map/ppermute | solution.py:372
  23.4 15.0 %collective-permute-start.8 = (bf16[640,128]{1,0:T(8,128)(2,1)S(1)}, bf16[640,128]{1,0:T(8,128)(2,1)S(1)}, u32[]{:S(2)}, u32[]{:S(2)}) collective-permute-start(bf16[640,128]{1,0:T(8,128)(2,1)S(1)} %bitcast.44), channel_id=1, source_target_pairs={{0,8},{4,12},{8,16},{12,20},{16,24},{20,28},{24,32},{28,36},{32,40... | collective-permute-start | bytes 491528 | tf_op jit(solution)/shard_map/ppermute | solution.py:372
  24.6 13.7 %collective-permute-start.5 = (bf16[12,128,128]{2,1,0:T(8,128)(2,1)S(1)}, bf16[12,128,128]{2,1,0:T(8,128)(2,1)S(1)}, u32[]{:S(2)}, u32[]{:S(2)}) collective-permute-start(bf16[12,128,128]{2,1,0:T(8,128)(2,1)S(1)} %pad_maximum_fusion.refs_4_), channel_id=1, source_target_pairs={{0,1},{1,0},{2,3},{3,2},{4,5},{5,4},{6,7},{7,6},{8,9},{9,8},{10,11... | collective-permute-start | bytes 1179656 | tf_op jit(solution)/shard_map/ppermute | solution.py:372
  30.2 8.5 %collective-permute-start.7 = (bf16[12,128,128]{2,1,0:T(8,128)(2,1)S(1)}, bf16[12,128,128]{2,1,0:T(8,128)(2,1)S(1)}, u32[]{:S(2)}, u32[]{:S(2)}) collective-permute-start(bf16[12,128,128]{2,1,0:T(8,128)(2,1)S(1)} %collective-permute-done.6.refs_6_), channel_id=1, source_target_pairs={{0,1},{1,0},{2,3},{3,2},{4,5},{5,4},{6,7},{7,6},{8,9},{9,8},{10,11... | collective-permute-start | bytes 1179656 | tf_op jit(solution)/shard_map/ppermute | solution.py:372
  38.3 8.8 %collective-permute-start.10 = (bf16[640,128]{1,0:T(8,128)(2,1)S(1)}, bf16[640,128]{1,0:T(8,128)(2,1)S(1)}, u32[]{:S(2)}, u32[]{:S(2)}) collective-permute-start(bf16[640,128]{1,0:T(8,128)(2,1)S(1)} %bitcast.45), channel_id=1, source_target_pairs={{0,16},{4,20},{8,24},{12,28},{16,32},{20,36},{24,40},{28,44},{32,4... | collective-permute-start | bytes 491528 | tf_op jit(solution)/shard_map/ppermute | solution.py:372
  38.4 14.4 %collective-permute-start.9 = (bf16[640,128]{1,0:T(8,128)(2,1)S(1)}, bf16[640,128]{1,0:T(8,128)(2,1)S(1)}, u32[]{:S(2)}, u32[]{:S(2)}) collective-permute-start(bf16[640,128]{1,0:T(8,128)(2,1)S(1)} %bitcast.46), channel_id=1, source_target_pairs={{0,12},{4,16},{8,20},{12,24},{16,28},{20,32},{24,36},{28,40},{32,4... | collective-permute-start | bytes 491528 | tf_op jit(solution)/shard_map/ppermute | solution.py:372
  38.5 19.4 %collective-permute-start.11 = (bf16[1280,128]{1,0:T(8,128)(2,1)S(1)}, bf16[1280,128]{1,0:T(8,128)(2,1)S(1)}, u32[]{:S(2)}, u32[]{:S(2)}) collective-permute-start(bf16[1280,128]{1,0:T(8,128)(2,1)S(1)} %pad_maximum_fusion.2), channel_id=1, source_target_pairs={{0,16},{4,20},{8,24},{12,28},{16,32},{20,36},{24,40},{28,44},{32,4... | collective-permute-start | bytes 983048 | tf_op jit(solution)/shard_map/ppermute | solution.py:372
  38.8 19.1 %copy-start.3 = (bf16[80,8,128]{2,1,0:T(8,128)(2,1)S(1)}, bf16[80,8,128]{2,1,0:T(8,128)(2,1)}, u32[]{:S(2)}) copy-start(bf16[80,8,128]{2,1,0:T(8,128)(2,1)} %param.12) | copy-start | bytes 491524
  44.7 15.6 %copy-start.6 = (f32[384,32]{1,0:T(8,128)S(1)}, f32[384,32]{1,0:T(8,128)}, u32[]{:S(2)}) copy-start(f32[384,32]{1,0:T(8,128)} %constant.35.clone.sum_ref) | copy-start | bytes 147460
  44.7 15.6 %copy-start.7 = (f32[3,8,384]{2,1,0:T(8,128)S(1)}, f32[3,8,384]{2,1,0:T(8,128)}, u32[]{:S(2)}) copy-start(f32[3,8,384]{2,1,0:T(8,128)} %constant.34.clone.mask_ref) | copy-start | bytes 110596
  60.4 13.4 %copy-start.4 = (s32[8,128]{1,0:T(8,128)S(1)}, s32[8,128]{1,0:T(8,128)}, u32[]{:S(2)}) copy-start(s32[8,128]{1,0:T(8,128)} %refs_7_.1) | copy-start | bytes 12292
  60.4 13.4 %copy-start.5 = (s32[8,128]{1,0:T(8,128)S(1)}, s32[8,128]{1,0:T(8,128)}, u32[]{:S(2)}) copy-start(s32[8,128]{1,0:T(8,128)} %refs_8_.1) | copy-start | bytes 12292
  68.0 10.1 %collective-permute-start.18 = (f32[96,128]{1,0:T(8,128)S(1)}, f32[96,128]{1,0:T(8,128)S(1)}, u32[]{:S(2)}, u32[]{:S(2)}) collective-permute-start(f32[96,128]{1,0:T(8,128)S(1)} %filter_grad.1), channel_id=1, source_target_pairs={{0,4},{4,0},{8,12},{12,8},{16,20},{20,16},{24,28},{28,24},{32,36},... | collective-permute-start | bytes 147464 | tf_op jit(solution)/shard_map/ppermute | solution.py:372
  68.6 9.4 %collective-permute-start.19 = (f32[96,128]{1,0:T(8,128)S(1)}, f32[96,128]{1,0:T(8,128)S(1)}, u32[]{:S(2)}, u32[]{:S(2)}) collective-permute-start(f32[96,128]{1,0:T(8,128)S(1)} %filter_grad.1), channel_id=1, source_target_pairs={{0,8},{4,12},{8,0},{12,4},{16,24},{20,28},{24,16},{28,20},{32,40},... | collective-permute-start | bytes 147464 | tf_op jit(solution)/shard_map/ppermute | solution.py:372
  73.3 4.7 %collective-permute-start.20 = (f32[96,128]{1,0:T(8,128)S(1)}, f32[96,128]{1,0:T(8,128)S(1)}, u32[]{:S(2)}, u32[]{:S(2)}) collective-permute-start(f32[96,128]{1,0:T(8,128)S(1)} %filter_grad.1), channel_id=1, source_target_pairs={{0,12},{4,8},{8,4},{12,0},{16,28},{20,24},{24,20},{28,16},{32,44},... | collective-permute-start | bytes 147464 | tf_op jit(solution)/shard_map/ppermute | solution.py:372
  78.0 6.0 %collective-permute-start.21 = (f32[96,128]{1,0:T(8,128)S(1)}, f32[96,128]{1,0:T(8,128)S(1)}, u32[]{:S(2)}, u32[]{:S(2)}) collective-permute-start(f32[96,128]{1,0:T(8,128)S(1)} %add_add_fusion.2), channel_id=1, source_target_pairs={{0,16},{4,20},{8,24},{12,28},{16,0},{20,4},{24,8},{28,12},{32,48},... | collective-permute-start | bytes 147464 | tf_op jit(solution)/shard_map/ppermute | solution.py:372
  78.1 5.9 %collective-permute-start.22 = (f32[96,128]{1,0:T(8,128)S(1)}, f32[96,128]{1,0:T(8,128)S(1)}, u32[]{:S(2)}, u32[]{:S(2)}) collective-permute-start(f32[96,128]{1,0:T(8,128)S(1)} %add_add_fusion.2), channel_id=1, source_target_pairs={{0,32},{4,36},{8,40},{12,44},{16,48},{20,52},{24,56},{28,60},{32,0... | collective-permute-start | bytes 147464 | tf_op jit(solution)/shard_map/ppermute | solution.py:372
  78.2 6.9 %collective-permute-start.23 = (f32[96,128]{1,0:T(8,128)S(1)}, f32[96,128]{1,0:T(8,128)S(1)}, u32[]{:S(2)}, u32[]{:S(2)}) collective-permute-start(f32[96,128]{1,0:T(8,128)S(1)} %add_add_fusion.2), channel_id=1, source_target_pairs={{0,48},{4,52},{8,56},{12,60},{16,32},{20,36},{24,40},{28,44},{32,1... | collective-permute-start | bytes 147464 | tf_op jit(solution)/shard_map/ppermute | solution.py:372
  82.5 20.6 %collective-permute-start.12 = (bf16[640,128]{1,0:T(8,128)(2,1)S(1)}, bf16[640,128]{1,0:T(8,128)(2,1)S(1)}, u32[]{:S(2)}, u32[]{:S(2)}) collective-permute-start(bf16[640,128]{1,0:T(8,128)(2,1)S(1)} %get-tuple-element.22), channel_id=1, source_target_pairs={{0,252},{4,0},{8,4},{12,8},{16,12},{20,16},{24,20},{28,24},{32,28}... | collective-permute-start | bytes 491528 | tf_op jit(solution)/shard_map/ppermute | solution.py:372
  85.1 11.8 %collective-permute-start.24 = (f32[96,128]{1,0:T(8,128)S(1)}, f32[96,128]{1,0:T(8,128)S(1)}, u32[]{:S(2)}, u32[]{:S(2)}) collective-permute-start(f32[96,128]{1,0:T(8,128)S(1)} %add_add_fusion.1), channel_id=1, source_target_pairs={{0,64},{4,68},{8,72},{12,76},{16,80},{20,84},{24,88},{28,92},{32,9... | collective-permute-start | bytes 147464 | tf_op jit(solution)/shard_map/ppermute | solution.py:372
  85.8 11.2 %collective-permute-start.25 = (f32[96,128]{1,0:T(8,128)S(1)}, f32[96,128]{1,0:T(8,128)S(1)}, u32[]{:S(2)}, u32[]{:S(2)}) collective-permute-start(f32[96,128]{1,0:T(8,128)S(1)} %add_add_fusion.1), channel_id=1, source_target_pairs={{0,128},{4,132},{8,136},{12,140},{16,144},{20,148},{24,152},{28,15... | collective-permute-start | bytes 147464 | tf_op jit(solution)/shard_map/ppermute | solution.py:372
  88.0 9.4 %collective-permute-start.26 = (f32[96,128]{1,0:T(8,128)S(1)}, f32[96,128]{1,0:T(8,128)S(1)}, u32[]{:S(2)}, u32[]{:S(2)}) collective-permute-start(f32[96,128]{1,0:T(8,128)S(1)} %add_add_fusion.1), channel_id=1, source_target_pairs={{0,192},{4,196},{8,200},{12,204},{16,208},{20,212},{24,216},{28,22... | collective-permute-start | bytes 147464 | tf_op jit(solution)/shard_map/ppermute | solution.py:372
  92.6 13.1 %collective-permute-start.13 = (bf16[640,128]{1,0:T(8,128)(2,1)S(1)}, bf16[640,128]{1,0:T(8,128)(2,1)S(1)}, u32[]{:S(2)}, u32[]{:S(2)}) collective-permute-start(bf16[640,128]{1,0:T(8,128)(2,1)S(1)} %get-tuple-element.23), channel_id=1, source_target_pairs={{0,248},{4,252},{8,0},{12,4},{16,8},{20,12},{24,16},{28,20},{32,24... | collective-permute-start | bytes 491528 | tf_op jit(solution)/shard_map/ppermute | solution.py:372
  96.9 10.4 %collective-permute-start.14 = (bf16[640,128]{1,0:T(8,128)(2,1)S(1)}, bf16[640,128]{1,0:T(8,128)(2,1)S(1)}, u32[]{:S(2)}, u32[]{:S(2)}) collective-permute-start(bf16[640,128]{1,0:T(8,128)(2,1)S(1)} %get-tuple-element.24), channel_id=1, source_target_pairs={{0,244},{4,248},{8,252},{12,0},{16,4},{20,8},{24,12},{28,16},{32,2... | collective-permute-start | bytes 491528 | tf_op jit(solution)/shard_map/ppermute | solution.py:372
  97.0 11.8 %collective-permute-start.15 = (bf16[640,128]{1,0:T(8,128)(2,1)S(1)}, bf16[640,128]{1,0:T(8,128)(2,1)S(1)}, u32[]{:S(2)}, u32[]{:S(2)}) collective-permute-start(bf16[640,128]{1,0:T(8,128)(2,1)S(1)} %get-tuple-element.25), channel_id=1, source_target_pairs={{0,240},{4,244},{8,248},{12,252},{16,0},{20,4},{24,8},{28,12},{32,... | collective-permute-start | bytes 491528 | tf_op jit(solution)/shard_map/ppermute | solution.py:372
  97.4 11.8 %collective-permute-start.16 = (bf16[640,128]{1,0:T(8,128)(2,1)S(1)}, bf16[640,128]{1,0:T(8,128)(2,1)S(1)}, u32[]{:S(2)}, u32[]{:S(2)}) collective-permute-start(bf16[640,128]{1,0:T(8,128)(2,1)S(1)} %get-tuple-element.26), channel_id=1, source_target_pairs={{0,236},{4,240},{8,244},{12,248},{16,252},{20,0},{24,4},{28,8},{32... | collective-permute-start | bytes 491528 | tf_op jit(solution)/shard_map/ppermute | solution.py:372
  103.1 16.9 %collective-permute-start.17 = (bf16[640,128]{1,0:T(8,128)(2,1)S(1)}, bf16[640,128]{1,0:T(8,128)(2,1)S(1)}, u32[]{:S(2)}, u32[]{:S(2)}) collective-permute-start(bf16[640,128]{1,0:T(8,128)(2,1)S(1)} %get-tuple-element.27), channel_id=1, source_target_pairs={{0,232},{4,236},{8,240},{12,244},{16,248},{20,252},{24,0},{28,4},{... | collective-permute-start | bytes 491528 | tf_op jit(solution)/shard_map/ppermute | solution.py:372
  105.7 15.1 %collective-permute-start.27 = (f32[96,128]{1,0:T(8,128)S(1)}, f32[96,128]{1,0:T(8,128)S(1)}, u32[]{:S(2)}, u32[]{:S(2)}) collective-permute-start(f32[96,128]{1,0:T(8,128)S(1)} %add_add_fusion), channel_id=1, source_target_pairs={{0,3},{1,2},{2,1},{3,0},{4,7},{5,6},{6,5},{7,4},{8,11},{9,10},{10,... | collective-permute-start | bytes 147464 | tf_op jit(solution)/shard_map/ppermute | solution.py:372
  107.3 13.6 %collective-permute-start.28 = (f32[96,128]{1,0:T(8,128)S(1)}, f32[96,128]{1,0:T(8,128)S(1)}, u32[]{:S(2)}, u32[]{:S(2)}) collective-permute-start(f32[96,128]{1,0:T(8,128)S(1)} %add_add_fusion), channel_id=1, source_target_pairs={{0,2},{1,3},{2,0},{3,1},{4,6},{5,7},{6,4},{7,5},{8,10},{9,11},{10,... | collective-permute-start | bytes 147464 | tf_op jit(solution)/shard_map/ppermute | solution.py:372
  108.8 12.1 %collective-permute-start.29 = (f32[96,128]{1,0:T(8,128)S(1)}, f32[96,128]{1,0:T(8,128)S(1)}, u32[]{:S(2)}, u32[]{:S(2)}) collective-permute-start(f32[96,128]{1,0:T(8,128)S(1)} %add_add_fusion), channel_id=1, source_target_pairs={{0,1},{1,0},{2,3},{3,2},{4,5},{5,4},{6,7},{7,6},{8,9},{9,8},{10,11... | collective-permute-start | bytes 147464 | tf_op jit(solution)/shard_map/ppermute | solution.py:372

commit v4 on v3

--- a/solution.py
+++ b/solution.py
@@ -407,7 +407,7 @@
     halo = jnp.concatenate([one[640:].reshape(12, 64, 128), after], axis=1)
     halo_far = across(halo, 2)
     later = together(right, after)
-    two, three, four = (along(later, k) for k in (2, 3, 4))
+    two, three, four = along(right, 2), along(later, 3), along(later, 4)
     pair = along(jnp.concatenate([one[:640], two]), 4)
     panels = [one, two, three, four, pair, right]
     own_later = together(own, after)

time: 124 us -> 124 us (level)
  starting transfers between devices: 41.6 us -> 51.9 us
  waiting for transfers between devices: 53.2 us -> 43.4 us
    ppermute x30, starting transfers between devices: 41.6 us -> 51.9 us  [moved(): return lax.ppermute(value, axis, pairs)]
    ppermute x30, waiting for transfers between devices: 53.2 us -> 43.4 us  [moved(): return lax.ppermute(value, axis, pairs)]
  transfers between devices with their start and end apart: 30 -> 30, of which waited for: 12 -> 10; matrix products, arithmetic and copies ran while one was open for 4% -> 4% of each run, Pallas kernels for 8% -> 8%
where the time goes in v4:
time: 124 us
  starting transfers between devices  51.9 us (42%)
  waiting for transfers between devices  43.4 us (35%)
  Pallas kernels  20.2 us (16%)
  local copies, waits for them, and re-layouts  4.61 us (4%)
  other arithmetic  2.49 us (2%)
    ppermute x30, starting transfers between devices, moved(): return lax.ppermute(value, axis, pairs)  51.9 us
    ppermute x30, waiting for transfers between devices, moved(): return lax.ppermute(value, axis, pairs)  43.4 us
    pallas_call x1, Pallas kernels, run_filter(): pl.pallas_call(filter_kernel, out_shape=jax.ShapeDtypeStruct((96, 128), F...  7.58 us
    pallas_call x1, Pallas kernels, run_conv(): pl.pallas_call(conv_kernel, out_shape=jax.ShapeDtypeStruct((DISP, 80, 128...  5.92 us
    pallas_call x1, Pallas kernels, run_grad(): pl.pallas_call(grad_kernel, out_shape=[jax.ShapeDtypeStruct((640, 128), F...  4.26 us
    slice x1, local copies, waits for them, and re-layouts, shards(): conv_cot[:, :, 6:].reshape(768, 128)  2.53 us
  transfers between devices with their start and end apart: 30, of which 10 were waited for; matrix products, arithmetic and copies ran while one was open for 4% of the time, Pallas kernels for 8%

profile of v4, /device:TPU:4, one launch (start us, length us, event | category | flops | bytes accessed | tf_op | source)
XLA Modules:
  0.0 123.7 jit_solution(12522839248731148437)
XLA Ops:
  0.7 3.3 %collective-permute-start.2 = (bf16[12,256,128]{2,1,0:T(8,128)(2,1)}, bf16[12,256,128]{2,1,0:T(8,128)(2,1)S(1)}, u32[]{:S(2)}, u32[]{:S(2)}) collective-permute-start(bf16[12,256,128]{2,1,0:T(8,128)(2,1)} %bitcast.39), channel_id=1, source_target_pairs={{0,2},{1,3},{2,0},{3,1},{4,6},{5,7},{6,4},{7,5},{8,10},{9,11},{10,... | collective-permute-start | bytes 2359304 | tf_op jit(solution)/shard_map/ppermute | solution.py:372
  4.0 2.5 %fusion.2 = (bf16[12,32,2,128]{3,2,1,0:T(2,128)(2,1)S(1)}, bf16[12,32,2,128]{3,2,1,0:T(2,128)(2,1)}) fusion(bf16[12,32,8,128]{3,2,1,0:T(8,128)(2,1)} %param.14), kind=kLoop, calls=%fused_computation.27 | loop fusion | bytes 786432 | tf_op jit(solution)/shard_map/slice | solution.py:405
  6.5 1.0 pad_maximum_fusion.1
  7.5 1.3 %collective-permute-start.4 = (bf16[1408,128]{1,0:T(8,128)(2,1)S(1)}, bf16[1408,128]{1,0:T(8,128)(2,1)S(1)}, u32[]{:S(2)}, u32[]{:S(2)}) collective-permute-start(bf16[1408,128]{1,0:T(8,128)(2,1)S(1)} %pad_maximum_fusion.1), channel_id=1, source_target_pairs={{0,4},{4,8},{8,12},{12,16},{16,20},{20,24},{24,28},{28,32},{32,36}... | collective-permute-start | bytes 1081352 | tf_op jit(solution)/shard_map/ppermute | solution.py:372
  8.8 0.8 collective-permute-start
  9.6 4.0 %collective-permute-start.8 = (bf16[640,128]{1,0:T(8,128)(2,1)}, bf16[640,128]{1,0:T(8,128)(2,1)S(1)}, u32[]{:S(2)}, u32[]{:S(2)}) collective-permute-start(bf16[640,128]{1,0:T(8,128)(2,1)} %bitcast.44), channel_id=1, source_target_pairs={{0,8},{4,12},{8,16},{12,20},{16,24},{20,28},{24,32},{28,36},{32,40... | collective-permute-start | bytes 491528 | tf_op jit(solution)/shard_map/ppermute | solution.py:372
  13.6 0.1 constant_dynamic-slice_fusion
  13.7 0.2 copy.27
  14.0 1.2 collective-permute-done
  15.2 3.0 %collective-permute-done.4.refs_0_ = bf16[1408,128]{1,0:T(8,128)(2,1)S(1)} collective-permute-done((bf16[1408,128]{1,0:T(8,128)(2,1)S(1)}, bf16[1408,128]{1,0:T(8,128)(2,1)S(1)}, u32[]{:S(2)}, u32[]{:S(2)}) %collective-permute-start.4) | collective-permute-done | bytes 360480 | tf_op jit(solution)/shard_map/ppermute | solution.py:372
  18.3 4.6 %collective-permute-done.2.refs_2_ = bf16[12,256,128]{2,1,0:T(8,128)(2,1)S(1)} collective-permute-done((bf16[12,256,128]{2,1,0:T(8,128)(2,1)}, bf16[12,256,128]{2,1,0:T(8,128)(2,1)S(1)}, u32[]{:S(2)}, u32[]{:S(2)}) %collective-permute-start.2) | collective-permute-done | bytes 786464 | tf_op jit(solution)/shard_map/ppermute | solution.py:372
  22.9 0.2 fusion
  23.4 0.6 collective-permute-start.5
  24.0 6.3 %collective-permute-done.6.refs_6_ = bf16[12,128,128]{2,1,0:T(8,128)(2,1)S(1)} collective-permute-done((bf16[12,128,128]{2,1,0:T(8,128)(2,1)S(1)}, bf16[12,128,128]{2,1,0:T(8,128)(2,1)S(1)}, u32[]{:S(2)}, u32[]{:S(2)}) %collective-permute-start.6) | collective-permute-done | bytes 393248 | tf_op jit(solution)/shard_map/ppermute | solution.py:372
  30.2 0.3 select_add_fusion
  30.6 2.3 %collective-permute-start.10 = (bf16[640,128]{1,0:T(8,128)(2,1)S(1)}, bf16[640,128]{1,0:T(8,128)(2,1)S(1)}, u32[]{:S(2)}, u32[]{:S(2)}) collective-permute-start(bf16[640,128]{1,0:T(8,128)(2,1)S(1)} %bitcast.45), channel_id=1, source_target_pairs={{0,16},{4,20},{8,24},{12,28},{16,32},{20,36},{24,40},{28,44},{32,4... | collective-permute-start | bytes 491528 | tf_op jit(solution)/shard_map/ppermute | solution.py:372
  32.9 1.7 %collective-permute-start.9 = (bf16[640,128]{1,0:T(8,128)(2,1)S(1)}, bf16[640,128]{1,0:T(8,128)(2,1)S(1)}, u32[]{:S(2)}, u32[]{:S(2)}) collective-permute-start(bf16[640,128]{1,0:T(8,128)(2,1)S(1)} %bitcast.46), channel_id=1, source_target_pairs={{0,12},{4,16},{8,20},{12,24},{16,28},{20,32},{24,36},{28,40},{32,4... | collective-permute-start | bytes 491528 | tf_op jit(solution)/shard_map/ppermute | solution.py:372
  34.6 1.9 %collective-permute-start.11 = (bf16[1280,128]{1,0:T(8,128)(2,1)S(1)}, bf16[1280,128]{1,0:T(8,128)(2,1)S(1)}, u32[]{:S(2)}, u32[]{:S(2)}) collective-permute-start(bf16[1280,128]{1,0:T(8,128)(2,1)S(1)} %pad_maximum_fusion.2), channel_id=1, source_target_pairs={{0,16},{4,20},{8,24},{12,28},{16,32},{20,36},{24,40},{28,44},{32,4... | collective-permute-start | bytes 983048 | tf_op jit(solution)/shard_map/ppermute | solution.py:372
  36.5 5.9 %filter_transpose.1.refs_6_ = bf16[48,80,128]{2,1,0:T(8,128)(2,1)S(1)} custom-call(s32[1]{0:T(128)} %bitcast.1.rank_ref, bf16[240,1152]{1,0:T(8,128)(2,1)S(1)} %bitcast.38, bf16[12,256,128]{2,1,0:T(8,128)(2,1)S(1)} %bitcast.41, bf16[12,256,128]{2,1,0:T(8,128)(2,1)S(1)} %collective-permute-done.1.refs_1_, ...), custom_call_target="tpu_custom_call" | custom-call | flops 7000000000 | bytes 6000000 | tf_op jit(solution)/shard_map/filter_transpose/pallas_call | solution.py:275
  42.5 0.1 collective-permute-done.10.refs_3_
  42.6 11.9 %collective-permute-done.9.refs_2_ = bf16[640,128]{1,0:T(8,128)(2,1)S(1)} collective-permute-done((bf16[640,128]{1,0:T(8,128)(2,1)S(1)}, bf16[640,128]{1,0:T(8,128)(2,1)S(1)}, u32[]{:S(2)}, u32[]{:S(2)}) %collective-permute-start.9) | collective-permute-done | bytes 163872 | tf_op jit(solution)/shard_map/ppermute | solution.py:372
  54.5 2.0 %collective-permute-done.11.refs_4_ = bf16[1280,128]{1,0:T(8,128)(2,1)S(1)} collective-permute-done((bf16[1280,128]{1,0:T(8,128)(2,1)S(1)}, bf16[1280,128]{1,0:T(8,128)(2,1)S(1)}, u32[]{:S(2)}, u32[]{:S(2)}) %collective-permute-start.11) | collective-permute-done | bytes 327712 | tf_op jit(solution)/shard_map/ppermute | solution.py:372
  56.4 2.4 %cost_volume.1.volume = bf16[52,240,128]{2,1,0:T(8,128)(2,1)S(1)} custom-call(bf16[640,128]{1,0:T(8,128)(2,1)S(1)} %bitcast.49, bf16[1408,128]{1,0:T(8,128)(2,1)S(1)} %collective-permute-done.4.refs_0_, bf16[640,128]{1,0:T(8,128)(2,1)S(1)} %collective-permute-done.8.refs_1_, bf16[640,128]{1,0:T(8,128)(2,1)S(1)} %collective-permute-done.9.refs_2_, ...), custom_call_target="tpu_custom_call" | custom-call | flops 5000000000 | bytes 4000000 | tf_op jit(solution)/shard_map/cost_volume/pallas_call | solution.py:288
  58.9 7.6 %filter_grad.1 = f32[96,128]{1,0:T(8,128)S(1)} custom-call(s32[1]{0:T(128)} %bitcast.1.rank_ref, bf16[52,240,128]{2,1,0:T(8,128)(2,1)S(1)} %cost_volume.1.volume, f32[3,8,384]{2,1,0:T(8,128)S(1)} %copy-done.7, f32[384,32]{1,0:T(8,128)S(1)} %copy-done.6, bf16[12,256,128]{2,1,0:T(8,128)(2,1)S(1)} %bitcast.42, ...), custom_call_target="tpu_custom_call" | custom-call | flops 8000000000 | bytes 4000000 | tf_op jit(solution)/shard_map/filter_grad/pallas_call | solution.py:313
  66.5 2.1 %collective-permute-start.18 = (f32[96,128]{1,0:T(8,128)S(1)}, f32[96,128]{1,0:T(8,128)S(1)}, u32[]{:S(2)}, u32[]{:S(2)}) collective-permute-start(f32[96,128]{1,0:T(8,128)S(1)} %filter_grad.1), channel_id=1, source_target_pairs={{0,4},{4,0},{8,12},{12,8},{16,20},{20,16},{24,28},{28,24},{32,36},... | collective-permute-start | bytes 147464 | tf_op jit(solution)/shard_map/ppermute | solution.py:372
  68.5 3.3 %collective-permute-start.19 = (f32[96,128]{1,0:T(8,128)S(1)}, f32[96,128]{1,0:T(8,128)S(1)}, u32[]{:S(2)}, u32[]{:S(2)}) collective-permute-start(f32[96,128]{1,0:T(8,128)S(1)} %filter_grad.1), channel_id=1, source_target_pairs={{0,8},{4,12},{8,0},{12,4},{16,24},{20,28},{24,16},{28,20},{32,40},... | collective-permute-start | bytes 147464 | tf_op jit(solution)/shard_map/ppermute | solution.py:372
  71.8 0.5 collective-permute-start.20
  72.3 4.3 %feature_grads.1 = (f32[640,128]{1,0:T(8,128)}, bf16[640,128]{1,0:T(8,128)(2,1)S(1)}, bf16[640,128]{1,0:T(8,128)(2,1)S(1)}, bf16[640,128]{1,0:T(8,128)(2,1)S(1)}...) custom-call(bf16[640,128]{1,0:T(8,128)(2,1)S(1)} %bitcast.50, ...), custom_call_target="tpu_custom_call" | custom-call | flops 5000000000 | bytes 4000000 | tf_op jit(solution)/shard_map/feature_grads/pallas_call | solution.py:330
  76.6 0.1 collective-permute-start.21
  76.7 0.1 collective-permute-start.22
  76.8 4.3 %collective-permute-start.23 = (f32[96,128]{1,0:T(8,128)S(1)}, f32[96,128]{1,0:T(8,128)S(1)}, u32[]{:S(2)}, u32[]{:S(2)}) collective-permute-start(f32[96,128]{1,0:T(8,128)S(1)} %add_add_fusion.2), channel_id=1, source_target_pairs={{0,48},{4,52},{8,56},{12,60},{16,32},{20,36},{24,40},{28,44},{32,1... | collective-permute-start | bytes 147464 | tf_op jit(solution)/shard_map/ppermute | solution.py:372
  81.1 1.6 %collective-permute-start.12 = (bf16[640,128]{1,0:T(8,128)(2,1)S(1)}, bf16[640,128]{1,0:T(8,128)(2,1)S(1)}, u32[]{:S(2)}, u32[]{:S(2)}) collective-permute-start(bf16[640,128]{1,0:T(8,128)(2,1)S(1)} %get-tuple-element.22), channel_id=1, source_target_pairs={{0,252},{4,0},{8,4},{12,8},{16,12},{20,16},{24,20},{28,24},{32,28}... | collective-permute-start | bytes 491528 | tf_op jit(solution)/shard_map/ppermute | solution.py:372
  82.6 1.1 collective-permute-done.23
  83.8 2.4 %collective-permute-start.24 = (f32[96,128]{1,0:T(8,128)S(1)}, f32[96,128]{1,0:T(8,128)S(1)}, u32[]{:S(2)}, u32[]{:S(2)}) collective-permute-start(f32[96,128]{1,0:T(8,128)S(1)} %add_add_fusion.1), channel_id=1, source_target_pairs={{0,64},{4,68},{8,72},{12,76},{16,80},{20,84},{24,88},{28,92},{32,9... | collective-permute-start | bytes 147464 | tf_op jit(solution)/shard_map/ppermute | solution.py:372
  86.1 0.5 collective-permute-start.25
  86.6 4.6 %collective-permute-start.26 = (f32[96,128]{1,0:T(8,128)S(1)}, f32[96,128]{1,0:T(8,128)S(1)}, u32[]{:S(2)}, u32[]{:S(2)}) collective-permute-start(f32[96,128]{1,0:T(8,128)S(1)} %add_add_fusion.1), channel_id=1, source_target_pairs={{0,192},{4,196},{8,200},{12,204},{16,208},{20,212},{24,216},{28,22... | collective-permute-start | bytes 147464 | tf_op jit(solution)/shard_map/ppermute | solution.py:372
  91.2 4.6 %collective-permute-start.13 = (bf16[640,128]{1,0:T(8,128)(2,1)S(1)}, bf16[640,128]{1,0:T(8,128)(2,1)S(1)}, u32[]{:S(2)}, u32[]{:S(2)}) collective-permute-start(bf16[640,128]{1,0:T(8,128)(2,1)S(1)} %get-tuple-element.23), channel_id=1, source_target_pairs={{0,248},{4,252},{8,0},{12,4},{16,8},{20,12},{24,16},{28,20},{32,24... | collective-permute-start | bytes 491528 | tf_op jit(solution)/shard_map/ppermute | solution.py:372
  95.9 1.0 collective-permute-start.15
  96.9 4.8 %collective-permute-start.16 = (bf16[640,128]{1,0:T(8,128)(2,1)S(1)}, bf16[640,128]{1,0:T(8,128)(2,1)S(1)}, u32[]{:S(2)}, u32[]{:S(2)}) collective-permute-start(bf16[640,128]{1,0:T(8,128)(2,1)S(1)} %get-tuple-element.26), channel_id=1, source_target_pairs={{0,236},{4,240},{8,244},{12,248},{16,252},{20,0},{24,4},{28,8},{32... | collective-permute-start | bytes 491528 | tf_op jit(solution)/shard_map/ppermute | solution.py:372
  101.7 2.8 %collective-permute-start.17 = (bf16[640,128]{1,0:T(8,128)(2,1)S(1)}, bf16[640,128]{1,0:T(8,128)(2,1)S(1)}, u32[]{:S(2)}, u32[]{:S(2)}) collective-permute-start(bf16[640,128]{1,0:T(8,128)(2,1)S(1)} %get-tuple-element.27), channel_id=1, source_target_pairs={{0,232},{4,236},{8,240},{12,244},{16,248},{20,252},{24,0},{28,4},{... | collective-permute-start | bytes 491528 | tf_op jit(solution)/shard_map/ppermute | solution.py:372
  104.7 1.2 collective-permute-done.14
  105.8 3.3 %collective-permute-start.28 = (f32[96,128]{1,0:T(8,128)S(1)}, f32[96,128]{1,0:T(8,128)S(1)}, u32[]{:S(2)}, u32[]{:S(2)}) collective-permute-start(f32[96,128]{1,0:T(8,128)S(1)} %add_add_fusion), channel_id=1, source_target_pairs={{0,2},{1,3},{2,0},{3,1},{4,6},{5,7},{6,4},{7,5},{8,10},{9,11},{10,... | collective-permute-start | bytes 147464 | tf_op jit(solution)/shard_map/ppermute | solution.py:372
  109.1 12.0 %collective-permute-done.17 = bf16[640,128]{1,0:T(8,128)(2,1)S(1)} collective-permute-done((bf16[640,128]{1,0:T(8,128)(2,1)S(1)}, bf16[640,128]{1,0:T(8,128)(2,1)S(1)}, u32[]{:S(2)}, u32[]{:S(2)}) %collective-permute-start.17) | collective-permute-done | bytes 163872 | tf_op jit(solution)/shard_map/ppermute | solution.py:372
  121.1 0.9 add_bitcast_fusion
  122.1 0.3 reshape.72
  122.4 0.2 slice_multiply_fusion
  122.6 0.1 copy.29
  122.8 1.0 copy.25
  (65 shorter events, 0.7 us)
Async XLA Ops:
  0.6 13.0 %copy-start = (bf16[32,40,3,3,3]{1,0,4,3,2:T(8,128)(2,1)S(1)}, bf16[32,40,3,3,3]{1,0,4,3,2:T(8,128)(2,1)}, u32[]{:S(2)}) copy-start(bf16[32,40,3,3,3]{1,0,4,3,2:T(8,128)(2,1)} %param.15) | copy-start | bytes 207364
  0.6 22.3 %copy-start.8 = (bf16[32,384,1,1,1]{1,0,4,3,2:T(8,128)(2,1)S(1)}, bf16[32,384,1,1,1]{1,0,4,3,2:T(8,128)(2,1)}, u32[]{:S(2)}) copy-start(bf16[32,384,1,1,1]{1,0,4,3,2:T(8,128)(2,1)} %constant.41) | copy-start | bytes 73732
  0.7 29.6 %copy-start.9 = (pred[8,384]{1,0:T(8,128)(4,1)S(1)}, pred[8,384]{1,0:T(8,128)(4,1)}, u32[]{:S(2)}) copy-start(pred[8,384]{1,0:T(8,128)(4,1)} %constant.31.clone) | copy-start | bytes 9220
  0.7 29.6 %copy-start.10 = (pred[8,384]{1,0:T(8,128)(4,1)S(1)}, pred[8,384]{1,0:T(8,128)(4,1)}, u32[]{:S(2)}) copy-start(pred[8,384]{1,0:T(8,128)(4,1)} %constant.32.clone) | copy-start | bytes 9220
  0.7 29.5 %copy-start.11 = (pred[8,384]{1,0:T(8,128)(4,1)S(1)}, pred[8,384]{1,0:T(8,128)(4,1)}, u32[]{:S(2)}) copy-start(pred[8,384]{1,0:T(8,128)(4,1)} %constant.33.clone) | copy-start | bytes 9220
  0.7 29.9 %copy-start.2 = (bf16[80,8,128]{2,1,0:T(8,128)(2,1)S(1)}, bf16[80,8,128]{2,1,0:T(8,128)(2,1)}, u32[]{:S(2)}) copy-start(bf16[80,8,128]{2,1,0:T(8,128)(2,1)} %param.13) | copy-start | bytes 491524
  0.7 22.2 %collective-permute-start.2 = (bf16[12,256,128]{2,1,0:T(8,128)(2,1)}, bf16[12,256,128]{2,1,0:T(8,128)(2,1)S(1)}, u32[]{:S(2)}, u32[]{:S(2)}) collective-permute-start(bf16[12,256,128]{2,1,0:T(8,128)(2,1)} %bitcast.39), channel_id=1, source_target_pairs={{0,2},{1,3},{2,0},{3,1},{4,6},{5,7},{6,4},{7,5},{8,10},{9,11},{10,... | collective-permute-start | bytes 2359304 | tf_op jit(solution)/shard_map/ppermute | solution.py:372
  6.5 30.0 %copy-start.1 = (bf16[12,32,8,128]{3,2,1,0:T(8,128)(2,1)S(1)}, bf16[12,32,8,128]{3,2,1,0:T(8,128)(2,1)}, u32[]{:S(2)}) copy-start(bf16[12,32,8,128]{3,2,1,0:T(8,128)(2,1)} %param.14) | copy-start | bytes 2359300
  7.5 10.6 %collective-permute-start.4 = (bf16[1408,128]{1,0:T(8,128)(2,1)S(1)}, bf16[1408,128]{1,0:T(8,128)(2,1)S(1)}, u32[]{:S(2)}, u32[]{:S(2)}) collective-permute-start(bf16[1408,128]{1,0:T(8,128)(2,1)S(1)} %pad_maximum_fusion.1), channel_id=1, source_target_pairs={{0,4},{4,8},{8,12},{12,16},{16,20},{20,24},{24,28},{28,32},{32,36}... | collective-permute-start | bytes 1081352 | tf_op jit(solution)/shard_map/ppermute | solution.py:372
  8.8 6.4 %collective-permute-start = (bf16[12,64,128]{2,1,0:T(8,128)(2,1)}, bf16[12,64,128]{2,1,0:T(8,128)(2,1)S(1)}, u32[]{:S(2)}, u32[]{:S(2)}) collective-permute-start(bf16[12,64,128]{2,1,0:T(8,128)(2,1)} %bitcast.10), channel_id=1, source_target_pairs={{0,252},{4,0},{8,4},{12,8},{16,12},{20,16},{24,20},{28,24},{32,28}... | collective-permute-start | bytes 589832 | tf_op jit(solution)/shard_map/ppermute | solution.py:372
  9.6 20.9 %collective-permute-start.8 = (bf16[640,128]{1,0:T(8,128)(2,1)}, bf16[640,128]{1,0:T(8,128)(2,1)S(1)}, u32[]{:S(2)}, u32[]{:S(2)}) collective-permute-start(bf16[640,128]{1,0:T(8,128)(2,1)} %bitcast.44), channel_id=1, source_target_pairs={{0,8},{4,12},{8,16},{12,20},{16,24},{20,28},{24,32},{28,36},{32,40... | collective-permute-start | bytes 491528 | tf_op jit(solution)/shard_map/ppermute | solution.py:372
  15.2 19.4 %collective-permute-start.1 = (bf16[12,256,128]{2,1,0:T(8,128)(2,1)}, bf16[12,256,128]{2,1,0:T(8,128)(2,1)S(1)}, u32[]{:S(2)}, u32[]{:S(2)}) collective-permute-start(bf16[12,256,128]{2,1,0:T(8,128)(2,1)} %bitcast.40), channel_id=1, source_target_pairs={{0,1},{1,0},{2,3},{3,2},{4,5},{5,4},{6,7},{7,6},{8,9},{9,8},{10,11... | collective-permute-start | bytes 2359304 | tf_op jit(solution)/shard_map/ppermute | solution.py:372
  18.2 12.0 %collective-permute-start.6 = (bf16[12,128,128]{2,1,0:T(8,128)(2,1)S(1)}, bf16[12,128,128]{2,1,0:T(8,128)(2,1)S(1)}, u32[]{:S(2)}, u32[]{:S(2)}) collective-permute-start(bf16[12,128,128]{2,1,0:T(8,128)(2,1)S(1)} %pad_maximum_fusion.refs_4_), channel_id=1, source_target_pairs={{0,2},{1,3},{2,0},{3,1},{4,6},{5,7},{6,4},{7,5},{8,10},{9,11},{10,... | collective-permute-start | bytes 1179656 | tf_op jit(solution)/shard_map/ppermute | solution.py:372
  22.9 13.6 %collective-permute-start.3 = (bf16[12,256,128]{2,1,0:T(8,128)(2,1)S(1)}, bf16[12,256,128]{2,1,0:T(8,128)(2,1)S(1)}, u32[]{:S(2)}, u32[]{:S(2)}) collective-permute-start(bf16[12,256,128]{2,1,0:T(8,128)(2,1)S(1)} %collective-permute-done.2.refs_2_), channel_id=1, source_target_pairs={{0,1},{1,0},{2,3},{3,2},{4,5},{5,4},{6,7},{7,6},{8,9},{9,8},{10,11... | collective-permute-start | bytes 2359304 | tf_op jit(solution)/shard_map/ppermute | solution.py:372
  23.4 9.5 %collective-permute-start.5 = (bf16[12,128,128]{2,1,0:T(8,128)(2,1)S(1)}, bf16[12,128,128]{2,1,0:T(8,128)(2,1)S(1)}, u32[]{:S(2)}, u32[]{:S(2)}) collective-permute-start(bf16[12,128,128]{2,1,0:T(8,128)(2,1)S(1)} %pad_maximum_fusion.refs_4_), channel_id=1, source_target_pairs={{0,1},{1,0},{2,3},{3,2},{4,5},{5,4},{6,7},{7,6},{8,9},{9,8},{10,11... | collective-permute-start | bytes 1179656 | tf_op jit(solution)/shard_map/ppermute | solution.py:372
  30.2 6.3 %collective-permute-start.7 = (bf16[12,128,128]{2,1,0:T(8,128)(2,1)S(1)}, bf16[12,128,128]{2,1,0:T(8,128)(2,1)S(1)}, u32[]{:S(2)}, u32[]{:S(2)}) collective-permute-start(bf16[12,128,128]{2,1,0:T(8,128)(2,1)S(1)} %collective-permute-done.6.refs_6_), channel_id=1, source_target_pairs={{0,1},{1,0},{2,3},{3,2},{4,5},{5,4},{6,7},{7,6},{8,9},{9,8},{10,11... | collective-permute-start | bytes 1179656 | tf_op jit(solution)/shard_map/ppermute | solution.py:372
  30.6 12.0 %collective-permute-start.10 = (bf16[640,128]{1,0:T(8,128)(2,1)S(1)}, bf16[640,128]{1,0:T(8,128)(2,1)S(1)}, u32[]{:S(2)}, u32[]{:S(2)}) collective-permute-start(bf16[640,128]{1,0:T(8,128)(2,1)S(1)} %bitcast.45), channel_id=1, source_target_pairs={{0,16},{4,20},{8,24},{12,28},{16,32},{20,36},{24,40},{28,44},{32,4... | collective-permute-start | bytes 491528 | tf_op jit(solution)/shard_map/ppermute | solution.py:372
  32.9 21.6 %collective-permute-start.9 = (bf16[640,128]{1,0:T(8,128)(2,1)S(1)}, bf16[640,128]{1,0:T(8,128)(2,1)S(1)}, u32[]{:S(2)}, u32[]{:S(2)}) collective-permute-start(bf16[640,128]{1,0:T(8,128)(2,1)S(1)} %bitcast.46), channel_id=1, source_target_pairs={{0,12},{4,16},{8,20},{12,24},{16,28},{20,32},{24,36},{28,40},{32,4... | collective-permute-start | bytes 491528 | tf_op jit(solution)/shard_map/ppermute | solution.py:372
  34.6 21.8 %collective-permute-start.11 = (bf16[1280,128]{1,0:T(8,128)(2,1)S(1)}, bf16[1280,128]{1,0:T(8,128)(2,1)S(1)}, u32[]{:S(2)}, u32[]{:S(2)}) collective-permute-start(bf16[1280,128]{1,0:T(8,128)(2,1)S(1)} %pad_maximum_fusion.2), channel_id=1, source_target_pairs={{0,16},{4,20},{8,24},{12,28},{16,32},{20,36},{24,40},{28,44},{32,4... | collective-permute-start | bytes 983048 | tf_op jit(solution)/shard_map/ppermute | solution.py:372
  36.5 19.9 %copy-start.3 = (bf16[80,8,128]{2,1,0:T(8,128)(2,1)S(1)}, bf16[80,8,128]{2,1,0:T(8,128)(2,1)}, u32[]{:S(2)}) copy-start(bf16[80,8,128]{2,1,0:T(8,128)(2,1)} %param.12) | copy-start | bytes 491524
  42.4 16.4 %copy-start.6 = (f32[384,32]{1,0:T(8,128)S(1)}, f32[384,32]{1,0:T(8,128)}, u32[]{:S(2)}) copy-start(f32[384,32]{1,0:T(8,128)} %constant.35.clone.sum_ref) | copy-start | bytes 147460
  42.5 16.4 %copy-start.7 = (f32[3,8,384]{2,1,0:T(8,128)S(1)}, f32[3,8,384]{2,1,0:T(8,128)}, u32[]{:S(2)}) copy-start(f32[3,8,384]{2,1,0:T(8,128)} %constant.34.clone.mask_ref) | copy-start | bytes 110596
  58.9 13.4 %copy-start.4 = (s32[8,128]{1,0:T(8,128)S(1)}, s32[8,128]{1,0:T(8,128)}, u32[]{:S(2)}) copy-start(s32[8,128]{1,0:T(8,128)} %refs_7_.1) | copy-start | bytes 12292
  58.9 13.4 %copy-start.5 = (s32[8,128]{1,0:T(8,128)S(1)}, s32[8,128]{1,0:T(8,128)}, u32[]{:S(2)}) copy-start(s32[8,128]{1,0:T(8,128)} %refs_8_.1) | copy-start | bytes 12292
  66.5 10.1 %collective-permute-start.18 = (f32[96,128]{1,0:T(8,128)S(1)}, f32[96,128]{1,0:T(8,128)S(1)}, u32[]{:S(2)}, u32[]{:S(2)}) collective-permute-start(f32[96,128]{1,0:T(8,128)S(1)} %filter_grad.1), channel_id=1, source_target_pairs={{0,4},{4,0},{8,12},{12,8},{16,20},{20,16},{24,28},{28,24},{32,36},... | collective-permute-start | bytes 147464 | tf_op jit(solution)/shard_map/ppermute | solution.py:372
  68.5 8.0 %collective-permute-start.19 = (f32[96,128]{1,0:T(8,128)S(1)}, f32[96,128]{1,0:T(8,128)S(1)}, u32[]{:S(2)}, u32[]{:S(2)}) collective-permute-start(f32[96,128]{1,0:T(8,128)S(1)} %filter_grad.1), channel_id=1, source_target_pairs={{0,8},{4,12},{8,0},{12,4},{16,24},{20,28},{24,16},{28,20},{32,40},... | collective-permute-start | bytes 147464 | tf_op jit(solution)/shard_map/ppermute | solution.py:372
  71.8 4.7 %collective-permute-start.20 = (f32[96,128]{1,0:T(8,128)S(1)}, f32[96,128]{1,0:T(8,128)S(1)}, u32[]{:S(2)}, u32[]{:S(2)}) collective-permute-start(f32[96,128]{1,0:T(8,128)S(1)} %filter_grad.1), channel_id=1, source_target_pairs={{0,12},{4,8},{8,4},{12,0},{16,28},{20,24},{24,20},{28,16},{32,44},... | collective-permute-start | bytes 147464 | tf_op jit(solution)/shard_map/ppermute | solution.py:372
  76.6 6.0 %collective-permute-start.21 = (f32[96,128]{1,0:T(8,128)S(1)}, f32[96,128]{1,0:T(8,128)S(1)}, u32[]{:S(2)}, u32[]{:S(2)}) collective-permute-start(f32[96,128]{1,0:T(8,128)S(1)} %add_add_fusion.2), channel_id=1, source_target_pairs={{0,16},{4,20},{8,24},{12,28},{16,0},{20,4},{24,8},{28,12},{32,48},... | collective-permute-start | bytes 147464 | tf_op jit(solution)/shard_map/ppermute | solution.py:372
  76.7 5.9 %collective-permute-start.22 = (f32[96,128]{1,0:T(8,128)S(1)}, f32[96,128]{1,0:T(8,128)S(1)}, u32[]{:S(2)}, u32[]{:S(2)}) collective-permute-start(f32[96,128]{1,0:T(8,128)S(1)} %add_add_fusion.2), channel_id=1, source_target_pairs={{0,32},{4,36},{8,40},{12,44},{16,48},{20,52},{24,56},{28,60},{32,0... | collective-permute-start | bytes 147464 | tf_op jit(solution)/shard_map/ppermute | solution.py:372
  76.8 7.0 %collective-permute-start.23 = (f32[96,128]{1,0:T(8,128)S(1)}, f32[96,128]{1,0:T(8,128)S(1)}, u32[]{:S(2)}, u32[]{:S(2)}) collective-permute-start(f32[96,128]{1,0:T(8,128)S(1)} %add_add_fusion.2), channel_id=1, source_target_pairs={{0,48},{4,52},{8,56},{12,60},{16,32},{20,36},{24,40},{28,44},{32,1... | collective-permute-start | bytes 147464 | tf_op jit(solution)/shard_map/ppermute | solution.py:372
  81.1 20.6 %collective-permute-start.12 = (bf16[640,128]{1,0:T(8,128)(2,1)S(1)}, bf16[640,128]{1,0:T(8,128)(2,1)S(1)}, u32[]{:S(2)}, u32[]{:S(2)}) collective-permute-start(bf16[640,128]{1,0:T(8,128)(2,1)S(1)} %get-tuple-element.22), channel_id=1, source_target_pairs={{0,252},{4,0},{8,4},{12,8},{16,12},{20,16},{24,20},{28,24},{32,28}... | collective-permute-start | bytes 491528 | tf_op jit(solution)/shard_map/ppermute | solution.py:372
  83.8 12.1 %collective-permute-start.24 = (f32[96,128]{1,0:T(8,128)S(1)}, f32[96,128]{1,0:T(8,128)S(1)}, u32[]{:S(2)}, u32[]{:S(2)}) collective-permute-start(f32[96,128]{1,0:T(8,128)S(1)} %add_add_fusion.1), channel_id=1, source_target_pairs={{0,64},{4,68},{8,72},{12,76},{16,80},{20,84},{24,88},{28,92},{32,9... | collective-permute-start | bytes 147464 | tf_op jit(solution)/shard_map/ppermute | solution.py:372
  86.1 9.7 %collective-permute-start.25 = (f32[96,128]{1,0:T(8,128)S(1)}, f32[96,128]{1,0:T(8,128)S(1)}, u32[]{:S(2)}, u32[]{:S(2)}) collective-permute-start(f32[96,128]{1,0:T(8,128)S(1)} %add_add_fusion.1), channel_id=1, source_target_pairs={{0,128},{4,132},{8,136},{12,140},{16,144},{20,148},{24,152},{28,15... | collective-permute-start | bytes 147464 | tf_op jit(solution)/shard_map/ppermute | solution.py:372
  86.6 10.3 %collective-permute-start.26 = (f32[96,128]{1,0:T(8,128)S(1)}, f32[96,128]{1,0:T(8,128)S(1)}, u32[]{:S(2)}, u32[]{:S(2)}) collective-permute-start(f32[96,128]{1,0:T(8,128)S(1)} %add_add_fusion.1), channel_id=1, source_target_pairs={{0,192},{4,196},{8,200},{12,204},{16,208},{20,212},{24,216},{28,22... | collective-permute-start | bytes 147464 | tf_op jit(solution)/shard_map/ppermute | solution.py:372
  91.2 13.3 %collective-permute-start.13 = (bf16[640,128]{1,0:T(8,128)(2,1)S(1)}, bf16[640,128]{1,0:T(8,128)(2,1)S(1)}, u32[]{:S(2)}, u32[]{:S(2)}) collective-permute-start(bf16[640,128]{1,0:T(8,128)(2,1)S(1)} %get-tuple-element.23), channel_id=1, source_target_pairs={{0,248},{4,252},{8,0},{12,4},{16,8},{20,12},{24,16},{28,20},{32,24... | collective-permute-start | bytes 491528 | tf_op jit(solution)/shard_map/ppermute | solution.py:372
  95.9 10.0 %collective-permute-start.14 = (bf16[640,128]{1,0:T(8,128)(2,1)S(1)}, bf16[640,128]{1,0:T(8,128)(2,1)S(1)}, u32[]{:S(2)}, u32[]{:S(2)}) collective-permute-start(bf16[640,128]{1,0:T(8,128)(2,1)S(1)} %get-tuple-element.24), channel_id=1, source_target_pairs={{0,244},{4,248},{8,252},{12,0},{16,4},{20,8},{24,12},{28,16},{32,2... | collective-permute-start | bytes 491528 | tf_op jit(solution)/shard_map/ppermute | solution.py:372
  95.9 13.2 %collective-permute-start.15 = (bf16[640,128]{1,0:T(8,128)(2,1)S(1)}, bf16[640,128]{1,0:T(8,128)(2,1)S(1)}, u32[]{:S(2)}, u32[]{:S(2)}) collective-permute-start(bf16[640,128]{1,0:T(8,128)(2,1)S(1)} %get-tuple-element.25), channel_id=1, source_target_pairs={{0,240},{4,244},{8,248},{12,252},{16,0},{20,4},{24,8},{28,12},{32,... | collective-permute-start | bytes 491528 | tf_op jit(solution)/shard_map/ppermute | solution.py:372
  96.9 12.2 %collective-permute-start.16 = (bf16[640,128]{1,0:T(8,128)(2,1)S(1)}, bf16[640,128]{1,0:T(8,128)(2,1)S(1)}, u32[]{:S(2)}, u32[]{:S(2)}) collective-permute-start(bf16[640,128]{1,0:T(8,128)(2,1)S(1)} %get-tuple-element.26), channel_id=1, source_target_pairs={{0,236},{4,240},{8,244},{12,248},{16,252},{20,0},{24,4},{28,8},{32... | collective-permute-start | bytes 491528 | tf_op jit(solution)/shard_map/ppermute | solution.py:372
  101.7 19.4 %collective-permute-start.17 = (bf16[640,128]{1,0:T(8,128)(2,1)S(1)}, bf16[640,128]{1,0:T(8,128)(2,1)S(1)}, u32[]{:S(2)}, u32[]{:S(2)}) collective-permute-start(bf16[640,128]{1,0:T(8,128)(2,1)S(1)} %get-tuple-element.27), channel_id=1, source_target_pairs={{0,232},{4,236},{8,240},{12,244},{16,248},{20,252},{24,0},{28,4},{... | collective-permute-start | bytes 491528 | tf_op jit(solution)/shard_map/ppermute | solution.py:372
  104.6 17.4 %collective-permute-start.27 = (f32[96,128]{1,0:T(8,128)S(1)}, f32[96,128]{1,0:T(8,128)S(1)}, u32[]{:S(2)}, u32[]{:S(2)}) collective-permute-start(f32[96,128]{1,0:T(8,128)S(1)} %add_add_fusion), channel_id=1, source_target_pairs={{0,3},{1,2},{2,1},{3,0},{4,7},{5,6},{6,5},{7,4},{8,11},{9,10},{10,... | collective-permute-start | bytes 147464 | tf_op jit(solution)/shard_map/ppermute | solution.py:372
  105.8 16.2 %collective-permute-start.28 = (f32[96,128]{1,0:T(8,128)S(1)}, f32[96,128]{1,0:T(8,128)S(1)}, u32[]{:S(2)}, u32[]{:S(2)}) collective-permute-start(f32[96,128]{1,0:T(8,128)S(1)} %add_add_fusion), channel_id=1, source_target_pairs={{0,2},{1,3},{2,0},{3,1},{4,6},{5,7},{6,4},{7,5},{8,10},{9,11},{10,... | collective-permute-start | bytes 147464 | tf_op jit(solution)/shard_map/ppermute | solution.py:372
  109.1 12.9 %collective-permute-start.29 = (f32[96,128]{1,0:T(8,128)S(1)}, f32[96,128]{1,0:T(8,128)S(1)}, u32[]{:S(2)}, u32[]{:S(2)}) collective-permute-start(f32[96,128]{1,0:T(8,128)S(1)} %add_add_fusion), channel_id=1, source_target_pairs={{0,1},{1,0},{2,3},{3,2},{4,5},{5,4},{6,7},{7,6},{8,9},{9,8},{10,11... | collective-permute-start | bytes 147464 | tf_op jit(solution)/shard_map/ppermute | solution.py:372
